TPU v7x, 32 devices: a whole 2x2x4 slice. The times are simulated.
32 devices in a mesh: span: 8 (over z, x), cross: 4 (over y, core).
Axes of the slice: x: 2, y: 2, z: 4, core: 2. Of those that a mesh axis runs over, the one named last changes fastest.
Arguments:
- populations: bfloat16 [19, 128, 128, 128], P(None, 'span', 'cross'), may hold values from 0.2 to 1.8
- cell_index: int32 [4096, 8], P(('span', 'cross')), may hold values from 0 to 65535
- marker_weight: float32 [4096, 8], P(('span', 'cross')), may hold values from 0 to 0.25
- segment_id: int32 [4096], P(('span', 'cross')), may hold values from 0 to 255, as said below
Outputs:
- populations_next: bfloat16 [19, 128, 128, 128], P(None, 'span', 'cross')
- eddy_coeff: float32 [128, 128], P('cross')
- segment_force: float32 [3, 256], P(None, ('span', 'cross'))
Inputs may be any that keep to these rules, and one draw needn't show every extreme that they name: cell_index addresses a cell of the block of the device that holds the marker, flat in the order (span, crossflow, stream) of that 16 x 32 x 128 block. `segment_id`: segments are owned 8 to a device in device order (span slowest); a marker's segment may be owned by any device.
All inputs are finite; a program needn't handle non-finite values.
Results may differ from a plain program's by a relative error of at most 0.0019.
The roundings to bfloat16 on the way count: a program that leaves them out, or rounds other values in their place, can miss the bound.
Values may be sent and summed in bfloat16 or wider, within the bound.
No kernel may reach another device: no remote copies, remote signals or barrier semaphores. Data moves between devices by JAX's collectives and lax.ppermute only.
A program may use at most 128 MiB of HBM per device.

v0:
```python
import functools

import jax
import jax.numpy as jnp
from jax import lax
from jax.experimental import pallas as pl
from jax.experimental.pallas import tpu as pltpu
from jax.sharding import PartitionSpec as P

SEG_DEV = 8
LANES = 128
HALO = 4
EXT = 40
PAD = 56
OWN = 10
TOP = 8
CHUNKS = (8, 16, 24, 32, 40)
VMEM = 40 * 1024 * 1024

eps_sum = 1e-06
base_visc = 0.005

VELOCITIES = [
    [0, 0, 0],
    [1, 0, 0],
    [-1, 0, 0],
    [0, 1, 0],
    [0, -1, 0],
    [0, 0, 1],
    [0, 0, -1],
    [1, 1, 0],
    [-1, -1, 0],
    [1, -1, 0],
    [-1, 1, 0],
    [1, 0, 1],
    [-1, 0, -1],
    [1, 0, -1],
    [-1, 0, 1],
    [0, 1, 1],
    [0, -1, -1],
    [0, 1, -1],
    [0, -1, 1],
]


def neighbours(axis):
    count = lax.axis_size(axis)
    forward = [(i, (i + 1) % count) for i in range(count)]
    backward = [(target, source) for source, target in forward]
    return forward, backward


def exchange(first, last, axis):
    forward, backward = neighbours(axis)
    low = lax.ppermute(last, axis, forward)
    high = lax.ppermute(first, axis, backward)
    return low, high


def full(shape, dtype):
    return jax.ShapeDtypeStruct(shape, dtype)


def in_vmem(count):
    return [pl.BlockSpec(memory_space=pltpu.VMEM)] * count


def params():
    return pltpu.CompilerParams(vmem_limit_bytes=VMEM)


def plus(array):
    return pltpu.roll(array, LANES - 1, 1)


def minus(array):
    return pltpu.roll(array, 1, 1)


def moments_kernel(pops_hbm, vel_ref, first_ref, last_ref, pops, sems):
    depth = pops.shape[1]
    part = depth // 4
    copies = []
    for index in range(4):
        planes = pl.ds(index * part, part)
        copies.append(
            pltpu.make_async_copy(pops_hbm.at[:, planes], pops.at[:, planes], sems.at[index])
        )
        copies[-1].start()

    def plane(z, carry):
        for half in range(2):
            rows = pl.ds(16 * half, 16)
            f = [pops[q, z, rows, :].astype(jnp.float32) for q in range(19)]
            flux = [0.0, 0.0, 0.0]
            density = f[0]
            for q in range(1, 19, 2):
                even, odd = f[q] + f[q + 1], f[q] - f[q + 1]
                density = density + even
                for dim in range(3):
                    sign = VELOCITIES[q][dim]
                    if sign:
                        flux[dim] = flux[dim] + odd if sign > 0 else flux[dim] - odd
            inverse = 1.0 / density
            for dim in range(3):
                speed = flux[dim] * inverse
                vel_ref[dim, z, rows, :] = speed
                if half == 0:
                    first_ref[dim, z] = speed[:HALO]
                else:
                    last_ref[dim, z] = speed[16 - HALO :]
        return carry

    for index in range(4):
        copies[index].wait()
        lax.fori_loop(index * part, (index + 1) * part, plane, 0)


def block_moments(populations):
    _, depth, width, lanes = populations.shape
    edge = full((3, depth, HALO, lanes), jnp.float32)
    return pl.pallas_call(
        moments_kernel,
        out_shape=(full((3, depth, width, lanes), jnp.float32), edge, edge),
        in_specs=[pl.BlockSpec(memory_space=pl.ANY)],
        out_specs=tuple(in_vmem(3)),
        scratch_shapes=[
            pltpu.VMEM(populations.shape, populations.dtype),
            pltpu.SemaphoreType.DMA((4,)),
        ],
        compiler_params=params(),
        name="moments",
    )(populations)


def edges_kernel(vel_ref, low_ref, high_ref, *outs):
    depth, width = vel_ref.shape[1:3]
    for start, out in zip((0, 2, depth - 4, depth - 2), outs):
        for dim in range(3):
            for index in range(2):
                z = start + index
                out[dim, index, pl.ds(0, HALO), :] = low_ref[dim, z]
                out[dim, index, pl.ds(HALO, width), :] = vel_ref[dim, z]
                out[dim, index, pl.ds(HALO + width, HALO), :] = high_ref[dim, z]


def edge_planes(vel, low, high):
    pair = full((3, 2, EXT, LANES), jnp.float32)
    return pl.pallas_call(
        edges_kernel,
        out_shape=(pair,) * 4,
        in_specs=in_vmem(3),
        out_specs=tuple(in_vmem(4)),
        compiler_params=params(),
        name="edges",
    )(vel, low, high)


def strain_parts(ref, p, row):
    grads = []
    for dim in range(3):
        here = ref[dim, p, pl.ds(row, 8), :]
        grads.append(
            (
                plus(here) - minus(here),
                ref[dim, p, pl.ds(row + 1, 8), :] - ref[dim, p, pl.ds(row - 1, 8), :],
                ref[dim, p + 1, pl.ds(row, 8), :] - ref[dim, p - 1, pl.ds(row, 8), :],
            )
        )
    parts = [
        grads[0][0],
        grads[1][1],
        grads[2][2],
        grads[0][1] + grads[1][0],
        grads[0][2] + grads[2][0],
        grads[1][2] + grads[2][1],
    ]
    straight = parts[0] * parts[0] + parts[1] * parts[1] + parts[2] * parts[2]
    mixed = parts[3] * parts[3] + parts[4] * parts[4] + parts[5] * parts[5]
    return parts, jnp.sqrt(0.5 * straight + 0.25 * mixed)


def weigh(low, middle, high):
    return (low + high) + (middle + middle)


PAIRS = ((0, 0), (1, 1), (2, 2), (0, 1), (0, 2), (1, 2))


def model_sums(planes, ext, hat, prods, zsum, acc_ref, store_mag):
    def first_pass(p, carry):
        for row in CHUNKS:
            rows = pl.ds(row, 8)
            parts, size = strain_parts(ext, p, row)
            store_mag(p, row, size)
            for k in range(6):
                prods[k, p, rows, :] = size * parts[k]
            for k, (i, j) in enumerate(PAIRS):
                prods[6 + k, p, rows, :] = ext[i, p, rows, :] * ext[j, p, rows, :]
            for dim in range(3):
                lines = []
                for shift in (-1, 0, 1):
                    at = pl.ds(row + shift, 8)
                    lines.append(
                        weigh(ext[dim, p - 1, at, :], ext[dim, p, at, :], ext[dim, p + 1, at, :])
                    )
                line = weigh(*lines)
                hat[dim, p, rows, :] = (1.0 / 64.0) * weigh(minus(line), line, plus(line))
        return carry

    lax.fori_loop(1, planes - 1, first_pass, 0)

    def second_pass(p, carry):
        for row in CHUNKS:
            rows = pl.ds(row, 8)
            for k in range(12):
                zsum[k, rows, :] = weigh(
                    prods[k, p - 1, rows, :], prods[k, p, rows, :], prods[k, p + 1, rows, :]
                )
        for row in CHUNKS:
            rows = pl.ds(row, 8)
            parts, size = strain_parts(hat, p, row)
            size = 256.0 * size
            here = [hat[dim, p, rows, :] for dim in range(3)]
            scaled = [64.0 * speed for speed in here]
            smooth = []
            for k in range(12):
                line = weigh(
                    zsum[k, pl.ds(row - 1, 8), :], zsum[k, rows, :], zsum[k, pl.ds(row + 1, 8), :]
                )
                smooth.append(weigh(minus(line), line, plus(line)))
            lm = 0.0
            squares = [0.0, 0.0]
            for k, (i, j) in enumerate(PAIRS):
                model = smooth[k] - size * parts[k]
                leonard = smooth[6 + k] - scaled[i] * here[j]
                lm = lm + leonard * model
                squares[k // 3] = squares[k // 3] + model * model
            out = pl.ds(row - TOP, 8)
            acc_ref[0, out, :] += (1.0 / 4096.0) * lm
            acc_ref[1, out, :] += (1.0 / 4096.0) * (squares[0] + 0.5 * squares[1])
        return carry

    lax.fori_loop(2, planes - 2, second_pass, 0)


def inner_kernel(vel_ref, low_ref, high_ref, acc_ref, mag_ref, ext, hat, prods, zsum):
    depth, width = vel_ref.shape[1:3]

    def assemble(p, carry):
        for dim in range(3):
            ext[dim, p, pl.ds(OWN - HALO, HALO), :] = low_ref[dim, p]
            ext[dim, p, pl.ds(OWN, width), :] = vel_ref[dim, p]
            ext[dim, p, pl.ds(OWN + width, HALO), :] = high_ref[dim, p]
        return carry

    lax.fori_loop(0, depth, assemble, 0)
    acc_ref[...] = jnp.zeros_like(acc_ref)

    def store_mag(p, row, size):
        mag_ref[p - 1, pl.ds(row - TOP, 8), :] = size

    model_sums(depth, ext, hat, prods, zsum, acc_ref, store_mag)


def model_scratch(planes):
    return [
        pltpu.VMEM((3, planes, PAD, LANES), jnp.float32),
        pltpu.VMEM((3, planes, PAD, LANES), jnp.float32),
        pltpu.VMEM((12, planes, PAD, LANES), jnp.float32),
        pltpu.VMEM((12, PAD, LANES), jnp.float32),
    ]


def inner_sums(vel, low, high):
    depth = vel.shape[1]
    return pl.pallas_call(
        inner_kernel,
        out_shape=(
            full((2, EXT, LANES), jnp.float32),
            full((depth - 2, EXT, LANES), jnp.float32),
        ),
        in_specs=in_vmem(3),
        out_specs=tuple(in_vmem(2)),
        scratch_shapes=model_scratch(depth),
        compiler_params=params(),
        name="inner_sums",
    )(vel, low, high)


def outer_kernel(*refs):
    blocks, (partial_ref, acc_ref, mag_ref, ext, hat, prods, zsum) = refs[:6], refs[6:]
    acc_ref[...] = partial_ref[...]
    for side in range(2):
        for place in range(3):
            for dim in range(3):
                for index in range(2):
                    ext[dim, 2 * place + index, pl.ds(OWN - HALO, EXT), :] = blocks[
                        3 * side + place
                    ][dim, index]

        def store_mag(p, row, size):
            slot = p - 1 if side == 0 else p - 1

            @pl.when((slot < 2) if side == 0 else (slot >= 2))
            def _():
                mag_ref[slot, pl.ds(row - TOP, 8), :] = size

        model_sums(6, ext, hat, prods, zsum, acc_ref, store_mag)


def outer_sums(blocks, partial):
    return pl.pallas_call(
        outer_kernel,
        out_shape=(
            full((2, EXT, LANES), jnp.float32),
            full((4, EXT, LANES), jnp.float32),
        ),
        in_specs=in_vmem(7),
        out_specs=tuple(in_vmem(2)),
        scratch_shapes=model_scratch(6),
        compiler_params=params(),
        name="outer_sums",
    )(*blocks, partial)


def load_block(pops_hbm, low_hbm, high_hbm, pops, sems):
    depth = pops.shape[1] - 2
    part = depth // 4
    pieces = [(low_hbm, pl.ds(0, 1))]
    pieces += [
        (pops_hbm.at[:, pl.ds(index * part, part)], pl.ds(1 + index * part, part))
        for index in range(4)
    ]
    pieces.append((high_hbm, pl.ds(depth + 1, 1)))
    copies = [
        pltpu.make_async_copy(source, pops.at[:, place], sems.at[index])
        for index, (source, place) in enumerate(pieces)
    ]
    for copy in copies:
        copy.start()
    return copies


def rows_kernel(pops_hbm, low_hbm, high_hbm, first_ref, last_ref, pops, rows, sems):
    copies = load_block(pops_hbm, low_hbm, high_hbm, pops, sems)
    planes, width = pops.shape[1:3]
    rows[...] = jnp.zeros_like(rows)
    for copy in copies:
        copy.wait()

    def plane(p, carry):
        for q in range(19):
            low = pops[q, p, pl.ds(0, 16), :].astype(jnp.float32)
            high = pops[q, p, pl.ds(width - 16, 16), :].astype(jnp.float32)
            rows[0, q, pl.ds(p, 1), :] = low[:1]
            rows[1, q, pl.ds(p, 1), :] = high[15:]
        return carry

    lax.fori_loop(0, planes, plane, 0)
    first_ref[...] = rows[0].astype(jnp.bfloat16)
    last_ref[...] = rows[1].astype(jnp.bfloat16)


def face_rows(populations, low, high):
    _, depth, width, lanes = populations.shape
    tall = -(-(depth + 2) // 16) * 16
    edge = full((19, tall, lanes), jnp.bfloat16)
    return pl.pallas_call(
        rows_kernel,
        out_shape=(edge, edge),
        in_specs=[pl.BlockSpec(memory_space=pl.ANY)] * 3,
        out_specs=tuple(in_vmem(2)),
        scratch_shapes=[
            pltpu.VMEM((19, depth + 2, width, lanes), jnp.bfloat16),
            pltpu.VMEM((2, 19, tall, lanes), jnp.float32),
            pltpu.SemaphoreType.DMA((6,)),
        ],
        compiler_params=params(),
        name="face_rows",
    )(populations, low, high)


def relax(f, rate):
    even = {q: f[q] + f[q + 1] for q in range(1, 19, 2)}
    odd = {q: f[q] - f[q + 1] for q in range(1, 19, 2)}
    x_xy, x_xz = odd[7] + odd[9], odd[11] + odd[13]
    y_yz, y_xy = odd[15] + odd[17], odd[7] - odd[9]
    z_xz, z_yz = odd[11] - odd[13], odd[15] - odd[17]
    flux, up, down, axis_odd = [], [], [], []
    for first, second, along in ((x_xy, x_xz, 1), (y_yz, y_xy, 3), (z_xz, z_yz, 5)):
        sides = first + second
        total = odd[along] + sides
        heat = 0.15 * (sides - (2.0 / 3.0) * total)
        twist = (1.98 / 8.0) * (first - second)
        flux.append(total)
        up.append(heat + twist)
        down.append(heat - twist)
        axis_odd.append(4.0 * heat)
    a, b, c = even[7] + even[9], even[11] + even[13], even[15] + even[17]
    axes = even[1] + even[3] + even[5]
    diagonals = a + b + c
    density = f[0] + axes + diagonals
    inverse = 1.0 / density
    speed = [total * inverse for total in flux]
    square = [total * part for total, part in zip(flux, speed)]
    energy = square[0] + square[1] + square[2]
    d_e = (1.19 / 126.0) * (diagonals - f[0] - energy)
    d_eps = (1.4 / 252.0) * (9.0 * f[0] - 7.0 * axes - 2.0 * diagonals + 5.5 * energy)
    ax_n, dg_n, eq_n = 3.0 * even[1] - axes, diagonals - 3.0 * c, 3.0 * square[0] - energy
    ax_w, dg_w, eq_w = even[3] - even[5], a - b, square[1] - square[2]
    quarter = 0.25 * rate
    d_n = (rate * (1.0 / 36.0)) * (ax_n + dg_n - eq_n)
    d_pn = (1.4 / 72.0) * (dg_n - 2.0 * ax_n + 0.5 * eq_n)
    d_w = (rate * (1.0 / 12.0)) * (ax_w + dg_w - eq_w)
    d_pw = (1.4 / 24.0) * (dg_w - 2.0 * ax_w + 0.5 * eq_w)
    d_xy = quarter * (even[7] - even[9] - flux[0] * speed[1])
    d_xz = quarter * (even[11] - even[13] - flux[0] * speed[2])
    d_yz = quarter * (even[15] - even[17] - flux[1] * speed[2])
    base_axis = 11.0 * d_e + 4.0 * d_eps
    base_diag = -8.0 * d_e - d_eps
    k_n, k_w = d_n - 2.0 * d_pn, d_w - 2.0 * d_pw
    l_n, l_w = d_n + d_pn, d_w + d_pw
    post = [None] * 19
    post[0] = f[0] + (30.0 * d_e - 12.0 * d_eps)
    rest = base_axis + k_n
    for q, change, skew in (
        (1, base_axis - 2.0 * k_n, axis_odd[0]),
        (3, rest - k_w, axis_odd[1]),
        (5, rest + k_w, axis_odd[2]),
    ):
        post[q] = f[q] + (change + skew)
        post[q + 1] = f[q + 1] + (change - skew)
    rest = base_diag - l_n
    for q, change, shear, one, two in (
        (7, rest - l_w, d_xy, up[0], down[1]),
        (11, rest + l_w, d_xz, down[0], up[2]),
        (15, base_diag + 2.0 * l_n, d_yz, up[1], down[2]),
    ):
        minus_shear, plus_shear = change - shear, change + shear
        same, other = one + two, one - two
        post[q] = f[q] + (minus_shear - same)
        post[q + 1] = f[q + 1] + (minus_shear + same)
        post[q + 2] = f[q + 2] + (plus_shear - other)
        post[q + 3] = f[q + 3] + (plus_shear + other)
    return post


def relax_rate(eddy, size):
    return 1.0 / (0.5 + 3.0 * (base_visc + eddy * size))


BEFORE = [q for q in range(19) if VELOCITIES[q][1] > 0]
AFTER = [q for q in range(19) if VELOCITIES[q][1] < 0]
FIRST = 8


def step_kernel(
    pops_hbm,
    low_hbm,
    high_hbm,
    before_ref,
    after_ref,
    sums_ref,
    mag_in_ref,
    mag_out_ref,
    cell_ref,
    weight_ref,
    segment_ref,
    next_hbm,
    eddy_ref,
    partial_ref,
    pops,
    post,
    nexts,
    table,
    eddy,
    line,
    sems,
    out_sems,
):
    copies = load_block(pops_hbm, low_hbm, high_hbm, pops, sems)
    planes, width = pops.shape[1:3]
    depth = planes - 2
    part = depth // 4
    eddy[...] = jnp.maximum(sums_ref[0] / (sums_ref[1] + eps_sum), 0.0)
    eddy_ref[...] = eddy[pl.ds(OWN - TOP, width), :]

    tall = before_ref.shape[1]
    for side, (source, wanted, row, place) in enumerate(
        (
            (before_ref, BEFORE, OWN - TOP - 1, FIRST - 1),
            (after_ref, AFTER, OWN - TOP + width, FIRST + width),
        )
    ):
        line[...] = jnp.zeros_like(line)
        for p in range(planes):
            if p < 2:
                size = mag_out_ref[p, pl.ds(row, 1), :]
            elif p < planes - 2:
                size = mag_in_ref[p - 2, pl.ds(row, 1), :]
            else:
                size = mag_out_ref[p - planes + 4, pl.ds(row, 1), :]
            line[pl.ds(p, 1), :] = size
        here = eddy[pl.ds(row, 1), :]
        for start in range(0, planes, 16):
            rows = pl.ds(start, 16)
            f = [source[q, rows, :].astype(jnp.float32) for q in range(19)]
            out = relax(f, relax_rate(here, line[rows, :]))
            for q in wanted:
                for index in range(min(16, planes - start)):
                    post[q, start + index, pl.ds(place, 1), :] = out[q][index : index + 1]

    def collide(p, size_ref, at):
        for half in range(2):
            rows = pl.ds(16 * half, 16)
            lines = pl.ds(OWN - TOP + 16 * half, 16)
            rate = relax_rate(eddy[lines, :], size_ref[at, lines, :])
            f = [pops[q, p, rows, :].astype(jnp.float32) for q in range(19)]
            out = relax(f, rate)
            for q in range(19):
                post[q, p, pl.ds(FIRST + 16 * half, 16), :] = out[q]

    def inner(p, carry):
        collide(p, mag_in_ref, p - 2)
        return carry

    for copy in copies:
        copy.wait()
    collide(0, mag_out_ref, 0)
    collide(1, mag_out_ref, 1)
    lax.fori_loop(2, planes - 2, inner, 0)
    collide(planes - 2, mag_out_ref, 2)
    collide(planes - 1, mag_out_ref, 3)

    def run(z, carry):
        for half in range(2):
            flux = [0.0, 0.0, 0.0]
            for q in range(19):
                shift_x, shift_y, shift_z = VELOCITIES[q]
                piece = post[q, z + 1 - shift_z, pl.ds(FIRST + 16 * half - shift_y, 16), :]
                if shift_x:
                    piece = minus(piece) if shift_x > 0 else plus(piece)
                moved = piece.astype(jnp.bfloat16)
                nexts[q, z, pl.ds(16 * half, 16), :] = moved
                if q:
                    moved = moved.astype(jnp.float32)
                for dim in range(3):
                    sign = VELOCITIES[q][dim]
                    if sign:
                        flux[dim] = flux[dim] + moved if sign > 0 else flux[dim] - moved
            at = pl.ds(pl.multiple_of(z * width + 16 * half, 16), 16)
            for dim in range(3):
                coarse = flux[dim].astype(jnp.bfloat16)
                fine = (flux[dim] - coarse.astype(jnp.float32)).astype(jnp.bfloat16)
                table[0, at, dim * LANES : (dim + 1) * LANES] = coarse
                table[1, at, dim * LANES : (dim + 1) * LANES] = fine
        return carry

    outs = []
    for index in range(4):
        lax.fori_loop(index * part, (index + 1) * part, run, 0)
        place = pl.ds(index * part, part)
        outs.append(
            pltpu.make_async_copy(nexts.at[:, place], next_hbm.at[:, place], out_sems.at[index])
        )
        outs[-1].start()

    taps, markers = cell_ref.shape
    flat_rows = depth * width
    row_of = lax.broadcasted_iota(jnp.int32, (flat_rows, markers), 0)
    lane_of = lax.broadcasted_iota(jnp.int32, (LANES, markers), 0)
    force = [jnp.zeros((1, markers), jnp.float32) for _ in range(3)]
    contract = (((0,), (0,)), ((), ()))
    for tap in range(taps):
        cell = cell_ref[pl.ds(tap, 1), :]
        row, lane = lax.shift_right_logical(cell, 7), lax.bitwise_and(cell, LANES - 1)
        pick = jnp.where(row_of == row, 1.0, 0.0).astype(jnp.bfloat16)
        picked = lax.dot_general(
            table[0], pick, contract, preferred_element_type=jnp.float32
        ) + lax.dot_general(table[1], pick, contract, preferred_element_type=jnp.float32)
        weight = jnp.where(lane_of == lane, -weight_ref[pl.ds(tap, 1), :], 0.0)
        for dim in range(3):
            lanes = picked[dim * LANES : (dim + 1) * LANES, :]
            force[dim] = force[dim] + jnp.sum(lanes * weight, axis=0, keepdims=True)

    owners = partial_ref.shape[0]
    segments = owners * SEG_DEV
    force = jnp.concatenate(force + [jnp.zeros((5, markers), jnp.float32)], axis=0)
    segment_of = lax.broadcasted_iota(jnp.int32, (segments, markers), 0)
    hit = jnp.where(segment_of == segment_ref[...], 1.0, 0.0)
    totals = lax.dot_general(
        force,
        hit,
        (((1,), (1,)), ((), ())),
        precision=lax.Precision.HIGHEST,
        preferred_element_type=jnp.float32,
    )
    owner_of = lax.broadcasted_iota(jnp.int32, (owners, segments), 0)
    at_segment = lax.broadcasted_iota(jnp.int32, (owners, segments), 1)
    mine = lax.shift_right_logical(at_segment, 3) == owner_of
    spot = lax.broadcasted_iota(jnp.int32, (segments, LANES), 0)
    at_lane = lax.broadcasted_iota(jnp.int32, (segments, LANES), 1)
    packed = jnp.zeros((owners, LANES), jnp.float32)
    for dim in range(3):
        spread = jnp.where(mine, totals[dim : dim + 1, :], 0.0)
        to_lane = lax.bitwise_and(spot, SEG_DEV - 1) + dim * SEG_DEV == at_lane
        packed = packed + jnp.dot(
            spread,
            jnp.where(to_lane, 1.0, 0.0),
            precision=lax.Precision.HIGHEST,
            preferred_element_type=jnp.float32,
        )
    partial_ref[:, 0, :] = packed
    for copy in outs:
        copy.wait()


def step(populations, low, high, before, after, sums, mag_in, mag_out, cells, weights, segments, owners):
    _, depth, width, lanes = populations.shape
    planes = depth + 2
    tall = before.shape[1]
    hbm = pl.BlockSpec(memory_space=pl.ANY)
    return pl.pallas_call(
        step_kernel,
        out_shape=(
            full(populations.shape, jnp.bfloat16),
            full((width, lanes), jnp.float32),
            full((owners, 1, lanes), jnp.float32),
        ),
        in_specs=[hbm] * 3 + in_vmem(8),
        out_specs=(hbm,) + tuple(in_vmem(2)),
        scratch_shapes=[
            pltpu.VMEM((19, planes, width, lanes), jnp.bfloat16),
            pltpu.VMEM((19, planes, FIRST + width + 8, lanes), jnp.float32),
            pltpu.VMEM(populations.shape, jnp.bfloat16),
            pltpu.VMEM((2, depth * width, 3 * lanes), jnp.bfloat16),
            pltpu.VMEM((EXT, lanes), jnp.float32),
            pltpu.VMEM((tall, lanes), jnp.float32),
            pltpu.SemaphoreType.DMA((6,)),
            pltpu.SemaphoreType.DMA((4,)),
        ],
        compiler_params=params(),
        name="step",
    )(populations, low, high, before, after, sums, mag_in, mag_out, cells, weights, segments)


def finish_kernel(arrived_ref, out_ref):
    total = jnp.sum(arrived_ref[:, 0, :], axis=0, keepdims=True)
    for dim in range(3):
        out_ref[pl.ds(dim, 1), :] = total[:, dim * SEG_DEV : (dim + 1) * SEG_DEV]


def span_sum(values):
    count = lax.axis_size("span")
    if count & (count - 1):
        return lax.psum(values, "span")
    distance = 1
    while distance < count:
        pairs = [(i, i ^ distance) for i in range(count)]
        values = values + lax.ppermute(values, "span", pairs)
        distance *= 2
    return values


def local(populations, cell_index, marker_weight, segment_id):
    owners = lax.axis_size("span") * lax.axis_size("cross")
    face_low, face_high = exchange(populations[:, :1], populations[:, -1:], "span")
    vel, first, last = block_moments(populations)
    low, high = exchange(first, last, "cross")
    edges = edge_planes(vel, low, high)
    below, above = exchange(edges[0], edges[3], "span")
    rows_first, rows_last = face_rows(populations, face_low, face_high)
    before, after = exchange(rows_first, rows_last, "cross")
    partial, mag_in = inner_sums(vel, low, high)
    sums, mag_out = outer_sums((below,) + tuple(edges) + (above,), partial)
    sums = span_sum(sums)
    populations_next, eddy_coeff, packed = step(
        populations,
        face_low,
        face_high,
        before,
        after,
        sums,
        mag_in,
        mag_out,
        cell_index.T,
        marker_weight.T,
        segment_id[None, :],
        owners,
    )
    arrived = lax.all_to_all(packed, ("span", "cross"), 0, 0)
    segment_force = pl.pallas_call(
        finish_kernel,
        out_shape=full((3, SEG_DEV), jnp.float32),
        in_specs=in_vmem(1),
        out_specs=in_vmem(1)[0],
        name="finish",
    )(arrived)
    return (populations_next, eddy_coeff, segment_force)


def solution(mesh):
    in_specs = (
        P(None, "span", "cross", None),
        P(("span", "cross"), None),
        P(("span", "cross"), None),
        P(("span", "cross")),
    )
    out_specs = (P(None, "span", "cross", None), P("cross", None), P(None, ("span", "cross")))
    return jax.shard_map(local, mesh=mesh, in_specs=in_specs, out_specs=out_specs, check_vma=False)
```

profile of v0, /device:TPU:0, one launch (start us, length us, event | category | flops | bytes accessed | tf_op | source)
XLA Modules:
  0.0 68.1 jit_solution(9178654040705668435)
XLA Ops:
  0.6 1.7 %copy-done = bf16[19,16,32,128]{3,2,1,0:T(8,128)(2,1)S(1)} copy-done((bf16[19,16,32,128]{3,2,1,0:T(8,128)(2,1)S(1)}, bf16[19,16,32,128]{3,2,1,0:T(8,128)(2,1)}, u32[]{:S(2)}) %copy-start) | copy-done | bytes 2490392
  2.3 0.9 %moments.1 = (f32[3,16,32,128]{3,2,1,0:T(8,128)S(1)}, f32[3,16,4,128]{3,2,1,0:T(4,128)S(1)}, f32[3,16,4,128]{3,2,1,0:T(4,128)S(1)}) custom-call(bf16[19,16,32,128]{3,2,1,0:T(8,128)(2,1)S(1)} %copy-done), custom_call_target="tpu_custom_call" | custom-call | tf_op jit(solution)/shard_map/moments/pallas_call | solution.py:122
  3.2 0.5 collective-permute-start.4
  3.7 2.0 %collective-permute-start.5 = (f32[3,16,4,128]{3,2,1,0:T(4,128)S(1)}, f32[3,16,4,128]{3,2,1,0:T(4,128)S(1)}, u32[]{:S(2)}, u32[]{:S(2)}) collective-permute-start(f32[3,16,4,128]{3,2,1,0:T(4,128)S(1)} %get-tuple-element.23), channel_id=1, source_target_pairs={{1,0},{2,1},{3,2},{0,3},{5,4},{6,5},{7,6},{4,7},{9,8},{10,9},{11,1... | collective-permute-start | bytes 294920 | tf_op jit(solution)/shard_map/ppermute | solution.py:56
  5.8 5.3 %collective-permute-start.1 = (bf16[19,1,32,128]{3,2,1,0:T(8,128)(2,1)S(1)}, bf16[19,1,32,128]{3,2,1,0:T(8,128)(2,1)S(1)}, u32[]{:S(2)}, u32[]{:S(2)}) collective-permute-start(bf16[19,1,32,128]{3,2,1,0:T(8,128)(2,1)S(1)} %get-tuple-element.35), channel_id=1, source_target_pairs={{4,0},{8,4},{12,8},{16,12},{20,16},{24,20},{28,24},{0,28},{5,1},{9... | collective-permute-start | bytes 466952 | tf_op jit(solution)/shard_map/ppermute | solution.py:56
  11.1 0.0 collective-permute-start
  11.1 0.0 collective-permute-done.4.low_ref
  11.1 0.0 collective-permute-done.5.high_ref
  11.2 0.0 copy-start.2
  11.2 0.0 copy-start.3
  11.2 0.0 copy-start.4
  11.2 0.1 collective-permute-start.6
  11.3 4.8 %collective-permute-start.7 = (f32[3,2,40,128]{3,2,1,0:T(8,128)S(1)}, f32[3,2,40,128]{3,2,1,0:T(8,128)S(1)}, u32[]{:S(2)}, u32[]{:S(2)}) collective-permute-start(f32[3,2,40,128]{3,2,1,0:T(8,128)S(1)} %get-tuple-element.25.refs_1_), channel_id=1, source_target_pairs={{4,0},{8,4},{12,8},{16,12},{20,16},{24,20},{28,24},{0,28},{5,1},{9... | collective-permute-start | bytes 368648 | tf_op jit(solution)/shard_map/ppermute | solution.py:56
  16.0 0.0 collective-permute-done.1.high_hbm
  16.0 4.7 %collective-permute-done.low_hbm = bf16[19,1,32,128]{3,2,1,0:T(8,128)(2,1)S(1)} collective-permute-done((bf16[19,1,32,128]{3,2,1,0:T(8,128)(2,1)S(1)}, bf16[19,1,32,128]{3,2,1,0:T(8,128)(2,1)S(1)}, u32[]{:S(2)}, u32[]{:S(2)}) %collective-permute-start) | collective-permute-done | bytes 155680 | tf_op jit(solution)/shard_map/ppermute | solution.py:55
  20.7 0.7 %face_rows.1 = (bf16[19,32,128]{2,1,0:T(8,128)(2,1)S(1)}, bf16[19,32,128]{2,1,0:T(8,128)(2,1)S(1)}) custom-call(bf16[19,16,32,128]{3,2,1,0:T(8,128)(2,1)S(1)} %copy-done.1, bf16[19,1,32,128]{3,2,1,0:T(8,128)(2,1)S(1)} %collective-permute-done.low_hbm, bf16[19,1,32,128]{3,2,1,0:T(8,128)(2,1)S(1)} %collective-permute-done.1.high_hbm), custom_call_target="tpu_custom_call" | custom-call | tf_op jit(solution)/shard_map/face_rows/pallas_call | solution.py:369
  21.5 0.1 collective-permute-start.2
  21.5 1.7 %collective-permute-start.3 = (bf16[19,32,128]{2,1,0:T(8,128)(2,1)S(1)}, bf16[19,32,128]{2,1,0:T(8,128)(2,1)S(1)}, u32[]{:S(2)}, u32[]{:S(2)}) collective-permute-start(bf16[19,32,128]{2,1,0:T(8,128)(2,1)S(1)} %get-tuple-element.20), channel_id=1, source_target_pairs={{1,0},{2,1},{3,2},{0,3},{5,4},{6,5},{7,6},{4,7},{9,8},{10,9},{11,1... | collective-permute-start | bytes 466952 | tf_op jit(solution)/shard_map/ppermute | solution.py:56
  23.3 5.3 %inner_sums.1 = (f32[2,40,128]{2,1,0:T(8,128)S(1)}, f32[14,40,128]{2,1,0:T(8,128)S(1)}) custom-call(f32[3,16,32,128]{3,2,1,0:T(8,128)S(1)} %get-tuple-element.21.vel_ref, f32[3,16,4,128]{3,2,1,0:T(4,128)S(1)} %collective-permute-done.4.low_ref, f32[3,16,4,128]{3,2,1,0:T(4,128)S(1)} %collective-permute-done.5.high_ref), custom_call_target="tpu_custom_call" | custom-call | tf_op jit(solution)/shard_map/inner_sums/pallas_call | solution.py:277
  28.6 0.0 collective-permute-done.7.refs_5_
  28.6 5.4 %outer_sums.1 = (f32[2,40,128]{2,1,0:T(8,128)S(1)}, f32[4,40,128]{2,1,0:T(8,128)S(1)}) custom-call(f32[3,2,40,128]{3,2,1,0:T(8,128)S(1)} %collective-permute-done.6.refs_0_, f32[3,2,40,128]{3,2,1,0:T(8,128)S(1)} %get-tuple-element.25.refs_1_, f32[3,2,40,128]{3,2,1,0:T(8,128)S(1)} %get-tuple-element.26.refs_2_, ...), custom_call_target="tpu_custom_call" | custom-call | tf_op jit(solution)/shard_map/outer_sums/pallas_call | solution.py:313
  34.0 0.2 collective-permute-start.8
  34.1 3.9 %collective-permute-done.8 = f32[2,40,128]{2,1,0:T(8,128)S(1)} collective-permute-done((f32[2,40,128]{2,1,0:T(8,128)S(1)}, f32[2,40,128]{2,1,0:T(8,128)S(1)}, u32[]{:S(2)}, u32[]{:S(2)}) %collective-permute-start.8) | collective-permute-done | bytes 40992 | tf_op jit(solution)/shard_map/ppermute | solution.py:661
  38.0 0.3 collective-permute-start.9
  38.3 3.7 %collective-permute-done.9 = f32[2,40,128]{2,1,0:T(8,128)S(1)} collective-permute-done((f32[2,40,128]{2,1,0:T(8,128)S(1)}, f32[2,40,128]{2,1,0:T(8,128)S(1)}, u32[]{:S(2)}, u32[]{:S(2)}) %collective-permute-start.9) | collective-permute-done | bytes 40992 | tf_op jit(solution)/shard_map/ppermute | solution.py:661
  42.0 1.4 %collective-permute-start.10 = (f32[2,40,128]{2,1,0:T(8,128)S(1)}, f32[2,40,128]{2,1,0:T(8,128)S(1)}, u32[]{:S(2)}, u32[]{:S(2)}) collective-permute-start(f32[2,40,128]{2,1,0:T(8,128)S(1)} %add.10), channel_id=1, source_target_pairs={{0,16},{4,20},{8,24},{12,28},{16,0},{20,4},{24,8},{28,12},{1,17},{... | collective-permute-start | bytes 122888 | tf_op jit(solution)/shard_map/ppermute | solution.py:661
  43.5 3.6 %collective-permute-done.10 = f32[2,40,128]{2,1,0:T(8,128)S(1)} collective-permute-done((f32[2,40,128]{2,1,0:T(8,128)S(1)}, f32[2,40,128]{2,1,0:T(8,128)S(1)}, u32[]{:S(2)}, u32[]{:S(2)}) %collective-permute-start.10) | collective-permute-done | bytes 40992 | tf_op jit(solution)/shard_map/ppermute | solution.py:661
  47.1 0.0 collective-permute-done.2.before_ref
  47.1 0.0 collective-permute-done.3.after_ref
  47.1 7.8 %step.1 = (bf16[19,16,32,128]{3,2,1,0:T(8,128)(2,1)}, f32[32,128]{1,0:T(8,128)}, f32[32,1,128]{2,1,0:T(1,128)S(1)}) custom-call(bf16[19,16,32,128]{3,2,1,0:T(8,128)(2,1)S(1)} %copy-done.1, bf16[19,1,32,128]{3,2,1,0:T(8,128)(2,1)S(1)} %collective-permute-done.low_hbm, bf16[19,1,32,128]{3,2,1,0:T(8,128)(2,1)S(1)} %collective-permute-done.1.high_hbm, ...), custom_call_target="tpu_custom_call" | custom-call | tf_op jit(solution)/shard_map/step/pallas_call | solution.py:624
  54.9 11.8 %all_to_all.5.arrived_ref = f32[32,1,128]{2,1,0:T(1,128)} all-to-all(f32[32,1,128]{2,1,0:T(1,128)S(1)} %get-tuple-element.34), channel_id=1, replica_groups=mesh['span'=8,'cross'=4] {'span','cross'}, dimensions={0} | all-to-all | bytes 32768 | tf_op jit(solution)/shard_map/all_to_all | solution.py:692
  66.7 1.4 %finish.1 = f32[3,8]{1,0:T(4,128)} custom-call(f32[32,1,128]{2,1,0:T(1,128)} %all_to_all.5.arrived_ref), custom_call_target="tpu_custom_call" | custom-call | tf_op jit(solution)/shard_map/finish/pallas_call | solution.py:693
  (12 shorter events, 0.1 us)
Async XLA Ops:
  0.6 1.7 %copy-start = (bf16[19,16,32,128]{3,2,1,0:T(8,128)(2,1)S(1)}, bf16[19,16,32,128]{3,2,1,0:T(8,128)(2,1)}, u32[]{:S(2)}) copy-start(bf16[19,16,32,128]{3,2,1,0:T(8,128)(2,1)} %pops_hbm.5) | copy-start | bytes 7471108
  2.3 18.4 %copy-start.1 = (bf16[19,16,32,128]{3,2,1,0:T(8,128)(2,1)S(1)}, bf16[19,16,32,128]{3,2,1,0:T(8,128)(2,1)}, u32[]{:S(2)}) copy-start(bf16[19,16,32,128]{3,2,1,0:T(8,128)(2,1)} %pops_hbm.5) | copy-start | bytes 7471108
  3.2 7.9 %collective-permute-start.4 = (f32[3,16,4,128]{3,2,1,0:T(4,128)S(1)}, f32[3,16,4,128]{3,2,1,0:T(4,128)S(1)}, u32[]{:S(2)}, u32[]{:S(2)}) collective-permute-start(f32[3,16,4,128]{3,2,1,0:T(4,128)S(1)} %get-tuple-element.22), channel_id=1, source_target_pairs={{0,1},{1,2},{2,3},{3,0},{4,5},{5,6},{6,7},{7,4},{8,9},{9,10},{10,1... | collective-permute-start | bytes 294920 | tf_op jit(solution)/shard_map/ppermute | solution.py:55
  3.7 7.4 %collective-permute-start.5 = (f32[3,16,4,128]{3,2,1,0:T(4,128)S(1)}, f32[3,16,4,128]{3,2,1,0:T(4,128)S(1)}, u32[]{:S(2)}, u32[]{:S(2)}) collective-permute-start(f32[3,16,4,128]{3,2,1,0:T(4,128)S(1)} %get-tuple-element.23), channel_id=1, source_target_pairs={{1,0},{2,1},{3,2},{0,3},{5,4},{6,5},{7,6},{4,7},{9,8},{10,9},{11,1... | collective-permute-start | bytes 294920 | tf_op jit(solution)/shard_map/ppermute | solution.py:56
  5.8 10.2 %collective-permute-start.1 = (bf16[19,1,32,128]{3,2,1,0:T(8,128)(2,1)S(1)}, bf16[19,1,32,128]{3,2,1,0:T(8,128)(2,1)S(1)}, u32[]{:S(2)}, u32[]{:S(2)}) collective-permute-start(bf16[19,1,32,128]{3,2,1,0:T(8,128)(2,1)S(1)} %get-tuple-element.35), channel_id=1, source_target_pairs={{4,0},{8,4},{12,8},{16,12},{20,16},{24,20},{28,24},{0,28},{5,1},{9... | collective-permute-start | bytes 466952 | tf_op jit(solution)/shard_map/ppermute | solution.py:56
  11.1 9.7 %collective-permute-start = (bf16[19,1,32,128]{3,2,1,0:T(8,128)(2,1)S(1)}, bf16[19,1,32,128]{3,2,1,0:T(8,128)(2,1)S(1)}, u32[]{:S(2)}, u32[]{:S(2)}) collective-permute-start(bf16[19,1,32,128]{3,2,1,0:T(8,128)(2,1)S(1)} %get-tuple-element.36), channel_id=1, source_target_pairs={{0,4},{4,8},{8,12},{12,16},{16,20},{20,24},{24,28},{28,0},{1,5},{5... | collective-permute-start | bytes 466952 | tf_op jit(solution)/shard_map/ppermute | solution.py:55
  11.2 36.0 %copy-start.2 = (s32[128,8]{0,1:T(8,128)S(1)}, s32[128,8]{0,1:T(8,128)}, u32[]{:S(2)}) copy-start(s32[128,8]{0,1:T(8,128)} %param.5) | copy-start | bytes 12292
  11.2 36.0 %copy-start.3 = (f32[128,8]{0,1:T(8,128)S(1)}, f32[128,8]{0,1:T(8,128)}, u32[]{:S(2)}) copy-start(f32[128,8]{0,1:T(8,128)} %param.6) | copy-start | bytes 12292
  11.2 36.0 %copy-start.4 = (s32[128]{0:T(128)S(1)}, s32[128]{0:T(128)}, u32[]{:S(2)}) copy-start(s32[128]{0:T(128)} %param.7) | copy-start | bytes 1540
  11.2 17.4 %collective-permute-start.6 = (f32[3,2,40,128]{3,2,1,0:T(8,128)S(1)}, f32[3,2,40,128]{3,2,1,0:T(8,128)S(1)}, u32[]{:S(2)}, u32[]{:S(2)}) collective-permute-start(f32[3,2,40,128]{3,2,1,0:T(8,128)S(1)} %get-tuple-element.24.refs_4_), channel_id=1, source_target_pairs={{0,4},{4,8},{8,12},{12,16},{16,20},{20,24},{24,28},{28,0},{1,5},{5... | collective-permute-start | bytes 368648 | tf_op jit(solution)/shard_map/ppermute | solution.py:55
  11.3 17.3 %collective-permute-start.7 = (f32[3,2,40,128]{3,2,1,0:T(8,128)S(1)}, f32[3,2,40,128]{3,2,1,0:T(8,128)S(1)}, u32[]{:S(2)}, u32[]{:S(2)}) collective-permute-start(f32[3,2,40,128]{3,2,1,0:T(8,128)S(1)} %get-tuple-element.25.refs_1_), channel_id=1, source_target_pairs={{4,0},{8,4},{12,8},{16,12},{20,16},{24,20},{28,24},{0,28},{5,1},{9... | collective-permute-start | bytes 368648 | tf_op jit(solution)/shard_map/ppermute | solution.py:56
  21.5 25.6 %collective-permute-start.2 = (bf16[19,32,128]{2,1,0:T(8,128)(2,1)S(1)}, bf16[19,32,128]{2,1,0:T(8,128)(2,1)S(1)}, u32[]{:S(2)}, u32[]{:S(2)}) collective-permute-start(bf16[19,32,128]{2,1,0:T(8,128)(2,1)S(1)} %get-tuple-element.19), channel_id=1, source_target_pairs={{0,1},{1,2},{2,3},{3,0},{4,5},{5,6},{6,7},{7,4},{8,9},{9,10},{10,1... | collective-permute-start | bytes 466952 | tf_op jit(solution)/shard_map/ppermute | solution.py:55
  21.5 25.6 %collective-permute-start.3 = (bf16[19,32,128]{2,1,0:T(8,128)(2,1)S(1)}, bf16[19,32,128]{2,1,0:T(8,128)(2,1)S(1)}, u32[]{:S(2)}, u32[]{:S(2)}) collective-permute-start(bf16[19,32,128]{2,1,0:T(8,128)(2,1)S(1)} %get-tuple-element.20), channel_id=1, source_target_pairs={{1,0},{2,1},{3,2},{0,3},{5,4},{6,5},{7,6},{4,7},{9,8},{10,9},{11,1... | collective-permute-start | bytes 466952 | tf_op jit(solution)/shard_map/ppermute | solution.py:56
  34.0 4.1 %collective-permute-start.8 = (f32[2,40,128]{2,1,0:T(8,128)S(1)}, f32[2,40,128]{2,1,0:T(8,128)S(1)}, u32[]{:S(2)}, u32[]{:S(2)}) collective-permute-start(f32[2,40,128]{2,1,0:T(8,128)S(1)} %get-tuple-element.29), channel_id=1, source_target_pairs={{0,4},{4,0},{8,12},{12,8},{16,20},{20,16},{24,28},{28,24},{1,5},{5... | collective-permute-start | bytes 122888 | tf_op jit(solution)/shard_map/ppermute | solution.py:661
  38.0 4.0 %collective-permute-start.9 = (f32[2,40,128]{2,1,0:T(8,128)S(1)}, f32[2,40,128]{2,1,0:T(8,128)S(1)}, u32[]{:S(2)}, u32[]{:S(2)}) collective-permute-start(f32[2,40,128]{2,1,0:T(8,128)S(1)} %add.9), channel_id=1, source_target_pairs={{0,8},{4,12},{8,0},{12,4},{16,24},{20,28},{24,16},{28,20},{1,9},{5... | collective-permute-start | bytes 122888 | tf_op jit(solution)/shard_map/ppermute | solution.py:661
  42.0 5.0 %collective-permute-start.10 = (f32[2,40,128]{2,1,0:T(8,128)S(1)}, f32[2,40,128]{2,1,0:T(8,128)S(1)}, u32[]{:S(2)}, u32[]{:S(2)}) collective-permute-start(f32[2,40,128]{2,1,0:T(8,128)S(1)} %add.10), channel_id=1, source_target_pairs={{0,16},{4,20},{8,24},{12,28},{16,0},{20,4},{24,8},{28,12},{1,17},{... | collective-permute-start | bytes 122888 | tf_op jit(solution)/shard_map/ppermute | solution.py:661
where the time goes:
time: 68.4 us; the launch traced here: 68.1 us
  Pallas kernels  21.5 us (31%)
  starting transfers between devices  16.3 us (24%)
  waiting for transfers between devices  16 us (23%)
  blocking collectives  11.8 us (17%)
  local copies, waits for them, and re-layouts  1.74 us (3%)
  between operations  0.79 us (1%)
    ppermute x4, starting transfers between devices, exchange(): high = lax.ppermute(first, axis, backward)  13.8 us
    all_to_all x1, blocking collectives, local(): arrived = lax.all_to_all(packed, ('span', 'cross'), 0, 0)  11.8 us
    ppermute x3, waiting for transfers between devices, span_sum(): values = values + lax.ppermute(values, 'span', pairs)  11.3 us
    pallas_call x1, Pallas kernels, step(): pl.pallas_call(step_kernel, out_shape=(full(populations.shape, jnp.bfloat...  7.77 us
    pallas_call x1, Pallas kernels, outer_sums(): pl.pallas_call(outer_kernel, out_shape=(full((2, EXT, LANES), jnp.float32...  5.39 us
    pallas_call x1, Pallas kernels, inner_sums(): pl.pallas_call(inner_kernel, out_shape=(full((2, EXT, LANES), jnp.float32...  5.29 us
    ppermute x4, waiting for transfers between devices, exchange(): low = lax.ppermute(last, axis, forward)  4.73 us
    ppermute x3, starting transfers between devices, span_sum(): values = values + lax.ppermute(values, 'span', pairs)  1.84 us
  transfers between devices with their start and end apart: 11, of which 4 were waited for; matrix products, arithmetic and copies ran while one was open for 0% of the time, Pallas kernels for 17%

commit v1 on v0

v1 whole, which is shorter than its diff:
```python
import functools

import jax
import jax.numpy as jnp
from jax import lax
from jax.experimental import pallas as pl
from jax.experimental.pallas import tpu as pltpu
from jax.sharding import PartitionSpec as P

SEG_DEV = 8
LANES = 128
HALO = 3
EXT = 40
PAD = 56
OWN = 10
TOP = 8
CHUNKS = (8, 16, 24, 32, 40)
VMEM = 28 * 1024 * 1024

eps_sum = 1e-06
base_visc = 0.005

VELOCITIES = [
    [0, 0, 0],
    [1, 0, 0],
    [-1, 0, 0],
    [0, 1, 0],
    [0, -1, 0],
    [0, 0, 1],
    [0, 0, -1],
    [1, 1, 0],
    [-1, -1, 0],
    [1, -1, 0],
    [-1, 1, 0],
    [1, 0, 1],
    [-1, 0, -1],
    [1, 0, -1],
    [-1, 0, 1],
    [0, 1, 1],
    [0, -1, -1],
    [0, 1, -1],
    [0, -1, 1],
]


def neighbours(axis):
    count = lax.axis_size(axis)
    forward = [(i, (i + 1) % count) for i in range(count)]
    backward = [(target, source) for source, target in forward]
    return forward, backward


def exchange(first, last, axis):
    forward, backward = neighbours(axis)
    low = lax.ppermute(last, axis, forward)
    high = lax.ppermute(first, axis, backward)
    return low, high


def full(shape, dtype):
    return jax.ShapeDtypeStruct(shape, dtype)


def in_vmem(count):
    return [pl.BlockSpec(memory_space=pltpu.VMEM)] * count


def params():
    return pltpu.CompilerParams(vmem_limit_bytes=VMEM)


def cost(micros):
    return pl.CostEstimate(flops=0, bytes_accessed=int(micros * 3.6e6), transcendentals=0)


def plus(array):
    return pltpu.roll(array, LANES - 1, 1)


def minus(array):
    return pltpu.roll(array, 1, 1)


def split(value):
    high = value.astype(jnp.bfloat16)
    return high, (value - high.astype(jnp.float32)).astype(jnp.bfloat16)


def join(high, low):
    return high.astype(jnp.float32) + low.astype(jnp.float32)


def moments_kernel(pops, vel_ref, y_first, y_last, z_first, z_last, rows):
    depth, width = pops.shape[1:3]

    def plane(z, carry):
        for half in range(width // 16):
            at = pl.ds(16 * half, 16)
            f = [pops[q, z, at, :].astype(jnp.float32) for q in range(19)]
            flux = [0.0, 0.0, 0.0]
            density = f[0]
            for q in range(1, 19, 2):
                even, odd = f[q] + f[q + 1], f[q] - f[q + 1]
                density = density + even
                for dim in range(3):
                    sign = VELOCITIES[q][dim]
                    if sign:
                        flux[dim] = flux[dim] + odd if sign > 0 else flux[dim] - odd
            inverse = 1.0 / density
            for dim in range(3):
                speed = flux[dim] * inverse
                vel_ref[dim, z, at, :] = speed
                for k in range(HALO):
                    if half == 0:
                        rows[0, dim * HALO + k, pl.ds(z, 1), :] = speed[k : k + 1]
                    if half == width // 16 - 1:
                        rows[1, dim * HALO + k, pl.ds(z, 1), :] = speed[15 - k : 16 - k]
        return carry

    lax.fori_loop(0, depth, plane, 0)
    for side, out in enumerate((y_first, y_last)):
        for dim in range(3):
            line = [rows[side, dim * HALO + k] for k in range(HALO)]
            out[4 * dim], out[4 * dim + 1] = split(line[0])
            for k in range(1, HALO):
                out[4 * dim + 1 + k] = (line[k] - line[k - 1]).astype(jnp.bfloat16)
    for near, far, out in ((0, 1, z_first), (depth - 1, depth - 2, z_last)):
        for dim in range(3):
            layer = vel_ref[dim, near]
            out[3 * dim], out[3 * dim + 1] = split(layer)
            out[3 * dim + 2] = (vel_ref[dim, far] - layer).astype(jnp.bfloat16)


def block_moments(populations):
    _, depth, width, lanes = populations.shape
    y_edge = full((12, depth, lanes), jnp.bfloat16)
    z_edge = full((9, width, lanes), jnp.bfloat16)
    return pl.pallas_call(
        moments_kernel,
        out_shape=(full((3, depth, width, lanes), jnp.float32), y_edge, y_edge, z_edge, z_edge),
        in_specs=in_vmem(1),
        out_specs=tuple(in_vmem(5)),
        scratch_shapes=[pltpu.VMEM((2, 3 * HALO, depth, lanes), jnp.float32)],
        compiler_params=params(),
        cost_estimate=cost(1),
        name="moments",
    )(populations)


def decode_rows(message, rows, side):
    for dim in range(3):
        line = join(message[4 * dim], message[4 * dim + 1])
        rows[side, dim * HALO] = line
        for k in range(1, HALO):
            line = line + message[4 * dim + 1 + k].astype(jnp.float32)
            rows[side, dim * HALO + k] = line


def place_plane(ext, p, vel_ref, rows, z):
    width = vel_ref.shape[2]
    for dim in range(3):
        ext[dim, p, pl.ds(OWN, width), :] = vel_ref[dim, z]
        for k in range(HALO):
            line = pl.ds(z, 1)
            ext[dim, p, pl.ds(OWN - 1 - k, 1), :] = rows[0, dim * HALO + k, line, :]
            ext[dim, p, pl.ds(OWN + width + k, 1), :] = rows[1, dim * HALO + k, line, :]


NOTE = 48
NOTE_ROWS = 72


def edges_kernel(low_ref, high_ref, cell_ref, weight_ref, segment_ref, first, last, rows):
    depth = low_ref.shape[1]
    decode_rows(low_ref, rows, 0)
    decode_rows(high_ref, rows, 1)
    taps = cell_ref.shape[0]
    for planes, out in (((0, 1), first), ((depth - 1, depth - 2), last)):
        out[...] = jnp.zeros_like(out)
        for dim in range(3):
            for index, z in enumerate(planes):
                for side in range(2):
                    for k in range(HALO):
                        row = 16 * dim + 8 * index + HALO * side + k
                        out[pl.ds(row, 1), :] = rows[side, dim * HALO + k, pl.ds(z, 1), :]
        out[pl.ds(NOTE, taps), :] = cell_ref[...].astype(jnp.float32)
        out[pl.ds(NOTE + taps, taps), :] = weight_ref[...]
        out[pl.ds(NOTE + 2 * taps, 1), :] = segment_ref[...].astype(jnp.float32)


def edge_notes(low, high, cells, weights, segments):
    note = full((NOTE_ROWS, LANES), jnp.float32)
    return pl.pallas_call(
        edges_kernel,
        out_shape=(note, note),
        in_specs=in_vmem(5),
        out_specs=tuple(in_vmem(2)),
        scratch_shapes=[pltpu.VMEM((2, 3 * HALO, low.shape[1], LANES), jnp.float32)],
        compiler_params=params(),
        cost_estimate=cost(0.2),
        name="edges",
    )(low, high, cells, weights, segments)


def strain_parts(ref, p, row):
    grads = []
    for dim in range(3):
        here = ref[dim, p, pl.ds(row, 8), :]
        grads.append(
            (
                plus(here) - minus(here),
                ref[dim, p, pl.ds(row + 1, 8), :] - ref[dim, p, pl.ds(row - 1, 8), :],
                ref[dim, p + 1, pl.ds(row, 8), :] - ref[dim, p - 1, pl.ds(row, 8), :],
            )
        )
    parts = [
        grads[0][0],
        grads[1][1],
        grads[2][2],
        grads[0][1] + grads[1][0],
        grads[0][2] + grads[2][0],
        grads[1][2] + grads[2][1],
    ]
    straight = parts[0] * parts[0] + parts[1] * parts[1] + parts[2] * parts[2]
    mixed = parts[3] * parts[3] + parts[4] * parts[4] + parts[5] * parts[5]
    return parts, jnp.sqrt(0.5 * straight + 0.25 * mixed)


def weigh(low, middle, high):
    return (low + high) + (middle + middle)


PAIRS = ((0, 0), (1, 1), (2, 2), (0, 1), (0, 2), (1, 2))


def model_sums(planes, ext, hat, prods, zsum, acc_ref, store_mag):
    def first_pass(p, carry):
        for row in CHUNKS:
            rows = pl.ds(row, 8)
            parts, size = strain_parts(ext, p, row)
            store_mag(p, row, size)
            for k in range(6):
                prods[k, p, rows, :] = size * parts[k]
            for k, (i, j) in enumerate(PAIRS):
                prods[6 + k, p, rows, :] = ext[i, p, rows, :] * ext[j, p, rows, :]
            for dim in range(3):
                lines = []
                for shift in (-1, 0, 1):
                    at = pl.ds(row + shift, 8)
                    lines.append(
                        weigh(ext[dim, p - 1, at, :], ext[dim, p, at, :], ext[dim, p + 1, at, :])
                    )
                line = weigh(*lines)
                hat[dim, p, rows, :] = (1.0 / 64.0) * weigh(minus(line), line, plus(line))
        return carry

    lax.fori_loop(1, planes - 1, first_pass, 0)

    def second_pass(p, carry):
        for row in CHUNKS:
            rows = pl.ds(row, 8)
            for k in range(12):
                zsum[k, rows, :] = weigh(
                    prods[k, p - 1, rows, :], prods[k, p, rows, :], prods[k, p + 1, rows, :]
                )
        for row in CHUNKS:
            rows = pl.ds(row, 8)
            parts, size = strain_parts(hat, p, row)
            size = 256.0 * size
            here = [hat[dim, p, rows, :] for dim in range(3)]
            scaled = [64.0 * speed for speed in here]
            smooth = []
            for k in range(12):
                line = weigh(
                    zsum[k, pl.ds(row - 1, 8), :], zsum[k, rows, :], zsum[k, pl.ds(row + 1, 8), :]
                )
                smooth.append(weigh(minus(line), line, plus(line)))
            lm = 0.0
            squares = [0.0, 0.0]
            for k, (i, j) in enumerate(PAIRS):
                model = smooth[k] - size * parts[k]
                leonard = smooth[6 + k] - scaled[i] * here[j]
                lm = lm + leonard * model
                squares[k // 3] = squares[k // 3] + model * model
            out = pl.ds(row - TOP, 8)
            acc_ref[0, out, :] += (1.0 / 4096.0) * lm
            acc_ref[1, out, :] += (1.0 / 4096.0) * (squares[0] + 0.5 * squares[1])
        return carry

    lax.fori_loop(2, planes - 2, second_pass, 0)


def inner_kernel(vel_ref, low_ref, high_ref, acc_ref, mag_ref, ext, hat, prods, zsum, rows):
    depth = vel_ref.shape[1]
    decode_rows(low_ref, rows, 0)
    decode_rows(high_ref, rows, 1)

    def assemble(p, carry):
        place_plane(ext, p, vel_ref, rows, p)
        return carry

    lax.fori_loop(0, depth, assemble, 0)
    acc_ref[...] = jnp.zeros_like(acc_ref)

    def store_mag(p, row, size):
        mag_ref[p - 1, pl.ds(row - TOP, 8), :] = size

    model_sums(depth, ext, hat, prods, zsum, acc_ref, store_mag)


def model_scratch(planes, depth):
    return [
        pltpu.VMEM((3, planes, PAD, LANES), jnp.float32),
        pltpu.VMEM((3, planes, PAD, LANES), jnp.float32),
        pltpu.VMEM((12, planes, PAD, LANES), jnp.float32),
        pltpu.VMEM((12, PAD, LANES), jnp.float32),
        pltpu.VMEM((2, 3 * HALO, depth, LANES), jnp.float32),
    ]


def inner_sums(vel, low, high):
    depth = vel.shape[1]
    return pl.pallas_call(
        inner_kernel,
        out_shape=(
            full((2, EXT, LANES), jnp.float32),
            full((depth - 2, EXT, LANES), jnp.float32),
        ),
        in_specs=in_vmem(3),
        out_specs=tuple(in_vmem(2)),
        scratch_shapes=model_scratch(depth, depth),
        compiler_params=params(),
        cost_estimate=cost(5),
        name="inner_sums",
    )(vel, low, high)


def outer_kernel(
    vel_ref,
    low_ref,
    high_ref,
    below_ref,
    above_ref,
    note_below,
    note_above,
    partial_ref,
    sums_ref,
    mag_ref,
    ext,
    hat,
    prods,
    zsum,
    rows,
    acc,
):
    depth, width = vel_ref.shape[1:3]
    decode_rows(low_ref, rows, 0)
    decode_rows(high_ref, rows, 1)
    acc[...] = partial_ref[...]
    for side, (message, note, places, start) in enumerate(
        ((below_ref, note_below, (1, 0), 0), (above_ref, note_above, (4, 5), depth - 4))
    ):
        for index in range(4):
            place_plane(ext, index + (2 if side == 0 else 0), vel_ref, rows, start + index)
        for dim in range(3):
            near = join(message[3 * dim], message[3 * dim + 1])
            far = near + message[3 * dim + 2].astype(jnp.float32)
            for index, (p, layer) in enumerate(zip(places, (near, far))):
                ext[dim, p, pl.ds(OWN, width), :] = layer
                row = 16 * dim + 8 * index
                for k in range(HALO):
                    ext[dim, p, pl.ds(OWN - 1 - k, 1), :] = note[pl.ds(row + k, 1), :]
                    ext[dim, p, pl.ds(OWN + width + k, 1), :] = note[pl.ds(row + HALO + k, 1), :]

        def store_mag(p, row, size):
            mag_ref[4 * side + p - 1, pl.ds(row - TOP, 8), :] = size

        model_sums(6, ext, hat, prods, zsum, acc, store_mag)
    lines = width + 2
    sums_ref[...] = jnp.zeros_like(sums_ref)
    for index in range(2):
        sums_ref[pl.ds(index * lines, lines), :] = acc[index, pl.ds(OWN - TOP - 1, lines), :]


def outer_sums(vel, low, high, below, above, note_below, note_above, partial):
    depth, width = vel.shape[1:3]
    return pl.pallas_call(
        outer_kernel,
        out_shape=(
            full((-(-2 * (width + 2) // 8) * 8, LANES), jnp.float32),
            full((8, EXT, LANES), jnp.float32),
        ),
        in_specs=in_vmem(8),
        out_specs=tuple(in_vmem(2)),
        scratch_shapes=model_scratch(6, depth) + [pltpu.VMEM((2, EXT, LANES), jnp.float32)],
        compiler_params=params(),
        cost_estimate=cost(2),
        name="outer_sums",
    )(vel, low, high, below, above, note_below, note_above, partial)


def rows_kernel(pops, after_this, first_ref, last_ref, rows):
    depth, width = pops.shape[1:3]

    def plane(z, carry):
        for q in range(19):
            low = pops[q, z, pl.ds(0, 16), :].astype(jnp.float32)
            high = pops[q, z, pl.ds(width - 16, 16), :].astype(jnp.float32)
            rows[0, q, pl.ds(z, 1), :] = low[:1]
            rows[1, q, pl.ds(z, 1), :] = high[15:]
        return carry

    lax.fori_loop(0, depth, plane, 0)
    first_ref[...] = rows[0].astype(jnp.bfloat16)
    last_ref[...] = rows[1].astype(jnp.bfloat16)


def face_rows(populations, after_this):
    _, depth, width, lanes = populations.shape
    edge = full((19, depth, lanes), jnp.bfloat16)
    return pl.pallas_call(
        rows_kernel,
        out_shape=(edge, edge),
        in_specs=in_vmem(1) + [pl.BlockSpec(memory_space=pl.ANY)],
        out_specs=tuple(in_vmem(2)),
        scratch_shapes=[pltpu.VMEM((2, 19, depth, lanes), jnp.float32)],
        compiler_params=params(),
        cost_estimate=cost(0.5),
        name="face_rows",
    )(populations, after_this)


def relax_parts(f):
    even = {q: f[q] + f[q + 1] for q in range(1, 19, 2)}
    odd = {q: f[q] - f[q + 1] for q in range(1, 19, 2)}
    x_xy, x_xz = odd[7] + odd[9], odd[11] + odd[13]
    y_yz, y_xy = odd[15] + odd[17], odd[7] - odd[9]
    z_xz, z_yz = odd[11] - odd[13], odd[15] - odd[17]
    flux, up, down, axis_odd = [], [], [], []
    for first, second, along in ((x_xy, x_xz, 1), (y_yz, y_xy, 3), (z_xz, z_yz, 5)):
        sides = first + second
        total = odd[along] + sides
        heat = 0.15 * (sides - (2.0 / 3.0) * total)
        twist = (1.98 / 8.0) * (first - second)
        flux.append(total)
        up.append(heat + twist)
        down.append(heat - twist)
        axis_odd.append(4.0 * heat)
    a, b, c = even[7] + even[9], even[11] + even[13], even[15] + even[17]
    axes = even[1] + even[3] + even[5]
    diagonals = a + b + c
    density = f[0] + axes + diagonals
    inverse = 1.0 / density
    speed = [total * inverse for total in flux]
    square = [total * part for total, part in zip(flux, speed)]
    energy = square[0] + square[1] + square[2]
    d_e = (1.19 / 126.0) * (diagonals - f[0] - energy)
    d_eps = (1.4 / 252.0) * (9.0 * f[0] - 7.0 * axes - 2.0 * diagonals + 5.5 * energy)
    ax_n, dg_n, eq_n = 3.0 * even[1] - axes, diagonals - 3.0 * c, 3.0 * square[0] - energy
    ax_w, dg_w, eq_w = even[3] - even[5], a - b, square[1] - square[2]
    d_pn = (1.4 / 72.0) * (dg_n - 2.0 * ax_n + 0.5 * eq_n)
    d_pw = (1.4 / 24.0) * (dg_w - 2.0 * ax_w + 0.5 * eq_w)
    shear = [
        (1.0 / 36.0) * (ax_n + dg_n - eq_n),
        (1.0 / 12.0) * (ax_w + dg_w - eq_w),
        0.25 * (even[7] - even[9] - flux[0] * speed[1]),
        0.25 * (even[11] - even[13] - flux[0] * speed[2]),
        0.25 * (even[15] - even[17] - flux[1] * speed[2]),
    ]
    base_axis = 11.0 * d_e + 4.0 * d_eps
    base_diag = -8.0 * d_e - d_eps
    base = [None] * 19
    base[0] = f[0] + (30.0 * d_e - 12.0 * d_eps)
    rest = base_axis - 2.0 * d_pn
    for q, change, skew in (
        (1, base_axis + 4.0 * d_pn, axis_odd[0]),
        (3, rest + 2.0 * d_pw, axis_odd[1]),
        (5, rest - 2.0 * d_pw, axis_odd[2]),
    ):
        base[q] = f[q] + (change + skew)
        base[q + 1] = f[q + 1] + (change - skew)
    rest = base_diag - d_pn
    for q, change, one, two in (
        (7, rest - d_pw, up[0], down[1]),
        (11, rest + d_pw, down[0], up[2]),
        (15, base_diag + 2.0 * d_pn, up[1], down[2]),
    ):
        same, other = one + two, one - two
        base[q] = f[q] + (change - same)
        base[q + 1] = f[q + 1] + (change + same)
        base[q + 2] = f[q + 2] + (change - other)
        base[q + 3] = f[q + 3] + (change + other)
    return base, shear


def shear_changes(shear, rate):
    n, w, xy, xz, yz = [rate * part for part in shear]
    lean = n + w
    tilt = n - w
    twice = n + n
    changes = [None] * 19
    changes[1] = changes[2] = -twice
    changes[3] = changes[4] = tilt
    changes[5] = changes[6] = lean
    changes[7] = changes[8] = -(lean + xy)
    changes[9] = changes[10] = xy - lean
    changes[11] = changes[12] = -(tilt + xz)
    changes[13] = changes[14] = xz - tilt
    changes[15] = changes[16] = twice - yz
    changes[17] = changes[18] = twice + yz
    return changes


def relax_rate(eddy, size):
    return 1.0 / (0.5 + 3.0 * (base_visc + eddy * size))


BEFORE = [q for q in range(19) if VELOCITIES[q][1] > 0]
AFTER = [q for q in range(19) if VELOCITIES[q][1] < 0]
RISING = [q for q in range(19) if VELOCITIES[q][2] > 0]
FALLING = [q for q in range(19) if VELOCITIES[q][2] < 0]
FIRST = 8


def ready_kernel(pops, before_ref, after_ref, after_this, base_ref, shear_ref, edge_ref, edge_shear):
    depth, width = pops.shape[1:3]
    for side, (source, wanted) in enumerate(((before_ref, BEFORE), (after_ref, AFTER))):
        base, shear = relax_parts([source[q].astype(jnp.float32) for q in range(19)])
        for index, q in enumerate(wanted):
            edge_ref[side, index] = base[q]
        for k in range(5):
            edge_shear[side, k] = shear[k]

    def plane(z, carry):
        for half in range(width // 16):
            rows = pl.ds(16 * half, 16)
            base, shear = relax_parts([pops[q, z, rows, :].astype(jnp.float32) for q in range(19)])
            for q in range(19):
                base_ref[q, z, rows, :] = base[q]
            for k in range(5):
                shear_ref[k, z, rows, :] = shear[k]
        return carry

    lax.fori_loop(0, depth, plane, 0)


def ready(populations, before, after, after_this):
    _, depth, width, lanes = populations.shape
    return pl.pallas_call(
        ready_kernel,
        out_shape=(
            full((19, depth, width, lanes), jnp.float32),
            full((5, depth, width, lanes), jnp.float32),
            full((2, 5, depth, lanes), jnp.float32),
            full((2, 5, depth, lanes), jnp.float32),
        ),
        in_specs=in_vmem(3) + [pl.BlockSpec(memory_space=pl.ANY)],
        out_specs=tuple(in_vmem(4)),
        compiler_params=params(),
        cost_estimate=cost(2.5),
        name="ready",
    )(populations, before, after, after_this)


def table_rows(table, at, flux):
    for dim in range(3):
        coarse, fine = split(flux[dim])
        table[0, at, dim * LANES : (dim + 1) * LANES] = coarse
        table[1, at, dim * LANES : (dim + 1) * LANES] = fine


def add_flux(flux, q, moved):
    for dim in range(3):
        sign = VELOCITIES[q][dim]
        if sign:
            flux[dim] = flux[dim] + moved if sign > 0 else flux[dim] - moved


def marker_force(table, start, rows, cells, weights):
    taps, markers = cells.shape
    row_of = lax.broadcasted_iota(jnp.int32, (rows, markers), 0) + start
    lane_of = lax.broadcasted_iota(jnp.int32, (LANES, markers), 0)
    contract = (((0,), (0,)), ((), ()))
    force = [jnp.zeros((1, markers), jnp.float32) for _ in range(3)]
    for tap in range(taps):
        cell = cells[tap : tap + 1, :]
        row, lane = lax.shift_right_logical(cell, 7), lax.bitwise_and(cell, LANES - 1)
        pick = jnp.where(row_of == row, 1.0, 0.0).astype(jnp.bfloat16)
        picked = lax.dot_general(
            table[0], pick, contract, preferred_element_type=jnp.float32
        ) + lax.dot_general(table[1], pick, contract, preferred_element_type=jnp.float32)
        weight = jnp.where(lane_of == lane, -weights[tap : tap + 1, :], 0.0)
        for dim in range(3):
            lanes = picked[dim * LANES : (dim + 1) * LANES, :]
            force[dim] = force[dim] + jnp.sum(lanes * weight, axis=0, keepdims=True)
    return jnp.concatenate(force + [jnp.zeros((5, markers), jnp.float32)], axis=0)


def step_kernel(
    base_ref,
    shear_ref,
    edge_ref,
    edge_shear,
    sums_ref,
    mag_in_ref,
    mag_out_ref,
    cell_ref,
    weight_ref,
    segment_ref,
    note_below,
    note_above,
    next_hbm,
    eddy_ref,
    partial_ref,
    rising_ref,
    falling_ref,
    post,
    nexts,
    table,
    face_table,
    eddy,
    line,
    out_sems,
):
    depth, width = shear_ref.shape[1:3]
    lines = width + 2
    part = depth // 4
    eddy[...] = jnp.zeros_like(eddy)
    eddy[pl.ds(OWN - TOP - 1, lines), :] = jnp.maximum(
        sums_ref[pl.ds(0, lines), :] / (sums_ref[pl.ds(lines, lines), :] + eps_sum), 0.0
    )
    eddy_ref[...] = eddy[pl.ds(OWN - TOP, width), :]

    for side, (wanted, row, place) in enumerate(
        ((BEFORE, OWN - TOP - 1, FIRST - 1), (AFTER, OWN - TOP + width, FIRST + width))
    ):
        for z in range(depth):
            if z == 0:
                size = mag_out_ref[1, pl.ds(row, 1), :]
            elif z == depth - 1:
                size = mag_out_ref[6, pl.ds(row, 1), :]
            else:
                size = mag_in_ref[z - 1, pl.ds(row, 1), :]
            line[pl.ds(z, 1), :] = size
        rate = relax_rate(eddy[pl.ds(row, 1), :], line[...])
        changes = shear_changes([edge_shear[side, k] for k in range(5)], rate)
        for index, q in enumerate(wanted):
            out = edge_ref[side, index] + changes[q]
            for z in range(depth):
                post[q, z, pl.ds(place, 1), :] = out[z : z + 1]

    def collide(z, size_ref, at):
        for half in range(width // 16):
            rows = pl.ds(16 * half, 16)
            around = pl.ds(OWN - TOP + 16 * half, 16)
            rate = relax_rate(eddy[around, :], size_ref[at, around, :])
            changes = shear_changes([shear_ref[k, z, rows, :] for k in range(5)], rate)
            for q in range(19):
                value = base_ref[q, z, rows, :]
                if q:
                    value = value + changes[q]
                post[q, z, pl.ds(FIRST + 16 * half, 16), :] = value

    def inner(z, carry):
        collide(z, mag_in_ref, z - 1)
        return carry

    collide(0, mag_out_ref, 1)
    collide(depth - 1, mag_out_ref, 6)
    lax.fori_loop(1, depth - 1, inner, 0)

    def shifted(q, z, half):
        shift_x, shift_y, _ = VELOCITIES[q]
        piece = post[q, z, pl.ds(FIRST + 16 * half - shift_y, 16), :]
        if shift_x:
            piece = minus(piece) if shift_x > 0 else plus(piece)
        return piece.astype(jnp.bfloat16)

    def run(z, leave_out=()):
        for half in range(width // 16):
            flux = [0.0, 0.0, 0.0]
            for q in range(19):
                if q in leave_out:
                    continue
                moved = shifted(q, z - VELOCITIES[q][2], half)
                nexts[q, z, pl.ds(16 * half, 16), :] = moved
                if q:
                    add_flux(flux, q, moved.astype(jnp.float32))
            table_rows(table, pl.ds(pl.multiple_of(z * width + 16 * half, 16), 16), flux)

    def run_inner(z, carry):
        run(z)
        return carry

    for side, (wanted, z, out) in enumerate(
        ((RISING, depth - 1, rising_ref), (FALLING, 0, falling_ref))
    ):
        for half in range(width // 16):
            rows = pl.ds(16 * half, 16)
            flux = [0.0, 0.0, 0.0]
            for index, q in enumerate(wanted):
                moved = shifted(q, z, half)
                out[index, rows, :] = moved
                add_flux(flux, q, moved.astype(jnp.float32))
            table_rows(face_table.at[side], rows, flux)

    outs = []
    for index in range(4):
        start, stop = index * part, (index + 1) * part
        if index == 0:
            run(0, RISING)
            start += 1
        if index == 3:
            run(depth - 1, FALLING)
            stop -= 1
        lax.fori_loop(start, stop, run_inner, 0)
        place = pl.ds(index * part, part)
        outs.append(
            pltpu.make_async_copy(nexts.at[:, place], next_hbm.at[:, place], out_sems.at[index])
        )
        outs[-1].start()

    owners = partial_ref.shape[0]
    taps, markers = cell_ref.shape
    segments = owners * SEG_DEV
    segment_of = lax.broadcasted_iota(jnp.int32, (segments, markers), 0)
    totals = jnp.zeros((8, segments), jnp.float32)
    groups = [
        (table, 0, depth * width, cell_ref[...], weight_ref[...], segment_ref[...]),
    ]
    for side, (note, start) in enumerate(((note_above, 0), (note_below, (depth - 1) * width))):
        groups.append(
            (
                face_table.at[side],
                start,
                width,
                note[pl.ds(NOTE, taps), :].astype(jnp.int32),
                note[pl.ds(NOTE + taps, taps), :],
                note[pl.ds(NOTE + 2 * taps, 1), :].astype(jnp.int32),
            )
        )
    for rows_table, start, rows, cells, weights, segment in groups:
        totals = totals + lax.dot_general(
            marker_force(rows_table, start, rows, cells, weights),
            jnp.where(segment_of == segment, 1.0, 0.0),
            (((1,), (1,)), ((), ())),
            precision=lax.Precision.HIGHEST,
            preferred_element_type=jnp.float32,
        )
    owner_of = lax.broadcasted_iota(jnp.int32, (owners, segments), 0)
    at_segment = lax.broadcasted_iota(jnp.int32, (owners, segments), 1)
    mine = lax.shift_right_logical(at_segment, 3) == owner_of
    spot = lax.broadcasted_iota(jnp.int32, (segments, LANES), 0)
    at_lane = lax.broadcasted_iota(jnp.int32, (segments, LANES), 1)
    packed = jnp.zeros((owners, LANES), jnp.float32)
    for dim in range(3):
        spread = jnp.where(mine, totals[dim : dim + 1, :], 0.0)
        to_lane = lax.bitwise_and(spot, SEG_DEV - 1) + dim * SEG_DEV == at_lane
        packed = packed + jnp.dot(
            spread,
            jnp.where(to_lane, 1.0, 0.0),
            precision=lax.Precision.HIGHEST,
            preferred_element_type=jnp.float32,
        )
    partial_ref[:, 0, :] = packed
    for copy in outs:
        copy.wait()


def step(parts, sums, mag_in, mag_out, cells, weights, segments, notes, owners):
    _, depth, width, lanes = parts[0].shape
    face = full((5, width, lanes), jnp.bfloat16)
    return pl.pallas_call(
        step_kernel,
        out_shape=(
            full((19, depth, width, lanes), jnp.bfloat16),
            full((width, lanes), jnp.float32),
            full((owners, 1, lanes), jnp.float32),
            face,
            face,
        ),
        in_specs=in_vmem(12),
        out_specs=(pl.BlockSpec(memory_space=pl.ANY),) + tuple(in_vmem(4)),
        scratch_shapes=[
            pltpu.VMEM((19, depth, FIRST + width + 8, lanes), jnp.float32),
            pltpu.VMEM((19, depth, width, lanes), jnp.bfloat16),
            pltpu.VMEM((2, depth * width, 3 * lanes), jnp.bfloat16),
            pltpu.VMEM((2, 2, width, 3 * lanes), jnp.bfloat16),
            pltpu.VMEM((EXT, lanes), jnp.float32),
            pltpu.VMEM((depth, lanes), jnp.float32),
            pltpu.SemaphoreType.DMA((4,)),
        ],
        compiler_params=params(),
        cost_estimate=cost(5),
        name="step",
    )(*parts, sums, mag_in, mag_out, cells, weights, segments, *notes)


def arrive_kernel(next_in, rising_ref, falling_ref, next_hbm, sems):
    depth = next_hbm.shape[1]
    copies = []
    for source, wanted, z in ((rising_ref, RISING, 0), (falling_ref, FALLING, depth - 1)):
        for index, q in enumerate(wanted):
            copies.append(
                pltpu.make_async_copy(source.at[index], next_hbm.at[q, z], sems.at[len(copies)])
            )
            copies[-1].start()
    for copy in copies:
        copy.wait()


def arrive(populations_next, rising, falling):
    hbm = pl.BlockSpec(memory_space=pl.ANY)
    return pl.pallas_call(
        arrive_kernel,
        out_shape=full(populations_next.shape, jnp.bfloat16),
        in_specs=[hbm] + in_vmem(2),
        out_specs=hbm,
        input_output_aliases={0: 0},
        scratch_shapes=[pltpu.SemaphoreType.DMA((10,))],
        compiler_params=params(),
        cost_estimate=cost(0.5),
        name="arrive",
    )(populations_next, rising, falling)


def finish_kernel(arrived_ref, out_ref):
    total = jnp.sum(arrived_ref[:, 0, :], axis=0, keepdims=True)
    for dim in range(3):
        out_ref[pl.ds(dim, 1), :] = total[:, dim * SEG_DEV : (dim + 1) * SEG_DEV]


def finish(arrived):
    return pl.pallas_call(
        finish_kernel,
        out_shape=full((3, SEG_DEV), jnp.float32),
        in_specs=in_vmem(1),
        out_specs=in_vmem(1)[0],
        name="finish",
    )(arrived)


def span_sum(values):
    count = lax.axis_size("span")
    if count & (count - 1):
        return lax.psum(values, "span")
    distance = 1
    while distance < count:
        pairs = [(i, i ^ distance) for i in range(count)]
        values = values + lax.ppermute(values, "span", pairs)
        distance *= 2
    return values


def local(populations, cell_index, marker_weight, segment_id):
    owners = lax.axis_size("span") * lax.axis_size("cross")
    cells, weights, segments = cell_index.T, marker_weight.T, segment_id[None, :]
    vel, y_first, y_last, z_first, z_last = block_moments(populations)
    low, high = exchange(y_first, y_last, "cross")
    below, above = exchange(z_first, z_last, "span")
    note_first, note_last = edge_notes(low, high, cells, weights, segments)
    notes = exchange(note_first, note_last, "span")
    partial, mag_in = inner_sums(vel, low, high)
    before, after = exchange(*face_rows(populations, partial), "cross")
    sums, mag_out = outer_sums(vel, low, high, below, above, *notes, partial)
    parts = ready(populations, before, after, sums)
    sums = span_sum(sums)
    moved, eddy_coeff, packed, rising, falling = step(
        parts, sums, mag_in, mag_out, cells, weights, segments, notes, owners
    )
    arrived = lax.all_to_all(packed, ("span", "cross"), 0, 0)
    populations_next = arrive(moved, *exchange(falling, rising, "span"))
    return (populations_next, eddy_coeff, finish(arrived))


def solution(mesh):
    in_specs = (
        P(None, "span", "cross", None),
        P(("span", "cross"), None),
        P(("span", "cross"), None),
        P(("span", "cross")),
    )
    out_specs = (P(None, "span", "cross", None), P("cross", None), P(None, ("span", "cross")))
    return jax.shard_map(local, mesh=mesh, in_specs=in_specs, out_specs=out_specs, check_vma=False)
```

time: 68.4 us -> 60 us (0.88)
  waiting for transfers between devices: 16 us -> 8.59 us
  starting transfers between devices: 16.3 us -> 19.2 us
  blocking collectives: 11.8 us -> 9.53 us
  Pallas kernels: 21.5 us -> 19.9 us
    ppermute x4 -> x5, waiting for transfers between devices: 4.73 us -> 0.01 us  [exchange(): low = lax.ppermute(last, axis, forward)]
    ppermute x3, waiting for transfers between devices: 11.3 us -> 8.57 us  [span_sum(): values = values + lax.ppermute(values, 'span', pairs)]
    ppermute x4 -> x5, starting transfers between devices: 0.62 us -> 3.09 us  [exchange(): low = lax.ppermute(last, axis, forward)]
    all_to_all x1, blocking collectives: 11.8 us -> 9.53 us  [local(): arrived = lax.all_to_all(packed, ('span', 'cross'), 0, 0)]
    ppermute x4 -> x5, starting transfers between devices: 13.8 us -> 16 us  [exchange(): high = lax.ppermute(first, axis, backward)]
    ppermute x3, starting transfers between devices: 1.84 us -> 0.08 us  [span_sum(): values = values + lax.ppermute(values, 'span', pairs)]
    pallas_call x5 -> x7, Pallas kernels: 15.3 us -> 13.8 us  [the longest x1 6.96 us: step(): pl.pallas_call(step_kernel, out_shape=(full((19, depth, width, lanes), jn...]
  transfers between devices with their start and end apart: 11 -> 13, of which waited for: 4 -> 3; matrix products, arithmetic and copies ran while one was open for 0% -> 0% of each run, Pallas kernels for 17% -> 15%
where the time goes in v1:
time: 60 us; the launch traced here: 59.7 us
  Pallas kernels  19.9 us (33%)
  starting transfers between devices  19.2 us (32%)
  blocking collectives  9.53 us (16%)
  waiting for transfers between devices  8.59 us (14%)
  local copies, waits for them, and re-layouts  1.71 us (3%)
  between operations  0.81 us (1%)
    ppermute x5, starting transfers between devices, exchange(): high = lax.ppermute(first, axis, backward)  16 us
    all_to_all x1, blocking collectives, local(): arrived = lax.all_to_all(packed, ('span', 'cross'), 0, 0)  9.53 us
    ppermute x3, waiting for transfers between devices, span_sum(): values = values + lax.ppermute(values, 'span', pairs)  8.57 us
    pallas_call x1, Pallas kernels, step(): pl.pallas_call(step_kernel, out_shape=(full((19, depth, width, lanes), jn...  6.96 us
    pallas_call x1, Pallas kernels, inner_sums(): pl.pallas_call(inner_kernel, out_shape=(full((2, EXT, LANES), jnp.float32...  5.37 us
    ppermute x5, starting transfers between devices, exchange(): low = lax.ppermute(last, axis, forward)  3.09 us
    pallas_call x1, Pallas kernels, outer_sums(): pl.pallas_call(outer_kernel, out_shape=(full((-(-2 * (width + 2) // 8) *...  2.36 us
    pallas_call x1, Pallas kernels, ready(): pl.pallas_call(ready_kernel, out_shape=(full((19, depth, width, lanes), j...  2.06 us
  transfers between devices with their start and end apart: 13, of which 3 were waited for; matrix products, arithmetic and copies ran while one was open for 0% of the time, Pallas kernels for 15%

profile of v1, /device:TPU:0, one launch (start us, length us, event | category | flops | bytes accessed | tf_op | source)
XLA Modules:
  0.0 59.7 jit_solution(8423935200111822910)
XLA Ops:
  0.6 1.7 %copy-done = bf16[19,16,32,128]{3,2,1,0:T(8,128)(2,1)S(1)} copy-done((bf16[19,16,32,128]{3,2,1,0:T(8,128)(2,1)S(1)}, bf16[19,16,32,128]{3,2,1,0:T(8,128)(2,1)}, u32[]{:S(2)}) %copy-start) | copy-done | bytes 2490392
  2.3 0.7 %moments.1 = (f32[3,16,32,128]{3,2,1,0:T(8,128)S(1)}, bf16[12,16,128]{2,1,0:T(8,128)(2,1)S(1)}, bf16[12,16,128]{2,1,0:T(8,128)(2,1)S(1)}, bf16[9,32,128]{2,1,0:T(8,128)(2,1)S(1)}, bf16[9,32,128]{2,1,0:T(8,128)(2,1)S(1)}) custom-call(bf16[19,16,32,128]{3,2,1,0:T(8,128)(2,1)S(1)} %copy-done), custom_call_target="tpu_custom_call" | custom-call | bytes 3600000 | tf_op jit(solution)/shard_map/moments/pallas_call | solution.py:138
  3.1 0.5 collective-permute-start
  3.6 2.0 %collective-permute-start.1 = (bf16[12,16,128]{2,1,0:T(8,128)(2,1)S(1)}, bf16[12,16,128]{2,1,0:T(8,128)(2,1)S(1)}, u32[]{:S(2)}, u32[]{:S(2)}) collective-permute-start(bf16[12,16,128]{2,1,0:T(8,128)(2,1)S(1)} %get-tuple-element.27), channel_id=1, source_target_pairs={{1,0},{2,1},{3,2},{0,3},{5,4},{6,5},{7,6},{4,7},{9,8},{10,9},{11,1... | collective-permute-start | bytes 147464 | tf_op jit(solution)/shard_map/ppermute | solution.py:56
  5.6 2.2 %collective-permute-start.4 = (bf16[9,32,128]{2,1,0:T(8,128)(2,1)S(1)}, bf16[9,32,128]{2,1,0:T(8,128)(2,1)S(1)}, u32[]{:S(2)}, u32[]{:S(2)}) collective-permute-start(bf16[9,32,128]{2,1,0:T(8,128)(2,1)S(1)} %get-tuple-element.31), channel_id=1, source_target_pairs={{0,4},{4,8},{8,12},{12,16},{16,20},{20,24},{24,28},{28,0},{1,5},{5... | collective-permute-start | bytes 221192 | tf_op jit(solution)/shard_map/ppermute | solution.py:55
  7.8 3.0 %collective-permute-start.5 = (bf16[9,32,128]{2,1,0:T(8,128)(2,1)S(1)}, bf16[9,32,128]{2,1,0:T(8,128)(2,1)S(1)}, u32[]{:S(2)}, u32[]{:S(2)}) collective-permute-start(bf16[9,32,128]{2,1,0:T(8,128)(2,1)S(1)} %get-tuple-element.32), channel_id=1, source_target_pairs={{4,0},{8,4},{12,8},{16,12},{20,16},{24,20},{28,24},{0,28},{5,1},{9... | collective-permute-start | bytes 221192 | tf_op jit(solution)/shard_map/ppermute | solution.py:56
  10.9 0.0 collective-permute-done.low_ref
  10.9 0.0 collective-permute-done.1.high_ref
  10.9 0.1 collective-permute-start.6
  11.0 4.7 %collective-permute-start.7 = (f32[72,128]{1,0:T(8,128)S(1)}, f32[72,128]{1,0:T(8,128)S(1)}, u32[]{:S(2)}, u32[]{:S(2)}) collective-permute-start(f32[72,128]{1,0:T(8,128)S(1)} %get-tuple-element.34), channel_id=1, source_target_pairs={{4,0},{8,4},{12,8},{16,12},{20,16},{24,20},{28,24},{0,28},{5,1},{9... | collective-permute-start | bytes 110600 | tf_op jit(solution)/shard_map/ppermute | solution.py:56
  15.7 5.4 %inner_sums.1 = (f32[2,40,128]{2,1,0:T(8,128)S(1)}, f32[14,40,128]{2,1,0:T(8,128)S(1)}) custom-call(f32[3,16,32,128]{3,2,1,0:T(8,128)S(1)} %get-tuple-element.25.vel_ref, bf16[12,16,128]{2,1,0:T(8,128)(2,1)S(1)} %collective-permute-done.low_ref, bf16[12,16,128]{2,1,0:T(8,128)(2,1)S(1)} %collective-permute-done.1.high_ref), custom_call_target="tpu_custom_call" | custom-call | bytes 18000000 | tf_op jit(solution)/shard_map/inner_sums/pallas_call | solution.py:323
  21.1 0.0 collective-permute-done.4.below_ref
  21.1 0.0 collective-permute-done.5.above_ref
  21.1 2.4 %outer_sums.1 = (f32[72,128]{1,0:T(8,128)S(1)}, f32[8,40,128]{2,1,0:T(8,128)S(1)}) custom-call(f32[3,16,32,128]{3,2,1,0:T(8,128)S(1)} %get-tuple-element.25.vel_ref, bf16[12,16,128]{2,1,0:T(8,128)(2,1)S(1)} %collective-permute-done.low_ref, bf16[12,16,128]{2,1,0:T(8,128)(2,1)S(1)} %collective-permute-done.1.high_ref, ...), custom_call_target="tpu_custom_call" | custom-call | bytes 7200000 | tf_op jit(solution)/shard_map/outer_sums/pallas_call | solution.py:387
  23.5 0.1 collective-permute-start.8
  23.6 0.3 face_rows.1
  23.8 0.1 collective-permute-start.2
  23.9 1.7 %collective-permute-start.3 = (bf16[19,16,128]{2,1,0:T(8,128)(2,1)S(1)}, bf16[19,16,128]{2,1,0:T(8,128)(2,1)S(1)}, u32[]{:S(2)}, u32[]{:S(2)}) collective-permute-start(bf16[19,16,128]{2,1,0:T(8,128)(2,1)S(1)} %get-tuple-element.30), channel_id=1, source_target_pairs={{1,0},{2,1},{3,2},{0,3},{5,4},{6,5},{7,6},{4,7},{9,8},{10,9},{11,1... | collective-permute-start | bytes 233480 | tf_op jit(solution)/shard_map/ppermute | solution.py:56
  25.7 1.9 %collective-permute-done.8 = f32[72,128]{1,0:T(8,128)S(1)} collective-permute-done((f32[72,128]{1,0:T(8,128)S(1)}, f32[72,128]{1,0:T(8,128)S(1)}, u32[]{:S(2)}, u32[]{:S(2)}) %collective-permute-start.8) | collective-permute-done | bytes 36896 | tf_op jit(solution)/shard_map/ppermute | solution.py:850
  27.5 3.9 %collective-permute-done.9 = f32[72,128]{1,0:T(8,128)S(1)} collective-permute-done((f32[72,128]{1,0:T(8,128)S(1)}, f32[72,128]{1,0:T(8,128)S(1)}, u32[]{:S(2)}, u32[]{:S(2)}) %collective-permute-start.9) | collective-permute-done | bytes 36896 | tf_op jit(solution)/shard_map/ppermute | solution.py:850
  31.5 0.0 collective-permute-start.10
  31.5 0.0 collective-permute-done.3.after_ref
  31.5 2.1 %ready.1 = (f32[19,16,32,128]{3,2,1,0:T(8,128)S(1)}, f32[5,16,32,128]{3,2,1,0:T(8,128)S(1)}, f32[2,5,16,128]{3,2,1,0:T(8,128)S(1)}, f32[2,5,16,128]{3,2,1,0:T(8,128)S(1)}) custom-call(bf16[19,16,32,128]{3,2,1,0:T(8,128)(2,1)S(1)} %copy-done.1, bf16[19,16,128]{2,1,0:T(8,128)(2,1)S(1)} %collective-permute-done.2.before_ref, ...), custom_call_target="tpu_custom_call" | custom-call | bytes 9000000 | tf_op jit(solution)/shard_map/ready/pallas_call | solution.py:549
  33.6 2.8 %collective-permute-done.10 = f32[72,128]{1,0:T(8,128)S(1)} collective-permute-done((f32[72,128]{1,0:T(8,128)S(1)}, f32[72,128]{1,0:T(8,128)S(1)}, u32[]{:S(2)}, u32[]{:S(2)}) %collective-permute-start.10) | collective-permute-done | bytes 36896 | tf_op jit(solution)/shard_map/ppermute | solution.py:850
  36.4 7.0 %step.1 = (bf16[19,16,32,128]{3,2,1,0:T(8,128)(2,1)}, f32[32,128]{1,0:T(8,128)}, f32[32,1,128]{2,1,0:T(1,128)S(1)}, bf16[5,32,128]{2,1,0:T(8,128)(2,1)S(1)}, bf16[5,32,128]{2,1,0:T(8,128)(2,1)S(1)}) custom-call(f32[19,16,32,128]{3,2,1,0:T(8,128)S(1)} %get-tuple-element.36.base_ref, f32[5,16,32,128]{3,2,1,0:T(8,128)S(1)} %get-tuple-element.37.shear_ref, ...), custom_call_target="tpu_custom_call" | custom-call | bytes 18000000 | tf_op jit(solution)/shard_map/step/pallas_call | solution.py:773
  43.3 0.3 collective-permute-start.11
  43.6 4.5 %collective-permute-start.12 = (bf16[5,32,128]{2,1,0:T(8,128)(2,1)S(1)}, bf16[5,32,128]{2,1,0:T(8,128)(2,1)S(1)}, u32[]{:S(2)}, u32[]{:S(2)}) collective-permute-start(bf16[5,32,128]{2,1,0:T(8,128)(2,1)S(1)} %get-tuple-element.44), channel_id=1, source_target_pairs={{4,0},{8,4},{12,8},{16,12},{20,16},{24,20},{28,24},{0,28},{5,1},{9... | collective-permute-start | bytes 122888 | tf_op jit(solution)/shard_map/ppermute | solution.py:56
  48.1 9.5 %all_to_all.5.arrived_ref = f32[32,1,128]{2,1,0:T(1,128)} all-to-all(f32[32,1,128]{2,1,0:T(1,128)S(1)} %get-tuple-element.46), channel_id=1, replica_groups=mesh['span'=8,'cross'=4] {'span','cross'}, dimensions={0} | all-to-all | bytes 32768 | tf_op jit(solution)/shard_map/all_to_all | solution.py:871
  57.6 1.4 %finish.1 = f32[3,8]{1,0:T(4,128)} custom-call(f32[32,1,128]{2,1,0:T(1,128)} %all_to_all.5.arrived_ref), custom_call_target="tpu_custom_call" | custom-call | tf_op jit(solution)/shard_map/finish/pallas_call | solution.py:834
  59.0 0.0 collective-permute-done.11.rising_ref
  59.0 0.0 collective-permute-done.12.falling_ref
  59.0 0.7 %arrive.1 = bf16[19,16,32,128]{3,2,1,0:T(8,128)(2,1)} custom-call(bf16[19,16,32,128]{3,2,1,0:T(8,128)(2,1)} %get-tuple-element.42.next_in, bf16[5,32,128]{2,1,0:T(8,128)(2,1)S(1)} %collective-permute-done.11.rising_ref, bf16[5,32,128]{2,1,0:T(8,128)(2,1)S(1)} %collective-permute-done.12.falling_ref), custom_call_target="tpu_custom_call", output_to_operand_aliasing={{}: (0, {})} | custom-call | bytes 1800000 | tf_op jit(solution)/shard_map/arrive/pallas_call | solution.py:814
  (17 shorter events, 0.1 us)
Async XLA Ops:
  0.6 1.7 %copy-start = (bf16[19,16,32,128]{3,2,1,0:T(8,128)(2,1)S(1)}, bf16[19,16,32,128]{3,2,1,0:T(8,128)(2,1)}, u32[]{:S(2)}) copy-start(bf16[19,16,32,128]{3,2,1,0:T(8,128)(2,1)} %pops.5) | copy-start | bytes 7471108
  2.3 8.5 %copy-start.2 = (s32[128,8]{0,1:T(8,128)S(1)}, s32[128,8]{0,1:T(8,128)}, u32[]{:S(2)}) copy-start(s32[128,8]{0,1:T(8,128)} %param.5) | copy-start | bytes 12292
  2.3 8.5 %copy-start.3 = (f32[128,8]{0,1:T(8,128)S(1)}, f32[128,8]{0,1:T(8,128)}, u32[]{:S(2)}) copy-start(f32[128,8]{0,1:T(8,128)} %param.6) | copy-start | bytes 12292
  2.3 8.5 %copy-start.4 = (s32[128]{0:T(128)S(1)}, s32[128]{0:T(128)}, u32[]{:S(2)}) copy-start(s32[128]{0:T(128)} %param.7) | copy-start | bytes 1540
  2.3 21.2 %copy-start.1 = (bf16[19,16,32,128]{3,2,1,0:T(8,128)(2,1)S(1)}, bf16[19,16,32,128]{3,2,1,0:T(8,128)(2,1)}, u32[]{:S(2)}) copy-start(bf16[19,16,32,128]{3,2,1,0:T(8,128)(2,1)} %pops.5) | copy-start | bytes 7471108
  3.1 7.8 %collective-permute-start = (bf16[12,16,128]{2,1,0:T(8,128)(2,1)S(1)}, bf16[12,16,128]{2,1,0:T(8,128)(2,1)S(1)}, u32[]{:S(2)}, u32[]{:S(2)}) collective-permute-start(bf16[12,16,128]{2,1,0:T(8,128)(2,1)S(1)} %get-tuple-element.26), channel_id=1, source_target_pairs={{0,1},{1,2},{2,3},{3,0},{4,5},{5,6},{6,7},{7,4},{8,9},{9,10},{10,1... | collective-permute-start | bytes 147464 | tf_op jit(solution)/shard_map/ppermute | solution.py:55
  3.6 7.3 %collective-permute-start.1 = (bf16[12,16,128]{2,1,0:T(8,128)(2,1)S(1)}, bf16[12,16,128]{2,1,0:T(8,128)(2,1)S(1)}, u32[]{:S(2)}, u32[]{:S(2)}) collective-permute-start(bf16[12,16,128]{2,1,0:T(8,128)(2,1)S(1)} %get-tuple-element.27), channel_id=1, source_target_pairs={{1,0},{2,1},{3,2},{0,3},{5,4},{6,5},{7,6},{4,7},{9,8},{10,9},{11,1... | collective-permute-start | bytes 147464 | tf_op jit(solution)/shard_map/ppermute | solution.py:56
  5.6 15.5 %collective-permute-start.4 = (bf16[9,32,128]{2,1,0:T(8,128)(2,1)S(1)}, bf16[9,32,128]{2,1,0:T(8,128)(2,1)S(1)}, u32[]{:S(2)}, u32[]{:S(2)}) collective-permute-start(bf16[9,32,128]{2,1,0:T(8,128)(2,1)S(1)} %get-tuple-element.31), channel_id=1, source_target_pairs={{0,4},{4,8},{8,12},{12,16},{16,20},{20,24},{24,28},{28,0},{1,5},{5... | collective-permute-start | bytes 221192 | tf_op jit(solution)/shard_map/ppermute | solution.py:55
  7.8 13.3 %collective-permute-start.5 = (bf16[9,32,128]{2,1,0:T(8,128)(2,1)S(1)}, bf16[9,32,128]{2,1,0:T(8,128)(2,1)S(1)}, u32[]{:S(2)}, u32[]{:S(2)}) collective-permute-start(bf16[9,32,128]{2,1,0:T(8,128)(2,1)S(1)} %get-tuple-element.32), channel_id=1, source_target_pairs={{4,0},{8,4},{12,8},{16,12},{20,16},{24,20},{28,24},{0,28},{5,1},{9... | collective-permute-start | bytes 221192 | tf_op jit(solution)/shard_map/ppermute | solution.py:56
  10.9 10.2 %collective-permute-start.6 = (f32[72,128]{1,0:T(8,128)S(1)}, f32[72,128]{1,0:T(8,128)S(1)}, u32[]{:S(2)}, u32[]{:S(2)}) collective-permute-start(f32[72,128]{1,0:T(8,128)S(1)} %get-tuple-element.33), channel_id=1, source_target_pairs={{0,4},{4,8},{8,12},{12,16},{16,20},{20,24},{24,28},{28,0},{1,5},{5... | collective-permute-start | bytes 110600 | tf_op jit(solution)/shard_map/ppermute | solution.py:55
  11.0 10.1 %collective-permute-start.7 = (f32[72,128]{1,0:T(8,128)S(1)}, f32[72,128]{1,0:T(8,128)S(1)}, u32[]{:S(2)}, u32[]{:S(2)}) collective-permute-start(f32[72,128]{1,0:T(8,128)S(1)} %get-tuple-element.34), channel_id=1, source_target_pairs={{4,0},{8,4},{12,8},{16,12},{20,16},{24,20},{28,24},{0,28},{5,1},{9... | collective-permute-start | bytes 110600 | tf_op jit(solution)/shard_map/ppermute | solution.py:56
  23.5 4.0 %collective-permute-start.8 = (f32[72,128]{1,0:T(8,128)S(1)}, f32[72,128]{1,0:T(8,128)S(1)}, u32[]{:S(2)}, u32[]{:S(2)}) collective-permute-start(f32[72,128]{1,0:T(8,128)S(1)} %get-tuple-element.35.after_this), channel_id=1, source_target_pairs={{0,4},{4,0},{8,12},{12,8},{16,20},{20,16},{24,28},{28,24},{1,5},{5... | collective-permute-start | bytes 110600 | tf_op jit(solution)/shard_map/ppermute | solution.py:850
  23.8 7.7 %collective-permute-start.2 = (bf16[19,16,128]{2,1,0:T(8,128)(2,1)S(1)}, bf16[19,16,128]{2,1,0:T(8,128)(2,1)S(1)}, u32[]{:S(2)}, u32[]{:S(2)}) collective-permute-start(bf16[19,16,128]{2,1,0:T(8,128)(2,1)S(1)} %get-tuple-element.29), channel_id=1, source_target_pairs={{0,1},{1,2},{2,3},{3,0},{4,5},{5,6},{6,7},{7,4},{8,9},{9,10},{10,1... | collective-permute-start | bytes 233480 | tf_op jit(solution)/shard_map/ppermute | solution.py:55
  23.9 7.6 %collective-permute-start.3 = (bf16[19,16,128]{2,1,0:T(8,128)(2,1)S(1)}, bf16[19,16,128]{2,1,0:T(8,128)(2,1)S(1)}, u32[]{:S(2)}, u32[]{:S(2)}) collective-permute-start(bf16[19,16,128]{2,1,0:T(8,128)(2,1)S(1)} %get-tuple-element.30), channel_id=1, source_target_pairs={{1,0},{2,1},{3,2},{0,3},{5,4},{6,5},{7,6},{4,7},{9,8},{10,9},{11,1... | collective-permute-start | bytes 233480 | tf_op jit(solution)/shard_map/ppermute | solution.py:56
  27.5 4.0 %collective-permute-start.9 = (f32[72,128]{1,0:T(8,128)S(1)}, f32[72,128]{1,0:T(8,128)S(1)}, u32[]{:S(2)}, u32[]{:S(2)}) collective-permute-start(f32[72,128]{1,0:T(8,128)S(1)} %add.9), channel_id=1, source_target_pairs={{0,8},{4,12},{8,0},{12,4},{16,24},{20,28},{24,16},{28,20},{1,9},{5... | collective-permute-start | bytes 110600 | tf_op jit(solution)/shard_map/ppermute | solution.py:850
  31.5 4.9 %collective-permute-start.10 = (f32[72,128]{1,0:T(8,128)S(1)}, f32[72,128]{1,0:T(8,128)S(1)}, u32[]{:S(2)}, u32[]{:S(2)}) collective-permute-start(f32[72,128]{1,0:T(8,128)S(1)} %add.10), channel_id=1, source_target_pairs={{0,16},{4,20},{8,24},{12,28},{16,0},{20,4},{24,8},{28,12},{1,17},{... | collective-permute-start | bytes 110600 | tf_op jit(solution)/shard_map/ppermute | solution.py:850
  43.3 15.7 %collective-permute-start.11 = (bf16[5,32,128]{2,1,0:T(8,128)(2,1)S(1)}, bf16[5,32,128]{2,1,0:T(8,128)(2,1)S(1)}, u32[]{:S(2)}, u32[]{:S(2)}) collective-permute-start(bf16[5,32,128]{2,1,0:T(8,128)(2,1)S(1)} %get-tuple-element.43), channel_id=1, source_target_pairs={{0,4},{4,8},{8,12},{12,16},{16,20},{20,24},{24,28},{28,0},{1,5},{5... | collective-permute-start | bytes 122888 | tf_op jit(solution)/shard_map/ppermute | solution.py:55
  43.6 15.4 %collective-permute-start.12 = (bf16[5,32,128]{2,1,0:T(8,128)(2,1)S(1)}, bf16[5,32,128]{2,1,0:T(8,128)(2,1)S(1)}, u32[]{:S(2)}, u32[]{:S(2)}) collective-permute-start(bf16[5,32,128]{2,1,0:T(8,128)(2,1)S(1)} %get-tuple-element.44), channel_id=1, source_target_pairs={{4,0},{8,4},{12,8},{16,12},{20,16},{24,20},{28,24},{0,28},{5,1},{9... | collective-permute-start | bytes 122888 | tf_op jit(solution)/shard_map/ppermute | solution.py:56

commit v2 on v1

--- a/solution.py
+++ b/solution.py
@@ -43,18 +43,34 @@
 ]
 
 
-def neighbours(axis):
+def swap(first, second, axis):
     count = lax.axis_size(axis)
-    forward = [(i, (i + 1) % count) for i in range(count)]
-    backward = [(target, source) for source, target in forward]
-    return forward, backward
-
-
-def exchange(first, last, axis):
-    forward, backward = neighbours(axis)
-    low = lax.ppermute(last, axis, forward)
-    high = lax.ppermute(first, axis, backward)
-    return low, high
+    near = [(i, i ^ 1) for i in range(count)]
+    other = [(i, (i + 1 if i % 2 else i - 1) % count) for i in range(count)]
+    return lax.ppermute(first, axis, near), lax.ppermute(second, axis, other)
+
+
+def is_odd(axis):
+    return lax.rem(lax.axis_index(axis), 2) == 1
+
+
+def send_pair(axis, upwards, downwards, first, second):
+    odd = is_odd(axis)
+
+    @pl.when(odd)
+    def _():
+        first[...] = downwards
+        second[...] = upwards
+
+    @pl.when(jnp.logical_not(odd))
+    def _():
+        first[...] = upwards
+        second[...] = downwards
+
+
+def below_above(axis, first, second):
+    odd = is_odd(axis)
+    return jnp.where(odd, first, second), jnp.where(odd, second, first)
 
 
 def full(shape, dtype):
@@ -79,6 +95,17 @@
 
 def minus(array):
     return pltpu.roll(array, 1, 1)
+
+
+STEP = 2.0**-15
+
+
+def encode(value):
+    return jnp.round(value * (1.0 / STEP)).astype(jnp.int32).astype(jnp.int16)
+
+
+def decode(coded):
+    return coded.astype(jnp.int32).astype(jnp.float32) * STEP
 
 
 def split(value):
@@ -86,11 +113,7 @@
     return high, (value - high.astype(jnp.float32)).astype(jnp.bfloat16)
 
 
-def join(high, low):
-    return high.astype(jnp.float32) + low.astype(jnp.float32)
-
-
-def moments_kernel(pops, vel_ref, y_first, y_last, z_first, z_last, rows):
+def moments_kernel(pops, vel_ref, first, second, rows):
     depth, width = pops.shape[1:3]
 
     def plane(z, carry):
@@ -118,28 +141,17 @@
         return carry
 
     lax.fori_loop(0, depth, plane, 0)
-    for side, out in enumerate((y_first, y_last)):
-        for dim in range(3):
-            line = [rows[side, dim * HALO + k] for k in range(HALO)]
-            out[4 * dim], out[4 * dim + 1] = split(line[0])
-            for k in range(1, HALO):
-                out[4 * dim + 1 + k] = (line[k] - line[k - 1]).astype(jnp.bfloat16)
-    for near, far, out in ((0, 1, z_first), (depth - 1, depth - 2, z_last)):
-        for dim in range(3):
-            layer = vel_ref[dim, near]
-            out[3 * dim], out[3 * dim + 1] = split(layer)
-            out[3 * dim + 2] = (vel_ref[dim, far] - layer).astype(jnp.bfloat16)
+    send_pair("cross", encode(rows[1]), encode(rows[0]), first, second)
 
 
 def block_moments(populations):
     _, depth, width, lanes = populations.shape
-    y_edge = full((12, depth, lanes), jnp.bfloat16)
-    z_edge = full((9, width, lanes), jnp.bfloat16)
+    edge = full((3 * HALO, depth, lanes), jnp.int16)
     return pl.pallas_call(
         moments_kernel,
-        out_shape=(full((3, depth, width, lanes), jnp.float32), y_edge, y_edge, z_edge, z_edge),
+        out_shape=(full((3, depth, width, lanes), jnp.float32), edge, edge),
         in_specs=in_vmem(1),
-        out_specs=tuple(in_vmem(5)),
+        out_specs=tuple(in_vmem(3)),
         scratch_shapes=[pltpu.VMEM((2, 3 * HALO, depth, lanes), jnp.float32)],
         compiler_params=params(),
         cost_estimate=cost(1),
@@ -147,13 +159,8 @@
     )(populations)
 
 
-def decode_rows(message, rows, side):
-    for dim in range(3):
-        line = join(message[4 * dim], message[4 * dim + 1])
-        rows[side, dim * HALO] = line
-        for k in range(1, HALO):
-            line = line + message[4 * dim + 1 + k].astype(jnp.float32)
-            rows[side, dim * HALO + k] = line
+def decode_rows(first, second, rows):
+    rows[0], rows[1] = below_above("cross", decode(first[...]), decode(second[...]))
 
 
 def place_plane(ext, p, vel_ref, rows, z):
@@ -166,40 +173,65 @@
             ext[dim, p, pl.ds(OWN + width + k, 1), :] = rows[1, dim * HALO + k, line, :]
 
 
-NOTE = 48
-NOTE_ROWS = 72
-
-
-def edges_kernel(low_ref, high_ref, cell_ref, weight_ref, segment_ref, first, last, rows):
-    depth = low_ref.shape[1]
-    decode_rows(low_ref, rows, 0)
-    decode_rows(high_ref, rows, 1)
+TALL = 40
+
+
+def edges_kernel(
+    vel_ref,
+    low_ref,
+    high_ref,
+    cell_ref,
+    weight_ref,
+    segment_ref,
+    first,
+    second,
+    rows,
+    planes,
+    note,
+    coded,
+):
+    depth, width = vel_ref.shape[1:3]
     taps = cell_ref.shape[0]
-    for planes, out in (((0, 1), first), ((depth - 1, depth - 2), last)):
-        out[...] = jnp.zeros_like(out)
+    decode_rows(low_ref, high_ref, rows)
+    fixed = weight_ref[...] * 2.0**16
+    coarse = jnp.round(fixed)
+    note[...] = jnp.zeros_like(note)
+    note[pl.ds(0, taps), :] = cell_ref[...].astype(jnp.float32) - 2.0**15
+    note[pl.ds(taps, taps), :] = coarse
+    note[pl.ds(2 * taps, taps), :] = jnp.round((fixed - coarse) * 2.0**15)
+    note[pl.ds(3 * taps, 1), :] = segment_ref[...].astype(jnp.float32)
+    for side, pair in enumerate(((0, 1), (depth - 1, depth - 2))):
+        planes[...] = jnp.zeros_like(planes)
         for dim in range(3):
-            for index, z in enumerate(planes):
-                for side in range(2):
-                    for k in range(HALO):
-                        row = 16 * dim + 8 * index + HALO * side + k
-                        out[pl.ds(row, 1), :] = rows[side, dim * HALO + k, pl.ds(z, 1), :]
-        out[pl.ds(NOTE, taps), :] = cell_ref[...].astype(jnp.float32)
-        out[pl.ds(NOTE + taps, taps), :] = weight_ref[...]
-        out[pl.ds(NOTE + 2 * taps, 1), :] = segment_ref[...].astype(jnp.float32)
-
-
-def edge_notes(low, high, cells, weights, segments):
-    note = full((NOTE_ROWS, LANES), jnp.float32)
+            for index, z in enumerate(pair):
+                slot = 2 * dim + index
+                planes[slot, pl.ds(HALO, width), :] = vel_ref[dim, z]
+                for k in range(HALO):
+                    line = pl.ds(z, 1)
+                    planes[slot, pl.ds(HALO - 1 - k, 1), :] = rows[0, dim * HALO + k, line, :]
+                    planes[slot, pl.ds(HALO + width + k, 1), :] = rows[1, dim * HALO + k, line, :]
+        coded[side, pl.ds(0, 6)] = encode(planes[...])
+        coded[side, 6] = note[...].astype(jnp.int32).astype(jnp.int16)
+    send_pair("span", coded[1], coded[0], first, second)
+
+
+def edge_planes(vel, low, high, cells, weights, segments):
+    pair = full((7, TALL, LANES), jnp.int16)
     return pl.pallas_call(
         edges_kernel,
-        out_shape=(note, note),
-        in_specs=in_vmem(5),
+        out_shape=(pair, pair),
+        in_specs=in_vmem(6),
         out_specs=tuple(in_vmem(2)),
-        scratch_shapes=[pltpu.VMEM((2, 3 * HALO, low.shape[1], LANES), jnp.float32)],
+        scratch_shapes=[
+            pltpu.VMEM((2, 3 * HALO, vel.shape[1], LANES), jnp.float32),
+            pltpu.VMEM((6, TALL, LANES), jnp.float32),
+            pltpu.VMEM((TALL, LANES), jnp.float32),
+            pltpu.VMEM((2, 7, TALL, LANES), jnp.int16),
+        ],
         compiler_params=params(),
         cost_estimate=cost(0.2),
         name="edges",
-    )(low, high, cells, weights, segments)
+    )(vel, low, high, cells, weights, segments)
 
 
 def strain_parts(ref, p, row):
@@ -292,8 +324,7 @@
 
 def inner_kernel(vel_ref, low_ref, high_ref, acc_ref, mag_ref, ext, hat, prods, zsum, rows):
     depth = vel_ref.shape[1]
-    decode_rows(low_ref, rows, 0)
-    decode_rows(high_ref, rows, 1)
+    decode_rows(low_ref, high_ref, rows)
 
     def assemble(p, carry):
         place_plane(ext, p, vel_ref, rows, p)
@@ -339,10 +370,8 @@
     vel_ref,
     low_ref,
     high_ref,
-    below_ref,
-    above_ref,
-    note_below,
-    note_above,
+    first_ref,
+    second_ref,
     partial_ref,
     sums_ref,
     mag_ref,
@@ -354,23 +383,19 @@
     acc,
 ):
     depth, width = vel_ref.shape[1:3]
-    decode_rows(low_ref, rows, 0)
-    decode_rows(high_ref, rows, 1)
+    decode_rows(low_ref, high_ref, rows)
     acc[...] = partial_ref[...]
-    for side, (message, note, places, start) in enumerate(
-        ((below_ref, note_below, (1, 0), 0), (above_ref, note_above, (4, 5), depth - 4))
+    below, above = below_above(
+        "span", decode(first_ref[pl.ds(0, 6)]), decode(second_ref[pl.ds(0, 6)])
+    )
+    for side, (message, places, start) in enumerate(
+        ((below, (1, 0), 0), (above, (4, 5), depth - 4))
     ):
         for index in range(4):
             place_plane(ext, index + (2 if side == 0 else 0), vel_ref, rows, start + index)
         for dim in range(3):
-            near = join(message[3 * dim], message[3 * dim + 1])
-            far = near + message[3 * dim + 2].astype(jnp.float32)
-            for index, (p, layer) in enumerate(zip(places, (near, far))):
-                ext[dim, p, pl.ds(OWN, width), :] = layer
-                row = 16 * dim + 8 * index
-                for k in range(HALO):
-                    ext[dim, p, pl.ds(OWN - 1 - k, 1), :] = note[pl.ds(row + k, 1), :]
-                    ext[dim, p, pl.ds(OWN + width + k, 1), :] = note[pl.ds(row + HALO + k, 1), :]
+            for index, p in enumerate(places):
+                ext[dim, p, pl.ds(OWN - HALO, TALL), :] = message[2 * dim + index]
 
         def store_mag(p, row, size):
             mag_ref[4 * side + p - 1, pl.ds(row - TOP, 8), :] = size
@@ -382,7 +407,7 @@
         sums_ref[pl.ds(index * lines, lines), :] = acc[index, pl.ds(OWN - TOP - 1, lines), :]
 
 
-def outer_sums(vel, low, high, below, above, note_below, note_above, partial):
+def outer_sums(vel, low, high, below, above, partial):
     depth, width = vel.shape[1:3]
     return pl.pallas_call(
         outer_kernel,
@@ -390,16 +415,16 @@
             full((-(-2 * (width + 2) // 8) * 8, LANES), jnp.float32),
             full((8, EXT, LANES), jnp.float32),
         ),
-        in_specs=in_vmem(8),
+        in_specs=in_vmem(6),
         out_specs=tuple(in_vmem(2)),
         scratch_shapes=model_scratch(6, depth) + [pltpu.VMEM((2, EXT, LANES), jnp.float32)],
         compiler_params=params(),
         cost_estimate=cost(2),
         name="outer_sums",
-    )(vel, low, high, below, above, note_below, note_above, partial)
-
-
-def rows_kernel(pops, after_this, first_ref, last_ref, rows):
+    )(vel, low, high, below, above, partial)
+
+
+def rows_kernel(pops, after_this, first, second, rows):
     depth, width = pops.shape[1:3]
 
     def plane(z, carry):
@@ -411,8 +436,9 @@
         return carry
 
     lax.fori_loop(0, depth, plane, 0)
-    first_ref[...] = rows[0].astype(jnp.bfloat16)
-    last_ref[...] = rows[1].astype(jnp.bfloat16)
+    send_pair(
+        "cross", rows[1].astype(jnp.bfloat16), rows[0].astype(jnp.bfloat16), first, second
+    )
 
 
 def face_rows(populations, after_this):
@@ -522,10 +548,14 @@
 FIRST = 8
 
 
-def ready_kernel(pops, before_ref, after_ref, after_this, base_ref, shear_ref, edge_ref, edge_shear):
+def ready_kernel(pops, first, second, after_this, base_ref, shear_ref, edge_ref, edge_shear):
     depth, width = pops.shape[1:3]
-    for side, (source, wanted) in enumerate(((before_ref, BEFORE), (after_ref, AFTER))):
-        base, shear = relax_parts([source[q].astype(jnp.float32) for q in range(19)])
+    rows = [
+        below_above("cross", first[q].astype(jnp.float32), second[q].astype(jnp.float32))
+        for q in range(19)
+    ]
+    for side, wanted in enumerate((BEFORE, AFTER)):
+        base, shear = relax_parts([pair[side] for pair in rows])
         for index, q in enumerate(wanted):
             edge_ref[side, index] = base[q]
         for k in range(5):
@@ -580,20 +610,25 @@
     taps, markers = cells.shape
     row_of = lax.broadcasted_iota(jnp.int32, (rows, markers), 0) + start
     lane_of = lax.broadcasted_iota(jnp.int32, (LANES, markers), 0)
+    row, lane = lax.shift_right_logical(cells, 7), lax.bitwise_and(cells, LANES - 1)
+    pick = jnp.concatenate(
+        [
+            jnp.where(row_of == row[tap : tap + 1, :], 1.0, 0.0).astype(jnp.bfloat16)
+            for tap in range(taps)
+        ],
+        axis=1,
+    )
     contract = (((0,), (0,)), ((), ()))
-    force = [jnp.zeros((1, markers), jnp.float32) for _ in range(3)]
+    picked = lax.dot_general(
+        table[0], pick, contract, preferred_element_type=jnp.float32
+    ) + lax.dot_general(table[1], pick, contract, preferred_element_type=jnp.float32)
+    force = [0.0, 0.0, 0.0]
     for tap in range(taps):
-        cell = cells[tap : tap + 1, :]
-        row, lane = lax.shift_right_logical(cell, 7), lax.bitwise_and(cell, LANES - 1)
-        pick = jnp.where(row_of == row, 1.0, 0.0).astype(jnp.bfloat16)
-        picked = lax.dot_general(
-            table[0], pick, contract, preferred_element_type=jnp.float32
-        ) + lax.dot_general(table[1], pick, contract, preferred_element_type=jnp.float32)
-        weight = jnp.where(lane_of == lane, -weights[tap : tap + 1, :], 0.0)
+        weight = jnp.where(lane_of == lane[tap : tap + 1, :], -weights[tap : tap + 1, :], 0.0)
+        at = slice(tap * markers, (tap + 1) * markers)
         for dim in range(3):
-            lanes = picked[dim * LANES : (dim + 1) * LANES, :]
-            force[dim] = force[dim] + jnp.sum(lanes * weight, axis=0, keepdims=True)
-    return jnp.concatenate(force + [jnp.zeros((5, markers), jnp.float32)], axis=0)
+            force[dim] = force[dim] + picked[dim * LANES : (dim + 1) * LANES, at] * weight
+    return [jnp.sum(part, axis=0, keepdims=True) for part in force]
 
 
 def step_kernel(
@@ -607,17 +642,18 @@
     cell_ref,
     weight_ref,
     segment_ref,
-    note_below,
-    note_above,
+    note_first,
+    note_second,
     next_hbm,
     eddy_ref,
     partial_ref,
-    rising_ref,
-    falling_ref,
+    first_ref,
+    second_ref,
     post,
     nexts,
     table,
     face_table,
+    faces,
     eddy,
     line,
     out_sems,
@@ -692,17 +728,16 @@
         run(z)
         return carry
 
-    for side, (wanted, z, out) in enumerate(
-        ((RISING, depth - 1, rising_ref), (FALLING, 0, falling_ref))
-    ):
+    for side, (wanted, z) in enumerate(((RISING, depth - 1), (FALLING, 0))):
         for half in range(width // 16):
             rows = pl.ds(16 * half, 16)
             flux = [0.0, 0.0, 0.0]
             for index, q in enumerate(wanted):
                 moved = shifted(q, z, half)
-                out[index, rows, :] = moved
+                faces[side, index, rows, :] = moved
                 add_flux(flux, q, moved.astype(jnp.float32))
             table_rows(face_table.at[side], rows, flux)
+    send_pair("span", faces[0], faces[1], first_ref, second_ref)
 
     outs = []
     for index in range(4):
@@ -722,47 +757,44 @@
 
     owners = partial_ref.shape[0]
     taps, markers = cell_ref.shape
-    segments = owners * SEG_DEV
-    segment_of = lax.broadcasted_iota(jnp.int32, (segments, markers), 0)
-    totals = jnp.zeros((8, segments), jnp.float32)
+    owner_of = lax.broadcasted_iota(jnp.int32, (owners, markers), 0)
+    place_of = lax.broadcasted_iota(jnp.int32, (SEG_DEV, markers), 0)
+    totals = [jnp.zeros((owners, SEG_DEV), jnp.float32) for _ in range(3)]
     groups = [
         (table, 0, depth * width, cell_ref[...], weight_ref[...], segment_ref[...]),
     ]
+    note_below, note_above = below_above(
+        "span", note_first[6].astype(jnp.int32), note_second[6].astype(jnp.int32)
+    )
     for side, (note, start) in enumerate(((note_above, 0), (note_below, (depth - 1) * width))):
         groups.append(
             (
                 face_table.at[side],
                 start,
                 width,
-                note[pl.ds(NOTE, taps), :].astype(jnp.int32),
-                note[pl.ds(NOTE + taps, taps), :],
-                note[pl.ds(NOTE + 2 * taps, 1), :].astype(jnp.int32),
+                note[:taps] + 2**15,
+                note[taps : 2 * taps].astype(jnp.float32) * 2.0**-16
+                + note[2 * taps : 3 * taps].astype(jnp.float32) * 2.0**-31,
+                note[3 * taps : 3 * taps + 1],
             )
         )
     for rows_table, start, rows, cells, weights, segment in groups:
-        totals = totals + lax.dot_general(
-            marker_force(rows_table, start, rows, cells, weights),
-            jnp.where(segment_of == segment, 1.0, 0.0),
-            (((1,), (1,)), ((), ())),
-            precision=lax.Precision.HIGHEST,
-            preferred_element_type=jnp.float32,
-        )
-    owner_of = lax.broadcasted_iota(jnp.int32, (owners, segments), 0)
-    at_segment = lax.broadcasted_iota(jnp.int32, (owners, segments), 1)
-    mine = lax.shift_right_logical(at_segment, 3) == owner_of
-    spot = lax.broadcasted_iota(jnp.int32, (segments, LANES), 0)
-    at_lane = lax.broadcasted_iota(jnp.int32, (segments, LANES), 1)
-    packed = jnp.zeros((owners, LANES), jnp.float32)
+        owner = jnp.where(owner_of == lax.shift_right_logical(segment, 3), 1.0, 0.0)
+        owner = owner.astype(jnp.bfloat16)
+        place = place_of == lax.bitwise_and(segment, SEG_DEV - 1)
+        for dim, force in enumerate(marker_force(rows_table, start, rows, cells, weights)):
+            rest = jnp.where(place, force, 0.0)
+            for _ in range(3):
+                coarse, _ = split(rest)
+                rest = rest - coarse.astype(jnp.float32)
+                totals[dim] = totals[dim] + lax.dot_general(
+                    owner,
+                    coarse,
+                    (((1,), (1,)), ((), ())),
+                    preferred_element_type=jnp.float32,
+                )
     for dim in range(3):
-        spread = jnp.where(mine, totals[dim : dim + 1, :], 0.0)
-        to_lane = lax.bitwise_and(spot, SEG_DEV - 1) + dim * SEG_DEV == at_lane
-        packed = packed + jnp.dot(
-            spread,
-            jnp.where(to_lane, 1.0, 0.0),
-            precision=lax.Precision.HIGHEST,
-            preferred_element_type=jnp.float32,
-        )
-    partial_ref[:, 0, :] = packed
+        partial_ref[:, dim, :] = totals[dim]
     for copy in outs:
         copy.wait()
 
@@ -775,7 +807,7 @@
         out_shape=(
             full((19, depth, width, lanes), jnp.bfloat16),
             full((width, lanes), jnp.float32),
-            full((owners, 1, lanes), jnp.float32),
+            full((owners, 3, SEG_DEV), jnp.float32),
             face,
             face,
         ),
@@ -786,6 +818,7 @@
             pltpu.VMEM((19, depth, width, lanes), jnp.bfloat16),
             pltpu.VMEM((2, depth * width, 3 * lanes), jnp.bfloat16),
             pltpu.VMEM((2, 2, width, 3 * lanes), jnp.bfloat16),
+            pltpu.VMEM((2, 5, width, lanes), jnp.bfloat16),
             pltpu.VMEM((EXT, lanes), jnp.float32),
             pltpu.VMEM((depth, lanes), jnp.float32),
             pltpu.SemaphoreType.DMA((4,)),
@@ -796,20 +829,31 @@
     )(*parts, sums, mag_in, mag_out, cells, weights, segments, *notes)
 
 
-def arrive_kernel(next_in, rising_ref, falling_ref, next_hbm, sems):
+def arrive_kernel(next_in, first, second, next_hbm, sems):
     depth = next_hbm.shape[1]
-    copies = []
-    for source, wanted, z in ((rising_ref, RISING, 0), (falling_ref, FALLING, depth - 1)):
-        for index, q in enumerate(wanted):
-            copies.append(
-                pltpu.make_async_copy(source.at[index], next_hbm.at[q, z], sems.at[len(copies)])
-            )
-            copies[-1].start()
-    for copy in copies:
-        copy.wait()
-
-
-def arrive(populations_next, rising, falling):
+    odd = is_odd("span")
+
+    def place(below, above):
+        copies = []
+        for source, wanted, z in ((below, RISING, 0), (above, FALLING, depth - 1)):
+            for index, q in enumerate(wanted):
+                copies.append(
+                    pltpu.make_async_copy(source.at[index], next_hbm.at[q, z], sems.at[len(copies)])
+                )
+                copies[-1].start()
+        for copy in copies:
+            copy.wait()
+
+    @pl.when(odd)
+    def _():
+        place(first, second)
+
+    @pl.when(jnp.logical_not(odd))
+    def _():
+        place(second, first)
+
+
+def arrive(populations_next, first, second):
     hbm = pl.BlockSpec(memory_space=pl.ANY)
     return pl.pallas_call(
         arrive_kernel,
@@ -821,56 +865,34 @@
         compiler_params=params(),
         cost_estimate=cost(0.5),
         name="arrive",
-    )(populations_next, rising, falling)
-
-
-def finish_kernel(arrived_ref, out_ref):
-    total = jnp.sum(arrived_ref[:, 0, :], axis=0, keepdims=True)
-    for dim in range(3):
-        out_ref[pl.ds(dim, 1), :] = total[:, dim * SEG_DEV : (dim + 1) * SEG_DEV]
-
-
-def finish(arrived):
-    return pl.pallas_call(
-        finish_kernel,
-        out_shape=full((3, SEG_DEV), jnp.float32),
-        in_specs=in_vmem(1),
-        out_specs=in_vmem(1)[0],
-        name="finish",
-    )(arrived)
-
-
-def span_sum(values):
-    count = lax.axis_size("span")
-    if count & (count - 1):
-        return lax.psum(values, "span")
-    distance = 1
-    while distance < count:
-        pairs = [(i, i ^ distance) for i in range(count)]
-        values = values + lax.ppermute(values, "span", pairs)
-        distance *= 2
-    return values
+    )(populations_next, first, second)
 
 
 def local(populations, cell_index, marker_weight, segment_id):
     owners = lax.axis_size("span") * lax.axis_size("cross")
     cells, weights, segments = cell_index.T, marker_weight.T, segment_id[None, :]
-    vel, y_first, y_last, z_first, z_last = block_moments(populations)
-    low, high = exchange(y_first, y_last, "cross")
-    below, above = exchange(z_first, z_last, "span")
-    note_first, note_last = edge_notes(low, high, cells, weights, segments)
-    notes = exchange(note_first, note_last, "span")
-    partial, mag_in = inner_sums(vel, low, high)
-    before, after = exchange(*face_rows(populations, partial), "cross")
-    sums, mag_out = outer_sums(vel, low, high, below, above, *notes, partial)
-    parts = ready(populations, before, after, sums)
-    sums = span_sum(sums)
-    moved, eddy_coeff, packed, rising, falling = step(
-        parts, sums, mag_in, mag_out, cells, weights, segments, notes, owners
+    vel, *lines = block_moments(populations)
+    lines = swap(*lines, "cross")
+    planes = swap(*edge_planes(vel, *lines, cells, weights, segments), "span")
+    partial, mag_in = inner_sums(vel, *lines)
+    faces = swap(*face_rows(populations, partial), "cross")
+    sums, mag_out = outer_sums(vel, *lines, *planes, partial)
+    parts = ready(populations, *faces, sums)
+    count = lax.axis_size("span")
+    if count & (count - 1):
+        sums = lax.psum(sums, "span")
+    else:
+        distance = 1
+        while distance < count:
+            pairs = [(i, i ^ distance) for i in range(count)]
+            sums = sums + lax.ppermute(sums, "span", pairs)
+            distance *= 2
+    moved, eddy_coeff, packed, *leaving = step(
+        parts, sums, mag_in, mag_out, cells, weights, segments, planes, owners
     )
     arrived = lax.all_to_all(packed, ("span", "cross"), 0, 0)
-    populations_next = arrive(moved, *exchange(falling, rising, "span"))
-    return (populations_next, eddy_coeff, finish(arrived))
+    populations_next = arrive(moved, *swap(*leaving, "span"))
+    return (populations_next, eddy_coeff, jnp.sum(arrived, axis=0))
 
 
 def solution(mesh):

time: 60 us -> 54.6 us (0.910)
  starting transfers between devices: 19.2 us -> 12.3 us
  Pallas kernels: 19.9 us -> 17.4 us
  blocking collectives: 9.53 us -> 11.4 us
  waiting for transfers between devices: 8.59 us -> 10.3 us
  other arithmetic: 0.02 us -> 0.64 us
    ppermute x13 -> x11, starting transfers between devices: 19.2 us -> 12.3 us  [the longest x8 12 us: swap(): return (lax.ppermute(first, axis, near), lax.ppermute(second, axis, other))]
    all_to_all x1, blocking collectives: 9.53 us -> 11.4 us  [local(): arrived = lax.all_to_all(packed, ('span', 'cross'), 0, 0)]
    ppermute x13 -> x11, waiting for transfers between devices: 8.59 us -> 10.3 us  [the longest x3 8.5 us: local(): sums = sums + lax.ppermute(sums, 'span', pairs)]
    pallas_call x2 -> x1, Pallas kernels: 1.43 us -> 0.13 us  [edge_planes(): pl.pallas_call(edges_kernel, out_shape=(pair, pair), in_specs=in_vmem(6),...]
    pallas_call x1, Pallas kernels: 6.96 us -> 5.73 us  [step(): pl.pallas_call(step_kernel, out_shape=(full((19, depth, width, lanes), jn...]
    reduce_sum x0 -> x1, other arithmetic: none -> 0.62 us  [local(): return (populations_next, eddy_coeff, jnp.sum(arrived, axis=0))]
  transfers between devices with their start and end apart: 13 -> 11, of which waited for: 3 -> 4; matrix products, arithmetic and copies ran while one was open for 0% -> 1% of each run, Pallas kernels for 15% -> 14%
where the time goes in v2:
time: 54.6 us; the launch traced here: 54.4 us
  Pallas kernels  17.4 us (32%)
  starting transfers between devices  12.3 us (23%)
  blocking collectives  11.4 us (21%)
  waiting for transfers between devices  10.3 us (19%)
  local copies, waits for them, and re-layouts  1.71 us (3%)
  between operations  0.75 us (1%)
  other arithmetic  0.64 us (1%)
    ppermute x8, starting transfers between devices, swap(): return (lax.ppermute(first, axis, near), lax.ppermute(second, axis, other))  12 us
    all_to_all x1, blocking collectives, local(): arrived = lax.all_to_all(packed, ('span', 'cross'), 0, 0)  11.4 us
    ppermute x3, waiting for transfers between devices, local(): sums = sums + lax.ppermute(sums, 'span', pairs)  8.5 us
    pallas_call x1, Pallas kernels, step(): pl.pallas_call(step_kernel, out_shape=(full((19, depth, width, lanes), jn...  5.73 us
    pallas_call x1, Pallas kernels, inner_sums(): pl.pallas_call(inner_kernel, out_shape=(full((2, EXT, LANES), jnp.float32...  5.38 us
    pallas_call x1, Pallas kernels, outer_sums(): pl.pallas_call(outer_kernel, out_shape=(full((-(-2 * (width + 2) // 8) *...  2.36 us
    pallas_call x1, Pallas kernels, ready(): pl.pallas_call(ready_kernel, out_shape=(full((19, depth, width, lanes), j...  2.06 us
    ppermute x8, waiting for transfers between devices, swap(): return (lax.ppermute(first, axis, near), lax.ppermute(second, axis, other))  1.77 us
  transfers between devices with their start and end apart: 11, of which 4 were waited for; matrix products, arithmetic and copies ran while one was open for 1% of the time, Pallas kernels for 14%

profile of v2, /device:TPU:0, one launch (start us, length us, event | category | flops | bytes accessed | tf_op | source)
XLA Modules:
  0.0 54.4 jit_solution(1062072632124570788)
XLA Ops:
  0.6 1.7 %copy-done = bf16[19,16,32,128]{3,2,1,0:T(8,128)(2,1)S(1)} copy-done((bf16[19,16,32,128]{3,2,1,0:T(8,128)(2,1)S(1)}, bf16[19,16,32,128]{3,2,1,0:T(8,128)(2,1)}, u32[]{:S(2)}) %copy-start) | copy-done | bytes 2490392
  2.3 0.7 %moments.1 = (f32[3,16,32,128]{3,2,1,0:T(8,128)S(1)}, s16[9,16,128]{2,1,0:T(8,128)(2,1)S(1)}, s16[9,16,128]{2,1,0:T(8,128)(2,1)S(1)}) custom-call(bf16[19,16,32,128]{3,2,1,0:T(8,128)(2,1)S(1)} %copy-done), custom_call_target="tpu_custom_call" | custom-call | bytes 3600000 | tf_op jit(solution)/shard_map/moments/pallas_call | solution.py:150
  3.1 0.5 collective-permute-start
  3.6 2.6 %collective-permute-start.1 = (s16[9,16,128]{2,1,0:T(8,128)(2,1)S(1)}, s16[9,16,128]{2,1,0:T(8,128)(2,1)S(1)}, u32[]{:S(2)}, u32[]{:S(2)}) collective-permute-start(s16[9,16,128]{2,1,0:T(8,128)(2,1)S(1)} %get-tuple-element.25), channel_id=1, source_target_pairs={{0,3},{1,2},{2,1},{3,0},{4,7},{5,6},{6,5},{7,4},{8,11},{9,10},{10,... | collective-permute-start | bytes 110600 | tf_op jit(solution)/shard_map/ppermute | solution.py:50
  6.2 0.0 collective-permute-done.low_ref
  6.2 1.8 %collective-permute-done.1.high_ref = s16[9,16,128]{2,1,0:T(8,128)(2,1)S(1)} collective-permute-done((s16[9,16,128]{2,1,0:T(8,128)(2,1)S(1)}, s16[9,16,128]{2,1,0:T(8,128)(2,1)S(1)}, u32[]{:S(2)}, u32[]{:S(2)}) %collective-permute-start.1) | collective-permute-done | bytes 36896 | tf_op jit(solution)/shard_map/ppermute | solution.py:50
  8.0 0.1 edges.1
  8.1 1.6 %collective-permute-start.4 = (s16[7,40,128]{2,1,0:T(8,128)(2,1)S(1)}, s16[7,40,128]{2,1,0:T(8,128)(2,1)S(1)}, u32[]{:S(2)}, u32[]{:S(2)}) collective-permute-start(s16[7,40,128]{2,1,0:T(8,128)(2,1)S(1)} %get-tuple-element.29), channel_id=1, source_target_pairs={{0,4},{4,0},{8,12},{12,8},{16,20},{20,16},{24,28},{28,24},{1,5},{5... | collective-permute-start | bytes 215048 | tf_op jit(solution)/shard_map/ppermute | solution.py:50
  9.8 3.6 %collective-permute-start.5 = (s16[7,40,128]{2,1,0:T(8,128)(2,1)S(1)}, s16[7,40,128]{2,1,0:T(8,128)(2,1)S(1)}, u32[]{:S(2)}, u32[]{:S(2)}) collective-permute-start(s16[7,40,128]{2,1,0:T(8,128)(2,1)S(1)} %get-tuple-element.30), channel_id=1, source_target_pairs={{0,28},{4,8},{8,4},{12,16},{16,12},{20,24},{24,20},{28,0},{1,29},{... | collective-permute-start | bytes 215048 | tf_op jit(solution)/shard_map/ppermute | solution.py:50
  13.3 5.4 %inner_sums.1 = (f32[2,40,128]{2,1,0:T(8,128)S(1)}, f32[14,40,128]{2,1,0:T(8,128)S(1)}) custom-call(f32[3,16,32,128]{3,2,1,0:T(8,128)S(1)} %get-tuple-element.23.vel_ref, s16[9,16,128]{2,1,0:T(8,128)(2,1)S(1)} %collective-permute-done.low_ref, s16[9,16,128]{2,1,0:T(8,128)(2,1)S(1)} %collective-permute-done.1.high_ref), custom_call_target="tpu_custom_call" | custom-call | bytes 18000000 | tf_op jit(solution)/shard_map/inner_sums/pallas_call | solution.py:354
  18.7 0.0 collective-permute-done.4.first_ref.note_first
  18.7 0.0 collective-permute-done.5.second_ref.note_second
  18.7 2.4 %outer_sums.1 = (f32[72,128]{1,0:T(8,128)S(1)}, f32[8,40,128]{2,1,0:T(8,128)S(1)}) custom-call(f32[3,16,32,128]{3,2,1,0:T(8,128)S(1)} %get-tuple-element.23.vel_ref, s16[9,16,128]{2,1,0:T(8,128)(2,1)S(1)} %collective-permute-done.low_ref, s16[9,16,128]{2,1,0:T(8,128)(2,1)S(1)} %collective-permute-done.1.high_ref, ...), custom_call_target="tpu_custom_call" | custom-call | bytes 7200000 | tf_op jit(solution)/shard_map/outer_sums/pallas_call | solution.py:412
  21.1 0.1 collective-permute-start.6
  21.2 0.3 face_rows.1
  21.5 0.1 collective-permute-start.2
  21.6 1.6 %collective-permute-start.3 = (bf16[19,16,128]{2,1,0:T(8,128)(2,1)S(1)}, bf16[19,16,128]{2,1,0:T(8,128)(2,1)S(1)}, u32[]{:S(2)}, u32[]{:S(2)}) collective-permute-start(bf16[19,16,128]{2,1,0:T(8,128)(2,1)S(1)} %get-tuple-element.28), channel_id=1, source_target_pairs={{0,3},{1,2},{2,1},{3,0},{4,7},{5,6},{6,5},{7,4},{8,11},{9,10},{10,... | collective-permute-start | bytes 233480 | tf_op jit(solution)/shard_map/ppermute | solution.py:50
  23.2 1.9 %collective-permute-done.6 = f32[72,128]{1,0:T(8,128)S(1)} collective-permute-done((f32[72,128]{1,0:T(8,128)S(1)}, f32[72,128]{1,0:T(8,128)S(1)}, u32[]{:S(2)}, u32[]{:S(2)}) %collective-permute-start.6) | collective-permute-done | bytes 36896 | tf_op jit(solution)/shard_map/ppermute | solution.py:888
  25.1 0.0 collective-permute-start.7
  25.1 3.9 %collective-permute-done.7 = f32[72,128]{1,0:T(8,128)S(1)} collective-permute-done((f32[72,128]{1,0:T(8,128)S(1)}, f32[72,128]{1,0:T(8,128)S(1)}, u32[]{:S(2)}, u32[]{:S(2)}) %collective-permute-start.7) | collective-permute-done | bytes 36896 | tf_op jit(solution)/shard_map/ppermute | solution.py:888
  29.1 0.2 collective-permute-start.8
  29.3 0.0 collective-permute-done.2.first
  29.3 0.0 collective-permute-done.3.second
  29.3 2.1 %ready.1 = (f32[19,16,32,128]{3,2,1,0:T(8,128)S(1)}, f32[5,16,32,128]{3,2,1,0:T(8,128)S(1)}, f32[2,5,16,128]{3,2,1,0:T(8,128)S(1)}, f32[2,5,16,128]{3,2,1,0:T(8,128)S(1)}) custom-call(bf16[19,16,32,128]{3,2,1,0:T(8,128)(2,1)S(1)} %copy-done.1, bf16[19,16,128]{2,1,0:T(8,128)(2,1)S(1)} %collective-permute-done.2.first, ...), custom_call_target="tpu_custom_call" | custom-call | bytes 9000000 | tf_op jit(solution)/shard_map/ready/pallas_call | solution.py:579
  31.3 2.6 %collective-permute-done.8 = f32[72,128]{1,0:T(8,128)S(1)} collective-permute-done((f32[72,128]{1,0:T(8,128)S(1)}, f32[72,128]{1,0:T(8,128)S(1)}, u32[]{:S(2)}, u32[]{:S(2)}) %collective-permute-start.8) | collective-permute-done | bytes 36896 | tf_op jit(solution)/shard_map/ppermute | solution.py:888
  34.0 5.7 %step.1 = (bf16[19,16,32,128]{3,2,1,0:T(8,128)(2,1)}, f32[32,128]{1,0:T(8,128)}, f32[32,3,8]{2,1,0:T(4,128)S(1)}, bf16[5,32,128]{2,1,0:T(8,128)(2,1)S(1)}, bf16[5,32,128]{2,1,0:T(8,128)(2,1)S(1)}) custom-call(f32[19,16,32,128]{3,2,1,0:T(8,128)S(1)} %get-tuple-element.32.base_ref, f32[5,16,32,128]{3,2,1,0:T(8,128)S(1)} %get-tuple-element.33.shear_ref, ...), custom_call_target="tpu_custom_call" | custom-call | bytes 18000000 | tf_op jit(solution)/shard_map/step/pallas_call | solution.py:805
  39.7 0.2 collective-permute-start.9
  39.9 1.8 %collective-permute-start.10 = (bf16[5,32,128]{2,1,0:T(8,128)(2,1)S(1)}, bf16[5,32,128]{2,1,0:T(8,128)(2,1)S(1)}, u32[]{:S(2)}, u32[]{:S(2)}) collective-permute-start(bf16[5,32,128]{2,1,0:T(8,128)(2,1)S(1)} %get-tuple-element.40), channel_id=1, source_target_pairs={{0,28},{4,8},{8,4},{12,16},{16,12},{20,24},{24,20},{28,0},{1,29},{... | collective-permute-start | bytes 122888 | tf_op jit(solution)/shard_map/ppermute | solution.py:50
  41.7 11.4 %all_to_all.5 = f32[32,3,8]{2,1,0:T(4,128)S(1)} all-to-all(f32[32,3,8]{2,1,0:T(4,128)S(1)} %get-tuple-element.42), channel_id=1, replica_groups=mesh['span'=8,'cross'=4] {'span','cross'}, dimensions={0} | all-to-all | bytes 6144 | tf_op jit(solution)/shard_map/all_to_all | solution.py:893
  53.1 0.6 %reduce_sum.9 = f32[3,8]{1,0:T(4,128)} reduce(f32[32,3,8]{2,1,0:T(4,128)S(1)} %all_to_all.5, f32[]{:T(128)} %constant.0.clone.1), dimensions={0}, to_apply=%region_0.0 | reduce | flops 744 | bytes 3172 | tf_op jit(solution)/shard_map/reduce_sum | solution.py:895
  53.7 0.0 collective-permute-done.9.first
  53.7 0.7 %arrive.1 = bf16[19,16,32,128]{3,2,1,0:T(8,128)(2,1)} custom-call(bf16[19,16,32,128]{3,2,1,0:T(8,128)(2,1)} %get-tuple-element.38.next_in, bf16[5,32,128]{2,1,0:T(8,128)(2,1)S(1)} %collective-permute-done.9.first, bf16[5,32,128]{2,1,0:T(8,128)(2,1)S(1)} %collective-permute-done.10.second), custom_call_target="tpu_custom_call", output_to_operand_aliasing={{}: (0, {})} | custom-call | bytes 1800000 | tf_op jit(solution)/shard_map/arrive/pallas_call | solution.py:858
  (13 shorter events, 0.0 us)
Async XLA Ops:
  0.6 1.7 %copy-start = (bf16[19,16,32,128]{3,2,1,0:T(8,128)(2,1)S(1)}, bf16[19,16,32,128]{3,2,1,0:T(8,128)(2,1)}, u32[]{:S(2)}) copy-start(bf16[19,16,32,128]{3,2,1,0:T(8,128)(2,1)} %pops.5) | copy-start | bytes 7471108
  2.3 5.7 %copy-start.2 = (s32[128,8]{0,1:T(8,128)S(1)}, s32[128,8]{0,1:T(8,128)}, u32[]{:S(2)}) copy-start(s32[128,8]{0,1:T(8,128)} %param.5) | copy-start | bytes 12292
  2.3 5.7 %copy-start.3 = (f32[128,8]{0,1:T(8,128)S(1)}, f32[128,8]{0,1:T(8,128)}, u32[]{:S(2)}) copy-start(f32[128,8]{0,1:T(8,128)} %param.6) | copy-start | bytes 12292
  2.3 5.7 %copy-start.4 = (s32[128]{0:T(128)S(1)}, s32[128]{0:T(128)}, u32[]{:S(2)}) copy-start(s32[128]{0:T(128)} %param.7) | copy-start | bytes 1540
  2.3 18.8 %copy-start.1 = (bf16[19,16,32,128]{3,2,1,0:T(8,128)(2,1)S(1)}, bf16[19,16,32,128]{3,2,1,0:T(8,128)(2,1)}, u32[]{:S(2)}) copy-start(bf16[19,16,32,128]{3,2,1,0:T(8,128)(2,1)} %pops.5) | copy-start | bytes 7471108
  3.1 3.2 %collective-permute-start = (s16[9,16,128]{2,1,0:T(8,128)(2,1)S(1)}, s16[9,16,128]{2,1,0:T(8,128)(2,1)S(1)}, u32[]{:S(2)}, u32[]{:S(2)}) collective-permute-start(s16[9,16,128]{2,1,0:T(8,128)(2,1)S(1)} %get-tuple-element.24), channel_id=1, source_target_pairs={{0,1},{1,0},{2,3},{3,2},{4,5},{5,4},{6,7},{7,6},{8,9},{9,8},{10,11... | collective-permute-start | bytes 110600 | tf_op jit(solution)/shard_map/ppermute | solution.py:50
  3.6 4.4 %collective-permute-start.1 = (s16[9,16,128]{2,1,0:T(8,128)(2,1)S(1)}, s16[9,16,128]{2,1,0:T(8,128)(2,1)S(1)}, u32[]{:S(2)}, u32[]{:S(2)}) collective-permute-start(s16[9,16,128]{2,1,0:T(8,128)(2,1)S(1)} %get-tuple-element.25), channel_id=1, source_target_pairs={{0,3},{1,2},{2,1},{3,0},{4,7},{5,6},{6,5},{7,4},{8,11},{9,10},{10,... | collective-permute-start | bytes 110600 | tf_op jit(solution)/shard_map/ppermute | solution.py:50
  8.1 10.6 %collective-permute-start.4 = (s16[7,40,128]{2,1,0:T(8,128)(2,1)S(1)}, s16[7,40,128]{2,1,0:T(8,128)(2,1)S(1)}, u32[]{:S(2)}, u32[]{:S(2)}) collective-permute-start(s16[7,40,128]{2,1,0:T(8,128)(2,1)S(1)} %get-tuple-element.29), channel_id=1, source_target_pairs={{0,4},{4,0},{8,12},{12,8},{16,20},{20,16},{24,28},{28,24},{1,5},{5... | collective-permute-start | bytes 215048 | tf_op jit(solution)/shard_map/ppermute | solution.py:50
  9.8 9.0 %collective-permute-start.5 = (s16[7,40,128]{2,1,0:T(8,128)(2,1)S(1)}, s16[7,40,128]{2,1,0:T(8,128)(2,1)S(1)}, u32[]{:S(2)}, u32[]{:S(2)}) collective-permute-start(s16[7,40,128]{2,1,0:T(8,128)(2,1)S(1)} %get-tuple-element.30), channel_id=1, source_target_pairs={{0,28},{4,8},{8,4},{12,16},{16,12},{20,24},{24,20},{28,0},{1,29},{... | collective-permute-start | bytes 215048 | tf_op jit(solution)/shard_map/ppermute | solution.py:50
  21.1 4.0 %collective-permute-start.6 = (f32[72,128]{1,0:T(8,128)S(1)}, f32[72,128]{1,0:T(8,128)S(1)}, u32[]{:S(2)}, u32[]{:S(2)}) collective-permute-start(f32[72,128]{1,0:T(8,128)S(1)} %get-tuple-element.31.after_this), channel_id=1, source_target_pairs={{0,4},{4,0},{8,12},{12,8},{16,20},{20,16},{24,28},{28,24},{1,5},{5... | collective-permute-start | bytes 110600 | tf_op jit(solution)/shard_map/ppermute | solution.py:888
  21.5 7.8 %collective-permute-start.2 = (bf16[19,16,128]{2,1,0:T(8,128)(2,1)S(1)}, bf16[19,16,128]{2,1,0:T(8,128)(2,1)S(1)}, u32[]{:S(2)}, u32[]{:S(2)}) collective-permute-start(bf16[19,16,128]{2,1,0:T(8,128)(2,1)S(1)} %get-tuple-element.27), channel_id=1, source_target_pairs={{0,1},{1,0},{2,3},{3,2},{4,5},{5,4},{6,7},{7,6},{8,9},{9,8},{10,11... | collective-permute-start | bytes 233480 | tf_op jit(solution)/shard_map/ppermute | solution.py:50
  21.6 7.7 %collective-permute-start.3 = (bf16[19,16,128]{2,1,0:T(8,128)(2,1)S(1)}, bf16[19,16,128]{2,1,0:T(8,128)(2,1)S(1)}, u32[]{:S(2)}, u32[]{:S(2)}) collective-permute-start(bf16[19,16,128]{2,1,0:T(8,128)(2,1)S(1)} %get-tuple-element.28), channel_id=1, source_target_pairs={{0,3},{1,2},{2,1},{3,0},{4,7},{5,6},{6,5},{7,4},{8,11},{9,10},{10,... | collective-permute-start | bytes 233480 | tf_op jit(solution)/shard_map/ppermute | solution.py:50
  25.1 4.0 %collective-permute-start.7 = (f32[72,128]{1,0:T(8,128)S(1)}, f32[72,128]{1,0:T(8,128)S(1)}, u32[]{:S(2)}, u32[]{:S(2)}) collective-permute-start(f32[72,128]{1,0:T(8,128)S(1)} %add.9), channel_id=1, source_target_pairs={{0,8},{4,12},{8,0},{12,4},{16,24},{20,28},{24,16},{28,20},{1,9},{5... | collective-permute-start | bytes 110600 | tf_op jit(solution)/shard_map/ppermute | solution.py:888
  29.1 4.9 %collective-permute-start.8 = (f32[72,128]{1,0:T(8,128)S(1)}, f32[72,128]{1,0:T(8,128)S(1)}, u32[]{:S(2)}, u32[]{:S(2)}) collective-permute-start(f32[72,128]{1,0:T(8,128)S(1)} %add.10), channel_id=1, source_target_pairs={{0,16},{4,20},{8,24},{12,28},{16,0},{20,4},{24,8},{28,12},{1,17},{... | collective-permute-start | bytes 110600 | tf_op jit(solution)/shard_map/ppermute | solution.py:888
  39.7 14.0 %collective-permute-start.9 = (bf16[5,32,128]{2,1,0:T(8,128)(2,1)S(1)}, bf16[5,32,128]{2,1,0:T(8,128)(2,1)S(1)}, u32[]{:S(2)}, u32[]{:S(2)}) collective-permute-start(bf16[5,32,128]{2,1,0:T(8,128)(2,1)S(1)} %get-tuple-element.39), channel_id=1, source_target_pairs={{0,4},{4,0},{8,12},{12,8},{16,20},{20,16},{24,28},{28,24},{1,5},{5... | collective-permute-start | bytes 122888 | tf_op jit(solution)/shard_map/ppermute | solution.py:50
  39.9 13.8 %collective-permute-start.10 = (bf16[5,32,128]{2,1,0:T(8,128)(2,1)S(1)}, bf16[5,32,128]{2,1,0:T(8,128)(2,1)S(1)}, u32[]{:S(2)}, u32[]{:S(2)}) collective-permute-start(bf16[5,32,128]{2,1,0:T(8,128)(2,1)S(1)} %get-tuple-element.40), channel_id=1, source_target_pairs={{0,28},{4,8},{8,4},{12,16},{16,12},{20,24},{24,20},{28,0},{1,29},{... | collective-permute-start | bytes 122888 | tf_op jit(solution)/shard_map/ppermute | solution.py:50

commit v3 on v2

--- a/solution.py
+++ b/solution.py
@@ -12,7 +12,7 @@
 HALO = 3
 EXT = 40
 PAD = 56
-OWN = 10
+OWN = 11
 TOP = 8
 CHUNKS = (8, 16, 24, 32, 40)
 VMEM = 28 * 1024 * 1024
@@ -234,17 +234,29 @@
     )(vel, low, high, cells, weights, segments)
 
 
-def strain_parts(ref, p, row):
-    grads = []
-    for dim in range(3):
-        here = ref[dim, p, pl.ds(row, 8), :]
-        grads.append(
-            (
-                plus(here) - minus(here),
-                ref[dim, p, pl.ds(row + 1, 8), :] - ref[dim, p, pl.ds(row - 1, 8), :],
-                ref[dim, p + 1, pl.ds(row, 8), :] - ref[dim, p - 1, pl.ds(row, 8), :],
-            )
+def plane_loop(start, stop, body, carry, most):
+    count = stop - start
+    step = max(size for size in range(1, most + 1) if count % size == 0)
+
+    def block(index, carry):
+        for shift in range(step):
+            carry = body(start + index * step + shift, carry)
+        return carry
+
+    if count == step:
+        return block(0, carry)
+    return lax.fori_loop(0, count // step, block, carry)
+
+
+def strain_parts(ref, p, row, before, here, after):
+    grads = [
+        (
+            plus(here[dim]) - minus(here[dim]),
+            ref[dim, p, pl.ds(row + 1, 8), :] - ref[dim, p, pl.ds(row - 1, 8), :],
+            after[dim] - before[dim],
         )
+        for dim in range(3)
+    ]
     parts = [
         grads[0][0],
         grads[1][1],
@@ -265,64 +277,71 @@
 PAIRS = ((0, 0), (1, 1), (2, 2), (0, 1), (0, 2), (1, 2))
 
 
-def model_sums(planes, ext, hat, prods, zsum, acc_ref, store_mag):
-    def first_pass(p, carry):
-        for row in CHUNKS:
-            rows = pl.ds(row, 8)
-            parts, size = strain_parts(ext, p, row)
+def three(ref, p, rows):
+    return [ref[dim, p, rows, :] for dim in range(3)]
+
+
+def model_sums(planes, ext, hat, zsum, zvel, acc_ref, store_mag):
+    for row in CHUNKS:
+        rows = pl.ds(row, 8)
+
+        def first_pass(p, carry):
+            before, here, lag, last = carry
+            after = three(ext, p + 1, rows)
+            parts, size = strain_parts(ext, p, row, before, here, after)
             store_mag(p, row, size)
-            for k in range(6):
-                prods[k, p, rows, :] = size * parts[k]
-            for k, (i, j) in enumerate(PAIRS):
-                prods[6 + k, p, rows, :] = ext[i, p, rows, :] * ext[j, p, rows, :]
+            prods = [size * part for part in parts] + [here[i] * here[j] for i, j in PAIRS]
+            for k in range(12):
+                zsum[k, p - 1, rows, :] = lag[k] + prods[k]
             for dim in range(3):
-                lines = []
-                for shift in (-1, 0, 1):
-                    at = pl.ds(row + shift, 8)
-                    lines.append(
-                        weigh(ext[dim, p - 1, at, :], ext[dim, p, at, :], ext[dim, p + 1, at, :])
-                    )
-                line = weigh(*lines)
-                hat[dim, p, rows, :] = (1.0 / 64.0) * weigh(minus(line), line, plus(line))
-        return carry
-
-    lax.fori_loop(1, planes - 1, first_pass, 0)
+                zvel[dim, p, rows, :] = weigh(before[dim], here[dim], after[dim])
+            lag = [last[k] + (prods[k] + prods[k]) for k in range(12)]
+            return here, after, lag, prods
+
+        none = [jnp.zeros((8, LANES), jnp.float32)] * 12
+        carry = (three(ext, 0, rows), three(ext, 1, rows), none, none)
+        plane_loop(1, planes - 1, first_pass, carry, 7)
 
     def second_pass(p, carry):
         for row in CHUNKS:
-            rows = pl.ds(row, 8)
-            for k in range(12):
-                zsum[k, rows, :] = weigh(
-                    prods[k, p - 1, rows, :], prods[k, p, rows, :], prods[k, p + 1, rows, :]
-                )
-        for row in CHUNKS:
-            rows = pl.ds(row, 8)
-            parts, size = strain_parts(hat, p, row)
+            for dim in range(3):
+                line = weigh(*[zvel[dim, p, pl.ds(row + shift, 8), :] for shift in (-1, 0, 1)])
+                hat[dim, p, pl.ds(row, 8), :] = (1.0 / 64.0) * weigh(minus(line), line, plus(line))
+        return carry
+
+    plane_loop(1, planes - 1, second_pass, 0, 2)
+
+    for row in CHUNKS:
+        rows = pl.ds(row, 8)
+
+        def third_pass(p, carry):
+            before, here, lm, mm = carry
+            after = three(hat, p + 1, rows)
+            parts, size = strain_parts(hat, p, row, before, here, after)
             size = 256.0 * size
-            here = [hat[dim, p, rows, :] for dim in range(3)]
             scaled = [64.0 * speed for speed in here]
-            smooth = []
-            for k in range(12):
-                line = weigh(
-                    zsum[k, pl.ds(row - 1, 8), :], zsum[k, rows, :], zsum[k, pl.ds(row + 1, 8), :]
-                )
-                smooth.append(weigh(minus(line), line, plus(line)))
-            lm = 0.0
             squares = [0.0, 0.0]
             for k, (i, j) in enumerate(PAIRS):
-                model = smooth[k] - size * parts[k]
-                leonard = smooth[6 + k] - scaled[i] * here[j]
-                lm = lm + leonard * model
+                smooth = []
+                for field in (k, 6 + k):
+                    line = weigh(
+                        *[zsum[field, p, pl.ds(row + shift, 8), :] for shift in (-1, 0, 1)]
+                    )
+                    smooth.append(weigh(minus(line), line, plus(line)))
+                model = smooth[0] - size * parts[k]
+                lm = lm + (smooth[1] - scaled[i] * here[j]) * model
                 squares[k // 3] = squares[k // 3] + model * model
-            out = pl.ds(row - TOP, 8)
-            acc_ref[0, out, :] += (1.0 / 4096.0) * lm
-            acc_ref[1, out, :] += (1.0 / 4096.0) * (squares[0] + 0.5 * squares[1])
-        return carry
-
-    lax.fori_loop(2, planes - 2, second_pass, 0)
-
-
-def inner_kernel(vel_ref, low_ref, high_ref, acc_ref, mag_ref, ext, hat, prods, zsum, rows):
+            return here, after, lm, mm + (squares[0] + 0.5 * squares[1])
+
+        none = jnp.zeros((8, LANES), jnp.float32)
+        carry = (three(hat, 1, rows), three(hat, 2, rows), none, none)
+        _, _, lm, mm = plane_loop(2, planes - 2, third_pass, carry, 6)
+        out = pl.ds(row - TOP, 8)
+        acc_ref[0, out, :] += (1.0 / 4096.0) * lm
+        acc_ref[1, out, :] += (1.0 / 4096.0) * mm
+
+
+def inner_kernel(vel_ref, low_ref, high_ref, acc_ref, mag_ref, ext, hat, zsum, zvel, rows):
     depth = vel_ref.shape[1]
     decode_rows(low_ref, high_ref, rows)
 
@@ -336,7 +355,7 @@
     def store_mag(p, row, size):
         mag_ref[p - 1, pl.ds(row - TOP, 8), :] = size
 
-    model_sums(depth, ext, hat, prods, zsum, acc_ref, store_mag)
+    model_sums(depth, ext, hat, zsum, zvel, acc_ref, store_mag)
 
 
 def model_scratch(planes, depth):
@@ -344,7 +363,7 @@
         pltpu.VMEM((3, planes, PAD, LANES), jnp.float32),
         pltpu.VMEM((3, planes, PAD, LANES), jnp.float32),
         pltpu.VMEM((12, planes, PAD, LANES), jnp.float32),
-        pltpu.VMEM((12, PAD, LANES), jnp.float32),
+        pltpu.VMEM((3, planes, PAD, LANES), jnp.float32),
         pltpu.VMEM((2, 3 * HALO, depth, LANES), jnp.float32),
     ]
 
@@ -377,8 +396,8 @@
     mag_ref,
     ext,
     hat,
-    prods,
     zsum,
+    zvel,
     rows,
     acc,
 ):
@@ -400,7 +419,7 @@
         def store_mag(p, row, size):
             mag_ref[4 * side + p - 1, pl.ds(row - TOP, 8), :] = size
 
-        model_sums(6, ext, hat, prods, zsum, acc, store_mag)
+        model_sums(6, ext, hat, zsum, zvel, acc, store_mag)
     lines = width + 2
     sums_ref[...] = jnp.zeros_like(sums_ref)
     for index in range(2):
@@ -829,9 +848,11 @@
     )(*parts, sums, mag_in, mag_out, cells, weights, segments, *notes)
 
 
-def arrive_kernel(next_in, first, second, next_hbm, sems):
+def arrive_kernel(next_in, first, second, arrived_hbm, next_hbm, force_ref, arrived, sems):
     depth = next_hbm.shape[1]
     odd = is_odd("span")
+    shares = pltpu.make_async_copy(arrived_hbm, arrived, sems.at[10])
+    shares.start()
 
     def place(below, above):
         copies = []
@@ -852,20 +873,29 @@
     def _():
         place(second, first)
 
-
-def arrive(populations_next, first, second):
+    shares.wait()
+    force_ref[...] = jnp.sum(arrived[...], axis=0)
+
+
+def arrive(populations_next, first, second, arrived):
     hbm = pl.BlockSpec(memory_space=pl.ANY)
     return pl.pallas_call(
         arrive_kernel,
-        out_shape=full(populations_next.shape, jnp.bfloat16),
-        in_specs=[hbm] + in_vmem(2),
-        out_specs=hbm,
+        out_shape=(
+            full(populations_next.shape, jnp.bfloat16),
+            full(arrived.shape[1:], jnp.float32),
+        ),
+        in_specs=[hbm] + in_vmem(2) + [hbm],
+        out_specs=(hbm, in_vmem(1)[0]),
         input_output_aliases={0: 0},
-        scratch_shapes=[pltpu.SemaphoreType.DMA((10,))],
+        scratch_shapes=[
+            pltpu.VMEM(arrived.shape, jnp.float32),
+            pltpu.SemaphoreType.DMA((11,)),
+        ],
         compiler_params=params(),
         cost_estimate=cost(0.5),
         name="arrive",
-    )(populations_next, first, second)
+    )(populations_next, first, second, arrived)
 
 
 def local(populations, cell_index, marker_weight, segment_id):
@@ -891,8 +921,8 @@
         parts, sums, mag_in, mag_out, cells, weights, segments, planes, owners
     )
     arrived = lax.all_to_all(packed, ("span", "cross"), 0, 0)
-    populations_next = arrive(moved, *swap(*leaving, "span"))
-    return (populations_next, eddy_coeff, jnp.sum(arrived, axis=0))
+    populations_next, segment_force = arrive(moved, *swap(*leaving, "span"), arrived)
+    return (populations_next, eddy_coeff, segment_force)
 
 
 def solution(mesh):

time: 54.6 us -> 54 us (0.989)
  other arithmetic: 0.64 us -> 0.02 us
    pallas_call x1, Pallas kernels: 0.72 us -> 1.38 us  [arrive(): pl.pallas_call(arrive_kernel, out_shape=(full(populations_next.shape, jnp...]
    reduce_sum x1 -> x0, other arithmetic: 0.62 us -> none  [local(): return (populations_next, eddy_coeff, jnp.sum(arrived, axis=0))]
    pallas_call x1, Pallas kernels: 2.36 us -> 1.79 us  [outer_sums(): pl.pallas_call(outer_kernel, out_shape=(full((-(-2 * (width + 2) // 8) *...]
  transfers between devices with their start and end apart: 11 -> 11, of which waited for: 4 -> 4; matrix products, arithmetic and copies ran while one was open for 1% -> 0% of each run, Pallas kernels for 14% -> 14%
where the time goes in v3:
time: 54 us; the launch traced here: 53.8 us
  Pallas kernels  17.4 us (32%)
  starting transfers between devices  12.3 us (23%)
  blocking collectives  11.4 us (21%)
  waiting for transfers between devices  10.3 us (19%)
  local copies, waits for them, and re-layouts  1.71 us (3%)
  between operations  0.75 us (1%)
    ppermute x8, starting transfers between devices, swap(): return (lax.ppermute(first, axis, near), lax.ppermute(second, axis, other))  12 us
    all_to_all x1, blocking collectives, local(): arrived = lax.all_to_all(packed, ('span', 'cross'), 0, 0)  11.4 us
    ppermute x3, waiting for transfers between devices, local(): sums = sums + lax.ppermute(sums, 'span', pairs)  8.5 us
    pallas_call x1, Pallas kernels, step(): pl.pallas_call(step_kernel, out_shape=(full((19, depth, width, lanes), jn...  5.73 us
    pallas_call x1, Pallas kernels, inner_sums(): pl.pallas_call(inner_kernel, out_shape=(full((2, EXT, LANES), jnp.float32...  5.28 us
    pallas_call x1, Pallas kernels, ready(): pl.pallas_call(ready_kernel, out_shape=(full((19, depth, width, lanes), j...  2.06 us
    pallas_call x1, Pallas kernels, outer_sums(): pl.pallas_call(outer_kernel, out_shape=(full((-(-2 * (width + 2) // 8) *...  1.79 us
    ppermute x8, waiting for transfers between devices, swap(): return (lax.ppermute(first, axis, near), lax.ppermute(second, axis, other))  1.77 us
  transfers between devices with their start and end apart: 11, of which 4 were waited for; matrix products, arithmetic and copies ran while one was open for 0% of the time, Pallas kernels for 14%

profile of v3, /device:TPU:0, one launch (start us, length us, event | category | flops | bytes accessed | tf_op | source)
XLA Modules:
  0.0 53.8 jit_solution(253071465138520207)
XLA Ops:
  0.6 1.7 %copy-done = bf16[19,16,32,128]{3,2,1,0:T(8,128)(2,1)S(1)} copy-done((bf16[19,16,32,128]{3,2,1,0:T(8,128)(2,1)S(1)}, bf16[19,16,32,128]{3,2,1,0:T(8,128)(2,1)}, u32[]{:S(2)}) %copy-start) | copy-done | bytes 2490392
  2.3 0.7 %moments.1 = (f32[3,16,32,128]{3,2,1,0:T(8,128)S(1)}, s16[9,16,128]{2,1,0:T(8,128)(2,1)S(1)}, s16[9,16,128]{2,1,0:T(8,128)(2,1)S(1)}) custom-call(bf16[19,16,32,128]{3,2,1,0:T(8,128)(2,1)S(1)} %copy-done), custom_call_target="tpu_custom_call" | custom-call | bytes 3600000 | tf_op jit(solution)/shard_map/moments/pallas_call | solution.py:150
  3.1 0.5 collective-permute-start
  3.6 2.6 %collective-permute-start.1 = (s16[9,16,128]{2,1,0:T(8,128)(2,1)S(1)}, s16[9,16,128]{2,1,0:T(8,128)(2,1)S(1)}, u32[]{:S(2)}, u32[]{:S(2)}) collective-permute-start(s16[9,16,128]{2,1,0:T(8,128)(2,1)S(1)} %get-tuple-element.27), channel_id=1, source_target_pairs={{0,3},{1,2},{2,1},{3,0},{4,7},{5,6},{6,5},{7,4},{8,11},{9,10},{10,... | collective-permute-start | bytes 110600 | tf_op jit(solution)/shard_map/ppermute | solution.py:50
  6.2 0.0 collective-permute-done.low_ref
  6.2 1.8 %collective-permute-done.1.high_ref = s16[9,16,128]{2,1,0:T(8,128)(2,1)S(1)} collective-permute-done((s16[9,16,128]{2,1,0:T(8,128)(2,1)S(1)}, s16[9,16,128]{2,1,0:T(8,128)(2,1)S(1)}, u32[]{:S(2)}, u32[]{:S(2)}) %collective-permute-start.1) | collective-permute-done | bytes 36896 | tf_op jit(solution)/shard_map/ppermute | solution.py:50
  8.0 0.1 edges.1
  8.1 1.6 %collective-permute-start.4 = (s16[7,40,128]{2,1,0:T(8,128)(2,1)S(1)}, s16[7,40,128]{2,1,0:T(8,128)(2,1)S(1)}, u32[]{:S(2)}, u32[]{:S(2)}) collective-permute-start(s16[7,40,128]{2,1,0:T(8,128)(2,1)S(1)} %get-tuple-element.31), channel_id=1, source_target_pairs={{0,4},{4,0},{8,12},{12,8},{16,20},{20,16},{24,28},{28,24},{1,5},{5... | collective-permute-start | bytes 215048 | tf_op jit(solution)/shard_map/ppermute | solution.py:50
  9.8 3.6 %collective-permute-start.5 = (s16[7,40,128]{2,1,0:T(8,128)(2,1)S(1)}, s16[7,40,128]{2,1,0:T(8,128)(2,1)S(1)}, u32[]{:S(2)}, u32[]{:S(2)}) collective-permute-start(s16[7,40,128]{2,1,0:T(8,128)(2,1)S(1)} %get-tuple-element.32), channel_id=1, source_target_pairs={{0,28},{4,8},{8,4},{12,16},{16,12},{20,24},{24,20},{28,0},{1,29},{... | collective-permute-start | bytes 215048 | tf_op jit(solution)/shard_map/ppermute | solution.py:50
  13.3 5.3 %inner_sums.1 = (f32[2,40,128]{2,1,0:T(8,128)S(1)}, f32[14,40,128]{2,1,0:T(8,128)S(1)}) custom-call(f32[3,16,32,128]{3,2,1,0:T(8,128)S(1)} %get-tuple-element.25.vel_ref, s16[9,16,128]{2,1,0:T(8,128)(2,1)S(1)} %collective-permute-done.low_ref, s16[9,16,128]{2,1,0:T(8,128)(2,1)S(1)} %collective-permute-done.1.high_ref), custom_call_target="tpu_custom_call" | custom-call | bytes 18000000 | tf_op jit(solution)/shard_map/inner_sums/pallas_call | solution.py:373
  18.6 0.0 collective-permute-done.4.first_ref.note_first
  18.6 0.0 collective-permute-done.5.second_ref.note_second
  18.6 1.8 %outer_sums.1 = (f32[72,128]{1,0:T(8,128)S(1)}, f32[8,40,128]{2,1,0:T(8,128)S(1)}) custom-call(f32[3,16,32,128]{3,2,1,0:T(8,128)S(1)} %get-tuple-element.25.vel_ref, s16[9,16,128]{2,1,0:T(8,128)(2,1)S(1)} %collective-permute-done.low_ref, s16[9,16,128]{2,1,0:T(8,128)(2,1)S(1)} %collective-permute-done.1.high_ref, ...), custom_call_target="tpu_custom_call" | custom-call | bytes 7200000 | tf_op jit(solution)/shard_map/outer_sums/pallas_call | solution.py:431
  20.4 0.1 collective-permute-start.6
  20.5 0.3 face_rows.1
  20.8 0.1 collective-permute-start.2
  20.9 1.6 %collective-permute-start.3 = (bf16[19,16,128]{2,1,0:T(8,128)(2,1)S(1)}, bf16[19,16,128]{2,1,0:T(8,128)(2,1)S(1)}, u32[]{:S(2)}, u32[]{:S(2)}) collective-permute-start(bf16[19,16,128]{2,1,0:T(8,128)(2,1)S(1)} %get-tuple-element.30), channel_id=1, source_target_pairs={{0,3},{1,2},{2,1},{3,0},{4,7},{5,6},{6,5},{7,4},{8,11},{9,10},{10,... | collective-permute-start | bytes 233480 | tf_op jit(solution)/shard_map/ppermute | solution.py:50
  22.5 1.9 %collective-permute-done.6 = f32[72,128]{1,0:T(8,128)S(1)} collective-permute-done((f32[72,128]{1,0:T(8,128)S(1)}, f32[72,128]{1,0:T(8,128)S(1)}, u32[]{:S(2)}, u32[]{:S(2)}) %collective-permute-start.6) | collective-permute-done | bytes 36896 | tf_op jit(solution)/shard_map/ppermute | solution.py:918
  24.4 0.0 collective-permute-start.7
  24.5 3.9 %collective-permute-done.7 = f32[72,128]{1,0:T(8,128)S(1)} collective-permute-done((f32[72,128]{1,0:T(8,128)S(1)}, f32[72,128]{1,0:T(8,128)S(1)}, u32[]{:S(2)}, u32[]{:S(2)}) %collective-permute-start.7) | collective-permute-done | bytes 36896 | tf_op jit(solution)/shard_map/ppermute | solution.py:918
  28.4 0.2 collective-permute-start.8
  28.6 0.0 collective-permute-done.2.first
  28.6 0.0 collective-permute-done.3.second
  28.6 2.1 %ready.1 = (f32[19,16,32,128]{3,2,1,0:T(8,128)S(1)}, f32[5,16,32,128]{3,2,1,0:T(8,128)S(1)}, f32[2,5,16,128]{3,2,1,0:T(8,128)S(1)}, f32[2,5,16,128]{3,2,1,0:T(8,128)S(1)}) custom-call(bf16[19,16,32,128]{3,2,1,0:T(8,128)(2,1)S(1)} %copy-done.1, bf16[19,16,128]{2,1,0:T(8,128)(2,1)S(1)} %collective-permute-done.2.first, ...), custom_call_target="tpu_custom_call" | custom-call | bytes 9000000 | tf_op jit(solution)/shard_map/ready/pallas_call | solution.py:598
  30.7 2.6 %collective-permute-done.8 = f32[72,128]{1,0:T(8,128)S(1)} collective-permute-done((f32[72,128]{1,0:T(8,128)S(1)}, f32[72,128]{1,0:T(8,128)S(1)}, u32[]{:S(2)}, u32[]{:S(2)}) %collective-permute-start.8) | collective-permute-done | bytes 36896 | tf_op jit(solution)/shard_map/ppermute | solution.py:918
  33.3 5.7 %step.1 = (bf16[19,16,32,128]{3,2,1,0:T(8,128)(2,1)}, f32[32,128]{1,0:T(8,128)}, f32[32,3,8]{2,1,0:T(4,128)S(1)}, bf16[5,32,128]{2,1,0:T(8,128)(2,1)S(1)}, bf16[5,32,128]{2,1,0:T(8,128)(2,1)S(1)}) custom-call(f32[19,16,32,128]{3,2,1,0:T(8,128)S(1)} %get-tuple-element.34.base_ref, f32[5,16,32,128]{3,2,1,0:T(8,128)S(1)} %get-tuple-element.35.shear_ref, ...), custom_call_target="tpu_custom_call" | custom-call | bytes 18000000 | tf_op jit(solution)/shard_map/step/pallas_call | solution.py:824
  39.0 0.2 collective-permute-start.9
  39.2 1.8 %collective-permute-start.10 = (bf16[5,32,128]{2,1,0:T(8,128)(2,1)S(1)}, bf16[5,32,128]{2,1,0:T(8,128)(2,1)S(1)}, u32[]{:S(2)}, u32[]{:S(2)}) collective-permute-start(bf16[5,32,128]{2,1,0:T(8,128)(2,1)S(1)} %get-tuple-element.42), channel_id=1, source_target_pairs={{0,28},{4,8},{8,4},{12,16},{16,12},{20,24},{24,20},{28,0},{1,29},{... | collective-permute-start | bytes 122888 | tf_op jit(solution)/shard_map/ppermute | solution.py:50
  41.0 11.4 %all_to_all.5.arrived_hbm = f32[32,3,8]{2,1,0:T(4,128)S(1)} all-to-all(f32[32,3,8]{2,1,0:T(4,128)S(1)} %get-tuple-element.43), channel_id=1, replica_groups=mesh['span'=8,'cross'=4] {'span','cross'}, dimensions={0} | all-to-all | bytes 6144 | tf_op jit(solution)/shard_map/all_to_all | solution.py:923
  52.4 0.0 collective-permute-done.9.first
  52.4 0.0 collective-permute-done.10.second
  52.4 1.4 %arrive.1 = (bf16[19,16,32,128]{3,2,1,0:T(8,128)(2,1)}, f32[3,8]{1,0:T(4,128)}) custom-call(bf16[19,16,32,128]{3,2,1,0:T(8,128)(2,1)} %get-tuple-element.40.next_in, bf16[5,32,128]{2,1,0:T(8,128)(2,1)S(1)} %collective-permute-done.9.first, bf16[5,32,128]{2,1,0:T(8,128)(2,1)S(1)} %collective-permute-done.10.second, ...), custom_call_target="tpu_custom_call", output_to_operand_aliasing={{0}: (0, {})} | custom-call | bytes 1800000 | tf_op jit(solution)/shard_map/arrive/pallas_call | solution.py:882
  (12 shorter events, 0.0 us)
Async XLA Ops:
  0.6 1.7 %copy-start = (bf16[19,16,32,128]{3,2,1,0:T(8,128)(2,1)S(1)}, bf16[19,16,32,128]{3,2,1,0:T(8,128)(2,1)}, u32[]{:S(2)}) copy-start(bf16[19,16,32,128]{3,2,1,0:T(8,128)(2,1)} %pops.5) | copy-start | bytes 7471108
  2.3 5.7 %copy-start.2 = (s32[128,8]{0,1:T(8,128)S(1)}, s32[128,8]{0,1:T(8,128)}, u32[]{:S(2)}) copy-start(s32[128,8]{0,1:T(8,128)} %param.5) | copy-start | bytes 12292
  2.3 5.7 %copy-start.3 = (f32[128,8]{0,1:T(8,128)S(1)}, f32[128,8]{0,1:T(8,128)}, u32[]{:S(2)}) copy-start(f32[128,8]{0,1:T(8,128)} %param.6) | copy-start | bytes 12292
  2.3 5.7 %copy-start.4 = (s32[128]{0:T(128)S(1)}, s32[128]{0:T(128)}, u32[]{:S(2)}) copy-start(s32[128]{0:T(128)} %param.7) | copy-start | bytes 1540
  2.3 18.2 %copy-start.1 = (bf16[19,16,32,128]{3,2,1,0:T(8,128)(2,1)S(1)}, bf16[19,16,32,128]{3,2,1,0:T(8,128)(2,1)}, u32[]{:S(2)}) copy-start(bf16[19,16,32,128]{3,2,1,0:T(8,128)(2,1)} %pops.5) | copy-start | bytes 7471108
  3.1 3.2 %collective-permute-start = (s16[9,16,128]{2,1,0:T(8,128)(2,1)S(1)}, s16[9,16,128]{2,1,0:T(8,128)(2,1)S(1)}, u32[]{:S(2)}, u32[]{:S(2)}) collective-permute-start(s16[9,16,128]{2,1,0:T(8,128)(2,1)S(1)} %get-tuple-element.26), channel_id=1, source_target_pairs={{0,1},{1,0},{2,3},{3,2},{4,5},{5,4},{6,7},{7,6},{8,9},{9,8},{10,11... | collective-permute-start | bytes 110600 | tf_op jit(solution)/shard_map/ppermute | solution.py:50
  3.6 4.4 %collective-permute-start.1 = (s16[9,16,128]{2,1,0:T(8,128)(2,1)S(1)}, s16[9,16,128]{2,1,0:T(8,128)(2,1)S(1)}, u32[]{:S(2)}, u32[]{:S(2)}) collective-permute-start(s16[9,16,128]{2,1,0:T(8,128)(2,1)S(1)} %get-tuple-element.27), channel_id=1, source_target_pairs={{0,3},{1,2},{2,1},{3,0},{4,7},{5,6},{6,5},{7,4},{8,11},{9,10},{10,... | collective-permute-start | bytes 110600 | tf_op jit(solution)/shard_map/ppermute | solution.py:50
  8.1 10.5 %collective-permute-start.4 = (s16[7,40,128]{2,1,0:T(8,128)(2,1)S(1)}, s16[7,40,128]{2,1,0:T(8,128)(2,1)S(1)}, u32[]{:S(2)}, u32[]{:S(2)}) collective-permute-start(s16[7,40,128]{2,1,0:T(8,128)(2,1)S(1)} %get-tuple-element.31), channel_id=1, source_target_pairs={{0,4},{4,0},{8,12},{12,8},{16,20},{20,16},{24,28},{28,24},{1,5},{5... | collective-permute-start | bytes 215048 | tf_op jit(solution)/shard_map/ppermute | solution.py:50
  9.8 8.9 %collective-permute-start.5 = (s16[7,40,128]{2,1,0:T(8,128)(2,1)S(1)}, s16[7,40,128]{2,1,0:T(8,128)(2,1)S(1)}, u32[]{:S(2)}, u32[]{:S(2)}) collective-permute-start(s16[7,40,128]{2,1,0:T(8,128)(2,1)S(1)} %get-tuple-element.32), channel_id=1, source_target_pairs={{0,28},{4,8},{8,4},{12,16},{16,12},{20,24},{24,20},{28,0},{1,29},{... | collective-permute-start | bytes 215048 | tf_op jit(solution)/shard_map/ppermute | solution.py:50
  20.4 4.0 %collective-permute-start.6 = (f32[72,128]{1,0:T(8,128)S(1)}, f32[72,128]{1,0:T(8,128)S(1)}, u32[]{:S(2)}, u32[]{:S(2)}) collective-permute-start(f32[72,128]{1,0:T(8,128)S(1)} %get-tuple-element.33.after_this), channel_id=1, source_target_pairs={{0,4},{4,0},{8,12},{12,8},{16,20},{20,16},{24,28},{28,24},{1,5},{5... | collective-permute-start | bytes 110600 | tf_op jit(solution)/shard_map/ppermute | solution.py:918
  20.8 7.8 %collective-permute-start.2 = (bf16[19,16,128]{2,1,0:T(8,128)(2,1)S(1)}, bf16[19,16,128]{2,1,0:T(8,128)(2,1)S(1)}, u32[]{:S(2)}, u32[]{:S(2)}) collective-permute-start(bf16[19,16,128]{2,1,0:T(8,128)(2,1)S(1)} %get-tuple-element.29), channel_id=1, source_target_pairs={{0,1},{1,0},{2,3},{3,2},{4,5},{5,4},{6,7},{7,6},{8,9},{9,8},{10,11... | collective-permute-start | bytes 233480 | tf_op jit(solution)/shard_map/ppermute | solution.py:50
  20.9 7.7 %collective-permute-start.3 = (bf16[19,16,128]{2,1,0:T(8,128)(2,1)S(1)}, bf16[19,16,128]{2,1,0:T(8,128)(2,1)S(1)}, u32[]{:S(2)}, u32[]{:S(2)}) collective-permute-start(bf16[19,16,128]{2,1,0:T(8,128)(2,1)S(1)} %get-tuple-element.30), channel_id=1, source_target_pairs={{0,3},{1,2},{2,1},{3,0},{4,7},{5,6},{6,5},{7,4},{8,11},{9,10},{10,... | collective-permute-start | bytes 233480 | tf_op jit(solution)/shard_map/ppermute | solution.py:50
  24.4 4.0 %collective-permute-start.7 = (f32[72,128]{1,0:T(8,128)S(1)}, f32[72,128]{1,0:T(8,128)S(1)}, u32[]{:S(2)}, u32[]{:S(2)}) collective-permute-start(f32[72,128]{1,0:T(8,128)S(1)} %add.9), channel_id=1, source_target_pairs={{0,8},{4,12},{8,0},{12,4},{16,24},{20,28},{24,16},{28,20},{1,9},{5... | collective-permute-start | bytes 110600 | tf_op jit(solution)/shard_map/ppermute | solution.py:918
  28.4 4.9 %collective-permute-start.8 = (f32[72,128]{1,0:T(8,128)S(1)}, f32[72,128]{1,0:T(8,128)S(1)}, u32[]{:S(2)}, u32[]{:S(2)}) collective-permute-start(f32[72,128]{1,0:T(8,128)S(1)} %add.10), channel_id=1, source_target_pairs={{0,16},{4,20},{8,24},{12,28},{16,0},{20,4},{24,8},{28,12},{1,17},{... | collective-permute-start | bytes 110600 | tf_op jit(solution)/shard_map/ppermute | solution.py:918
  39.0 13.4 %collective-permute-start.9 = (bf16[5,32,128]{2,1,0:T(8,128)(2,1)S(1)}, bf16[5,32,128]{2,1,0:T(8,128)(2,1)S(1)}, u32[]{:S(2)}, u32[]{:S(2)}) collective-permute-start(bf16[5,32,128]{2,1,0:T(8,128)(2,1)S(1)} %get-tuple-element.41), channel_id=1, source_target_pairs={{0,4},{4,0},{8,12},{12,8},{16,20},{20,16},{24,28},{28,24},{1,5},{5... | collective-permute-start | bytes 122888 | tf_op jit(solution)/shard_map/ppermute | solution.py:50
  39.2 13.2 %collective-permute-start.10 = (bf16[5,32,128]{2,1,0:T(8,128)(2,1)S(1)}, bf16[5,32,128]{2,1,0:T(8,128)(2,1)S(1)}, u32[]{:S(2)}, u32[]{:S(2)}) collective-permute-start(bf16[5,32,128]{2,1,0:T(8,128)(2,1)S(1)} %get-tuple-element.42), channel_id=1, source_target_pairs={{0,28},{4,8},{8,4},{12,16},{16,12},{20,24},{24,20},{28,0},{1,29},{... | collective-permute-start | bytes 122888 | tf_op jit(solution)/shard_map/ppermute | solution.py:50

commit v4 on v3

--- a/solution.py
+++ b/solution.py
@@ -152,7 +152,9 @@
         out_shape=(full((3, depth, width, lanes), jnp.float32), edge, edge),
         in_specs=in_vmem(1),
         out_specs=tuple(in_vmem(3)),
-        scratch_shapes=[pltpu.VMEM((2, 3 * HALO, depth, lanes), jnp.float32)],
+        scratch_shapes=[
+            pltpu.VMEM((2, 3 * HALO, depth, lanes), jnp.float32),
+        ],
         compiler_params=params(),
         cost_estimate=cost(1),
         name="moments",
@@ -625,29 +627,97 @@
             flux[dim] = flux[dim] + moved if sign > 0 else flux[dim] - moved
 
 
-def marker_force(table, start, rows, cells, weights):
+def picks_kernel(
+    cell_ref, weight_ref, segment_ref, note_first, note_second, after_this, own, faces, masks, owner
+):
+    taps, markers = cell_ref.shape
+    cells_all, width = own.shape[1], faces.shape[2]
+    owners = owner.shape[1]
+    note_below, note_above = below_above(
+        "span", note_first[6].astype(jnp.int32), note_second[6].astype(jnp.int32)
+    )
+    groups = [(cell_ref[...], weight_ref[...], segment_ref[...])]
+    for note in (note_above, note_below):
+        groups.append(
+            (
+                note[:taps] + 2**15,
+                note[taps : 2 * taps].astype(jnp.float32) * 2.0**-16
+                + note[2 * taps : 3 * taps].astype(jnp.float32) * 2.0**-31,
+                note[3 * taps : 3 * taps + 1],
+            )
+        )
+    owner_of = lax.broadcasted_iota(jnp.int32, (owners, markers), 0)
+    for group, (cells, weights, segment) in enumerate(groups):
+        row = lax.shift_right_logical(cells, 7).astype(jnp.float32).T.astype(jnp.int32)
+        lane = lax.bitwise_and(cells, LANES - 1).astype(jnp.float32).T.astype(jnp.int32)
+        weight = weights.T
+        count = cells_all if group == 0 else width
+        start = cells_all - width if group == 2 else 0
+        row_of = lax.broadcasted_iota(jnp.int32, (markers, count), 1) + start
+        lane_of = lax.broadcasted_iota(jnp.int32, (markers, LANES), 1)
+        for tap in range(taps):
+            at = pl.ds(tap * markers, markers)
+            pick = jnp.where(row_of == row[:, tap : tap + 1], 1.0, 0.0).astype(jnp.bfloat16)
+            if group == 0:
+                own[at, :] = pick
+            else:
+                faces[group - 1, at, :] = pick
+            masks[group, at, :] = jnp.where(
+                lane_of == lane[:, tap : tap + 1], -weight[:, tap : tap + 1], 0.0
+            )
+        hit = jnp.where(owner_of == lax.shift_right_logical(segment, 3), 1.0, 0.0)
+        owner[group] = hit.astype(jnp.bfloat16)
+
+
+def marker_picks(cells, weights, segments, notes, after_this, rows, width, owners):
     taps, markers = cells.shape
-    row_of = lax.broadcasted_iota(jnp.int32, (rows, markers), 0) + start
-    lane_of = lax.broadcasted_iota(jnp.int32, (LANES, markers), 0)
-    row, lane = lax.shift_right_logical(cells, 7), lax.bitwise_and(cells, LANES - 1)
-    pick = jnp.concatenate(
-        [
-            jnp.where(row_of == row[tap : tap + 1, :], 1.0, 0.0).astype(jnp.bfloat16)
-            for tap in range(taps)
-        ],
-        axis=1,
+    return pl.pallas_call(
+        picks_kernel,
+        out_shape=(
+            full((taps * markers, rows), jnp.bfloat16),
+            full((2, taps * markers, width), jnp.bfloat16),
+            full((3, taps * markers, LANES), jnp.float32),
+            full((3, owners, markers), jnp.bfloat16),
+        ),
+        in_specs=in_vmem(5) + [pl.BlockSpec(memory_space=pl.ANY)],
+        out_specs=tuple(in_vmem(4)),
+        compiler_params=params(),
+        cost_estimate=cost(1),
+        name="picks",
+    )(cells, weights, segments, *notes, after_this)
+
+
+def parts_of(value):
+    coarse, _ = split(value)
+    rest = value - coarse.astype(jnp.float32)
+    middle, fine = split(rest)
+    return coarse, middle, fine
+
+
+def across(first, second):
+    total = 0.0
+    for part in parts_of(second):
+        total = total + lax.dot_general(
+            first, part, (((1,), (1,)), ((), ())), preferred_element_type=jnp.float32
+        )
+    return total
+
+
+def marker_force(table, pick, mask_ref, group, taps):
+    picked = jnp.dot(pick, table[0], preferred_element_type=jnp.float32) + jnp.dot(
+        pick, table[1], preferred_element_type=jnp.float32
     )
-    contract = (((0,), (0,)), ((), ()))
-    picked = lax.dot_general(
-        table[0], pick, contract, preferred_element_type=jnp.float32
-    ) + lax.dot_general(table[1], pick, contract, preferred_element_type=jnp.float32)
-    force = [0.0, 0.0, 0.0]
-    for tap in range(taps):
-        weight = jnp.where(lane_of == lane[tap : tap + 1, :], -weights[tap : tap + 1, :], 0.0)
-        at = slice(tap * markers, (tap + 1) * markers)
-        for dim in range(3):
-            force[dim] = force[dim] + picked[dim * LANES : (dim + 1) * LANES, at] * weight
-    return [jnp.sum(part, axis=0, keepdims=True) for part in force]
+    markers = picked.shape[0] // taps
+    force = []
+    for dim in range(3):
+        total = 0.0
+        for tap in range(taps):
+            at = slice(tap * markers, (tap + 1) * markers)
+            mask = mask_ref[group, pl.ds(tap * markers, markers), :]
+            total = total + picked[at, dim * LANES : (dim + 1) * LANES] * mask
+        force.append(total)
+    ones = jnp.ones((8, LANES), jnp.bfloat16)
+    return across(ones, jnp.concatenate(force, axis=0))[:1]
 
 
 def step_kernel(
@@ -658,11 +728,13 @@
     sums_ref,
     mag_in_ref,
     mag_out_ref,
-    cell_ref,
-    weight_ref,
     segment_ref,
     note_first,
     note_second,
+    own_ref,
+    face_ref,
+    mask_ref,
+    owner_ref,
     next_hbm,
     eddy_ref,
     partial_ref,
@@ -774,52 +846,43 @@
         )
         outs[-1].start()
 
-    owners = partial_ref.shape[0]
-    taps, markers = cell_ref.shape
-    owner_of = lax.broadcasted_iota(jnp.int32, (owners, markers), 0)
-    place_of = lax.broadcasted_iota(jnp.int32, (SEG_DEV, markers), 0)
-    totals = [jnp.zeros((owners, SEG_DEV), jnp.float32) for _ in range(3)]
-    groups = [
-        (table, 0, depth * width, cell_ref[...], weight_ref[...], segment_ref[...]),
-    ]
     note_below, note_above = below_above(
         "span", note_first[6].astype(jnp.int32), note_second[6].astype(jnp.int32)
     )
-    for side, (note, start) in enumerate(((note_above, 0), (note_below, (depth - 1) * width))):
-        groups.append(
-            (
-                face_table.at[side],
-                start,
-                width,
-                note[:taps] + 2**15,
-                note[taps : 2 * taps].astype(jnp.float32) * 2.0**-16
-                + note[2 * taps : 3 * taps].astype(jnp.float32) * 2.0**-31,
-                note[3 * taps : 3 * taps + 1],
+    markers = segment_ref.shape[1]
+    taps = own_ref.shape[0] // markers
+    place_of = lax.broadcasted_iota(jnp.int32, (SEG_DEV, markers), 0)
+    spread = []
+    for group, (rows_table, pick, segment) in enumerate(
+        (
+            (table, own_ref[...], segment_ref[...]),
+            (face_table.at[0], face_ref[0], note_above[3 * taps : 3 * taps + 1]),
+            (face_table.at[1], face_ref[1], note_below[3 * taps : 3 * taps + 1]),
+        )
+    ):
+        force = marker_force(rows_table, pick, mask_ref, group, taps)
+        place = place_of == lax.bitwise_and(segment, SEG_DEV - 1)
+        spread.append(
+            jnp.concatenate(
+                [
+                    jnp.where(place, force[:, dim * markers : (dim + 1) * markers], 0.0)
+                    for dim in range(3)
+                ],
+                axis=0,
             )
         )
-    for rows_table, start, rows, cells, weights, segment in groups:
-        owner = jnp.where(owner_of == lax.shift_right_logical(segment, 3), 1.0, 0.0)
-        owner = owner.astype(jnp.bfloat16)
-        place = place_of == lax.bitwise_and(segment, SEG_DEV - 1)
-        for dim, force in enumerate(marker_force(rows_table, start, rows, cells, weights)):
-            rest = jnp.where(place, force, 0.0)
-            for _ in range(3):
-                coarse, _ = split(rest)
-                rest = rest - coarse.astype(jnp.float32)
-                totals[dim] = totals[dim] + lax.dot_general(
-                    owner,
-                    coarse,
-                    (((1,), (1,)), ((), ())),
-                    preferred_element_type=jnp.float32,
-                )
+    totals = 0.0
+    for group in range(3):
+        totals = totals + across(owner_ref[group], spread[group])
     for dim in range(3):
-        partial_ref[:, dim, :] = totals[dim]
+        partial_ref[:, dim, :] = totals[:, dim * SEG_DEV : (dim + 1) * SEG_DEV]
     for copy in outs:
         copy.wait()
 
 
-def step(parts, sums, mag_in, mag_out, cells, weights, segments, notes, owners):
+def step(parts, sums, mag_in, mag_out, segments, notes, picks):
     _, depth, width, lanes = parts[0].shape
+    owners = picks[3].shape[1]
     face = full((5, width, lanes), jnp.bfloat16)
     return pl.pallas_call(
         step_kernel,
@@ -830,7 +893,7 @@
             face,
             face,
         ),
-        in_specs=in_vmem(12),
+        in_specs=in_vmem(14),
         out_specs=(pl.BlockSpec(memory_space=pl.ANY),) + tuple(in_vmem(4)),
         scratch_shapes=[
             pltpu.VMEM((19, depth, FIRST + width + 8, lanes), jnp.float32),
@@ -845,7 +908,7 @@
         compiler_params=params(),
         cost_estimate=cost(5),
         name="step",
-    )(*parts, sums, mag_in, mag_out, cells, weights, segments, *notes)
+    )(*parts, sums, mag_in, mag_out, segments, *notes, *picks)
 
 
 def arrive_kernel(next_in, first, second, arrived_hbm, next_hbm, force_ref, arrived, sems):
@@ -905,20 +968,27 @@
     lines = swap(*lines, "cross")
     planes = swap(*edge_planes(vel, *lines, cells, weights, segments), "span")
     partial, mag_in = inner_sums(vel, *lines)
+    sums, mag_out = outer_sums(vel, *lines, *planes, partial)
     faces = swap(*face_rows(populations, partial), "cross")
-    sums, mag_out = outer_sums(vel, *lines, *planes, partial)
     parts = ready(populations, *faces, sums)
+    rows, width = populations.shape[1] * populations.shape[2], populations.shape[2]
     count = lax.axis_size("span")
     if count & (count - 1):
         sums = lax.psum(sums, "span")
+        picks = marker_picks(cells, weights, segments, planes, sums, rows, width, owners)
     else:
         distance = 1
         while distance < count:
             pairs = [(i, i ^ distance) for i in range(count)]
-            sums = sums + lax.ppermute(sums, "span", pairs)
+            other = lax.ppermute(sums, "span", pairs)
+            if distance == 2:
+                picks = marker_picks(cells, weights, segments, planes, sums, rows, width, owners)
+                sums, picks = lax.optimization_barrier((sums + other, picks))
+            else:
+                sums = sums + other
             distance *= 2
     moved, eddy_coeff, packed, *leaving = step(
-        parts, sums, mag_in, mag_out, cells, weights, segments, planes, owners
+        parts, sums, mag_in, mag_out, segments, planes, picks
     )
     arrived = lax.all_to_all(packed, ("span", "cross"), 0, 0)
     populations_next, segment_force = arrive(moved, *swap(*leaving, "span"), arrived)

time: 54 us -> 55.3 us (1.024)
  Pallas kernels: 17.4 us -> 20.3 us
  waiting for transfers between devices: 10.3 us -> 8.72 us
    ppermute x3, waiting for transfers between devices: 8.5 us -> 6.94 us  [local(): other = lax.ppermute(sums, 'span', pairs)]
    pallas_call x0 -> x1, Pallas kernels: none -> 1.55 us  [marker_picks(): pl.pallas_call(picks_kernel, out_shape=(full((taps * markers, rows), jnp....]
    pallas_call x1, Pallas kernels: 5.73 us -> 7.11 us  [step(): pl.pallas_call(step_kernel, out_shape=(full((19, depth, width, lanes), jn...]
  transfers between devices with their start and end apart: 11 -> 11, of which waited for: 4 -> 4; matrix products, arithmetic and copies ran while one was open for 0% -> 0% of each run, Pallas kernels for 14% -> 17%
where the time goes in v4:
time: 55.3 us; the launch traced here: 55.2 us
  Pallas kernels  20.3 us (37%)
  starting transfers between devices  12.3 us (22%)
  blocking collectives  11.4 us (21%)
  waiting for transfers between devices  8.72 us (16%)
  local copies, waits for them, and re-layouts  1.71 us (3%)
  between operations  0.75 us (1%)
    ppermute x8, starting transfers between devices, swap(): return (lax.ppermute(first, axis, near), lax.ppermute(second, axis, other))  12 us
    all_to_all x1, blocking collectives, local(): arrived = lax.all_to_all(packed, ('span', 'cross'), 0, 0)  11.4 us
    pallas_call x1, Pallas kernels, step(): pl.pallas_call(step_kernel, out_shape=(full((19, depth, width, lanes), jn...  7.11 us
    ppermute x3, waiting for transfers between devices, local(): other = lax.ppermute(sums, 'span', pairs)  6.94 us
    pallas_call x1, Pallas kernels, inner_sums(): pl.pallas_call(inner_kernel, out_shape=(full((2, EXT, LANES), jnp.float32...  5.28 us
    pallas_call x1, Pallas kernels, ready(): pl.pallas_call(ready_kernel, out_shape=(full((19, depth, width, lanes), j...  2.07 us
    pallas_call x1, Pallas kernels, outer_sums(): pl.pallas_call(outer_kernel, out_shape=(full((-(-2 * (width + 2) // 8) *...  1.79 us
    ppermute x8, waiting for transfers between devices, swap(): return (lax.ppermute(first, axis, near), lax.ppermute(second, axis, other))  1.77 us
  transfers between devices with their start and end apart: 11, of which 4 were waited for; matrix products, arithmetic and copies ran while one was open for 0% of the time, Pallas kernels for 17%

profile of v4, /device:TPU:0, one launch (start us, length us, event | category | flops | bytes accessed | tf_op | source)
XLA Modules:
  0.0 55.2 jit_solution(2633567824571669428)
XLA Ops:
  0.6 1.7 %copy-done = bf16[19,16,32,128]{3,2,1,0:T(8,128)(2,1)S(1)} copy-done((bf16[19,16,32,128]{3,2,1,0:T(8,128)(2,1)S(1)}, bf16[19,16,32,128]{3,2,1,0:T(8,128)(2,1)}, u32[]{:S(2)}) %copy-start) | copy-done | bytes 2490392
  2.3 0.7 %moments.1 = (f32[3,16,32,128]{3,2,1,0:T(8,128)S(1)}, s16[9,16,128]{2,1,0:T(8,128)(2,1)S(1)}, s16[9,16,128]{2,1,0:T(8,128)(2,1)S(1)}) custom-call(bf16[19,16,32,128]{3,2,1,0:T(8,128)(2,1)S(1)} %copy-done), custom_call_target="tpu_custom_call" | custom-call | bytes 3600000 | tf_op jit(solution)/shard_map/moments/pallas_call | solution.py:150
  3.1 0.5 collective-permute-start
  3.6 2.6 %collective-permute-start.1 = (s16[9,16,128]{2,1,0:T(8,128)(2,1)S(1)}, s16[9,16,128]{2,1,0:T(8,128)(2,1)S(1)}, u32[]{:S(2)}, u32[]{:S(2)}) collective-permute-start(s16[9,16,128]{2,1,0:T(8,128)(2,1)S(1)} %get-tuple-element.36), channel_id=1, source_target_pairs={{0,3},{1,2},{2,1},{3,0},{4,7},{5,6},{6,5},{7,4},{8,11},{9,10},{10,... | collective-permute-start | bytes 110600 | tf_op jit(solution)/shard_map/ppermute | solution.py:50
  6.2 0.0 collective-permute-done.low_ref
  6.2 1.8 %collective-permute-done.1.high_ref = s16[9,16,128]{2,1,0:T(8,128)(2,1)S(1)} collective-permute-done((s16[9,16,128]{2,1,0:T(8,128)(2,1)S(1)}, s16[9,16,128]{2,1,0:T(8,128)(2,1)S(1)}, u32[]{:S(2)}, u32[]{:S(2)}) %collective-permute-start.1) | collective-permute-done | bytes 36896 | tf_op jit(solution)/shard_map/ppermute | solution.py:50
  8.0 0.1 edges.1
  8.1 1.6 %collective-permute-start.4 = (s16[7,40,128]{2,1,0:T(8,128)(2,1)S(1)}, s16[7,40,128]{2,1,0:T(8,128)(2,1)S(1)}, u32[]{:S(2)}, u32[]{:S(2)}) collective-permute-start(s16[7,40,128]{2,1,0:T(8,128)(2,1)S(1)} %get-tuple-element.40), channel_id=1, source_target_pairs={{0,4},{4,0},{8,12},{12,8},{16,20},{20,16},{24,28},{28,24},{1,5},{5... | collective-permute-start | bytes 215048 | tf_op jit(solution)/shard_map/ppermute | solution.py:50
  9.8 3.6 %collective-permute-start.5 = (s16[7,40,128]{2,1,0:T(8,128)(2,1)S(1)}, s16[7,40,128]{2,1,0:T(8,128)(2,1)S(1)}, u32[]{:S(2)}, u32[]{:S(2)}) collective-permute-start(s16[7,40,128]{2,1,0:T(8,128)(2,1)S(1)} %get-tuple-element.41), channel_id=1, source_target_pairs={{0,28},{4,8},{8,4},{12,16},{16,12},{20,24},{24,20},{28,0},{1,29},{... | collective-permute-start | bytes 215048 | tf_op jit(solution)/shard_map/ppermute | solution.py:50
  13.3 5.3 %inner_sums.1 = (f32[2,40,128]{2,1,0:T(8,128)S(1)}, f32[14,40,128]{2,1,0:T(8,128)S(1)}) custom-call(f32[3,16,32,128]{3,2,1,0:T(8,128)S(1)} %get-tuple-element.34.vel_ref, s16[9,16,128]{2,1,0:T(8,128)(2,1)S(1)} %collective-permute-done.low_ref, s16[9,16,128]{2,1,0:T(8,128)(2,1)S(1)} %collective-permute-done.1.high_ref), custom_call_target="tpu_custom_call" | custom-call | bytes 18000000 | tf_op jit(solution)/shard_map/inner_sums/pallas_call | solution.py:375
  18.6 0.0 collective-permute-done.4.first_ref.note_first
  18.6 0.0 collective-permute-done.5.second_ref.note_second
  18.6 1.8 %outer_sums.1 = (f32[72,128]{1,0:T(8,128)S(1)}, f32[8,40,128]{2,1,0:T(8,128)S(1)}) custom-call(f32[3,16,32,128]{3,2,1,0:T(8,128)S(1)} %get-tuple-element.34.vel_ref, s16[9,16,128]{2,1,0:T(8,128)(2,1)S(1)} %collective-permute-done.low_ref, s16[9,16,128]{2,1,0:T(8,128)(2,1)S(1)} %collective-permute-done.1.high_ref, ...), custom_call_target="tpu_custom_call" | custom-call | bytes 7200000 | tf_op jit(solution)/shard_map/outer_sums/pallas_call | solution.py:433
  20.4 0.1 collective-permute-start.6
  20.5 0.3 face_rows.1
  20.8 0.1 collective-permute-start.2
  20.9 1.6 %collective-permute-start.3 = (bf16[19,16,128]{2,1,0:T(8,128)(2,1)S(1)}, bf16[19,16,128]{2,1,0:T(8,128)(2,1)S(1)}, u32[]{:S(2)}, u32[]{:S(2)}) collective-permute-start(bf16[19,16,128]{2,1,0:T(8,128)(2,1)S(1)} %get-tuple-element.39), channel_id=1, source_target_pairs={{0,3},{1,2},{2,1},{3,0},{4,7},{5,6},{6,5},{7,4},{8,11},{9,10},{10,... | collective-permute-start | bytes 233480 | tf_op jit(solution)/shard_map/ppermute | solution.py:50
  22.5 1.9 %collective-permute-done.6 = f32[72,128]{1,0:T(8,128)S(1)} collective-permute-done((f32[72,128]{1,0:T(8,128)S(1)}, f32[72,128]{1,0:T(8,128)S(1)}, u32[]{:S(2)}, u32[]{:S(2)}) %collective-permute-start.6) | collective-permute-done | bytes 36896 | tf_op jit(solution)/shard_map/ppermute | solution.py:983
  24.4 0.0 collective-permute-start.7
  24.5 1.5 %picks.1 = (bf16[1024,512]{1,0:T(8,128)(2,1)S(1)}, bf16[2,1024,32]{2,1,0:T(8,128)(2,1)S(1)}, f32[3,1024,128]{2,1,0:T(8,128)S(1)}, bf16[3,32,128]{2,1,0:T(8,128)(2,1)S(1)}) custom-call(s32[8,128]{1,0:T(8,128)S(1)} %bitcast.4, f32[8,128]{1,0:T(8,128)S(1)} %bitcast.6, s32[1,128]{1,0:T(1,128)S(1)} %bitcast.8, ...), custom_call_target="tpu_custom_call" | custom-call | bytes 3600000 | tf_op jit(solution)/shard_map/picks/pallas_call | solution.py:674
  26.0 2.4 %collective-permute-done.7 = f32[72,128]{1,0:T(8,128)S(1)} collective-permute-done((f32[72,128]{1,0:T(8,128)S(1)}, f32[72,128]{1,0:T(8,128)S(1)}, u32[]{:S(2)}, u32[]{:S(2)}) %collective-permute-start.7) | collective-permute-done | bytes 36896 | tf_op jit(solution)/shard_map/ppermute | solution.py:983
  28.4 0.2 collective-permute-start.8
  28.6 0.0 collective-permute-done.2.first
  28.6 2.1 %ready.1 = (f32[19,16,32,128]{3,2,1,0:T(8,128)S(1)}, f32[5,16,32,128]{3,2,1,0:T(8,128)S(1)}, f32[2,5,16,128]{3,2,1,0:T(8,128)S(1)}, f32[2,5,16,128]{3,2,1,0:T(8,128)S(1)}) custom-call(bf16[19,16,32,128]{3,2,1,0:T(8,128)(2,1)S(1)} %copy-done.1, bf16[19,16,128]{2,1,0:T(8,128)(2,1)S(1)} %collective-permute-done.2.first, ...), custom_call_target="tpu_custom_call" | custom-call | bytes 9000000 | tf_op jit(solution)/shard_map/ready/pallas_call | solution.py:600
  30.7 2.6 %collective-permute-done.8 = f32[72,128]{1,0:T(8,128)S(1)} collective-permute-done((f32[72,128]{1,0:T(8,128)S(1)}, f32[72,128]{1,0:T(8,128)S(1)}, u32[]{:S(2)}, u32[]{:S(2)}) %collective-permute-start.8) | collective-permute-done | bytes 36896 | tf_op jit(solution)/shard_map/ppermute | solution.py:983
  33.3 7.1 %step.1 = (bf16[19,16,32,128]{3,2,1,0:T(8,128)(2,1)}, f32[32,128]{1,0:T(8,128)}, f32[32,3,8]{2,1,0:T(4,128)S(1)}, bf16[5,32,128]{2,1,0:T(8,128)(2,1)S(1)}, bf16[5,32,128]{2,1,0:T(8,128)(2,1)S(1)}) custom-call(f32[19,16,32,128]{3,2,1,0:T(8,128)S(1)} %get-tuple-element.43.base_ref, f32[5,16,32,128]{3,2,1,0:T(8,128)S(1)} %get-tuple-element.44.shear_ref, ...), custom_call_target="tpu_custom_call" | custom-call | bytes 18000000 | tf_op jit(solution)/shard_map/step/pallas_call | solution.py:887
  40.4 0.2 collective-permute-start.9
  40.6 1.8 %collective-permute-start.10 = (bf16[5,32,128]{2,1,0:T(8,128)(2,1)S(1)}, bf16[5,32,128]{2,1,0:T(8,128)(2,1)S(1)}, u32[]{:S(2)}, u32[]{:S(2)}) collective-permute-start(bf16[5,32,128]{2,1,0:T(8,128)(2,1)S(1)} %get-tuple-element.60), channel_id=1, source_target_pairs={{0,28},{4,8},{8,4},{12,16},{16,12},{20,24},{24,20},{28,0},{1,29},{... | collective-permute-start | bytes 122888 | tf_op jit(solution)/shard_map/ppermute | solution.py:50
  42.4 11.4 %all_to_all.5.arrived_hbm = f32[32,3,8]{2,1,0:T(4,128)S(1)} all-to-all(f32[32,3,8]{2,1,0:T(4,128)S(1)} %get-tuple-element.61), channel_id=1, replica_groups=mesh['span'=8,'cross'=4] {'span','cross'}, dimensions={0} | all-to-all | bytes 6144 | tf_op jit(solution)/shard_map/all_to_all | solution.py:993
  53.8 0.0 collective-permute-done.9.first
  53.8 0.0 collective-permute-done.10.second
  53.8 1.4 %arrive.1 = (bf16[19,16,32,128]{3,2,1,0:T(8,128)(2,1)}, f32[3,8]{1,0:T(4,128)}) custom-call(bf16[19,16,32,128]{3,2,1,0:T(8,128)(2,1)} %get-tuple-element.58.next_in, bf16[5,32,128]{2,1,0:T(8,128)(2,1)S(1)} %collective-permute-done.9.first, bf16[5,32,128]{2,1,0:T(8,128)(2,1)S(1)} %collective-permute-done.10.second, ...), custom_call_target="tpu_custom_call", output_to_operand_aliasing={{0}: (0, {})} | custom-call | bytes 1800000 | tf_op jit(solution)/shard_map/arrive/pallas_call | solution.py:945
  (13 shorter events, 0.0 us)
Async XLA Ops:
  0.6 1.7 %copy-start = (bf16[19,16,32,128]{3,2,1,0:T(8,128)(2,1)S(1)}, bf16[19,16,32,128]{3,2,1,0:T(8,128)(2,1)}, u32[]{:S(2)}) copy-start(bf16[19,16,32,128]{3,2,1,0:T(8,128)(2,1)} %pops.5) | copy-start | bytes 7471108
  2.3 5.7 %copy-start.2 = (s32[128,8]{0,1:T(8,128)S(1)}, s32[128,8]{0,1:T(8,128)}, u32[]{:S(2)}) copy-start(s32[128,8]{0,1:T(8,128)} %param.5) | copy-start | bytes 12292
  2.3 5.7 %copy-start.3 = (f32[128,8]{0,1:T(8,128)S(1)}, f32[128,8]{0,1:T(8,128)}, u32[]{:S(2)}) copy-start(f32[128,8]{0,1:T(8,128)} %param.6) | copy-start | bytes 12292
  2.3 5.7 %copy-start.4 = (s32[128]{0:T(128)S(1)}, s32[128]{0:T(128)}, u32[]{:S(2)}) copy-start(s32[128]{0:T(128)} %param.7) | copy-start | bytes 1540
  2.3 18.2 %copy-start.1 = (bf16[19,16,32,128]{3,2,1,0:T(8,128)(2,1)S(1)}, bf16[19,16,32,128]{3,2,1,0:T(8,128)(2,1)}, u32[]{:S(2)}) copy-start(bf16[19,16,32,128]{3,2,1,0:T(8,128)(2,1)} %pops.5) | copy-start | bytes 7471108
  3.1 3.2 %collective-permute-start = (s16[9,16,128]{2,1,0:T(8,128)(2,1)S(1)}, s16[9,16,128]{2,1,0:T(8,128)(2,1)S(1)}, u32[]{:S(2)}, u32[]{:S(2)}) collective-permute-start(s16[9,16,128]{2,1,0:T(8,128)(2,1)S(1)} %get-tuple-element.35), channel_id=1, source_target_pairs={{0,1},{1,0},{2,3},{3,2},{4,5},{5,4},{6,7},{7,6},{8,9},{9,8},{10,11... | collective-permute-start | bytes 110600 | tf_op jit(solution)/shard_map/ppermute | solution.py:50
  3.6 4.4 %collective-permute-start.1 = (s16[9,16,128]{2,1,0:T(8,128)(2,1)S(1)}, s16[9,16,128]{2,1,0:T(8,128)(2,1)S(1)}, u32[]{:S(2)}, u32[]{:S(2)}) collective-permute-start(s16[9,16,128]{2,1,0:T(8,128)(2,1)S(1)} %get-tuple-element.36), channel_id=1, source_target_pairs={{0,3},{1,2},{2,1},{3,0},{4,7},{5,6},{6,5},{7,4},{8,11},{9,10},{10,... | collective-permute-start | bytes 110600 | tf_op jit(solution)/shard_map/ppermute | solution.py:50
  8.1 10.5 %collective-permute-start.4 = (s16[7,40,128]{2,1,0:T(8,128)(2,1)S(1)}, s16[7,40,128]{2,1,0:T(8,128)(2,1)S(1)}, u32[]{:S(2)}, u32[]{:S(2)}) collective-permute-start(s16[7,40,128]{2,1,0:T(8,128)(2,1)S(1)} %get-tuple-element.40), channel_id=1, source_target_pairs={{0,4},{4,0},{8,12},{12,8},{16,20},{20,16},{24,28},{28,24},{1,5},{5... | collective-permute-start | bytes 215048 | tf_op jit(solution)/shard_map/ppermute | solution.py:50
  9.8 8.9 %collective-permute-start.5 = (s16[7,40,128]{2,1,0:T(8,128)(2,1)S(1)}, s16[7,40,128]{2,1,0:T(8,128)(2,1)S(1)}, u32[]{:S(2)}, u32[]{:S(2)}) collective-permute-start(s16[7,40,128]{2,1,0:T(8,128)(2,1)S(1)} %get-tuple-element.41), channel_id=1, source_target_pairs={{0,28},{4,8},{8,4},{12,16},{16,12},{20,24},{24,20},{28,0},{1,29},{... | collective-permute-start | bytes 215048 | tf_op jit(solution)/shard_map/ppermute | solution.py:50
  20.4 4.0 %collective-permute-start.6 = (f32[72,128]{1,0:T(8,128)S(1)}, f32[72,128]{1,0:T(8,128)S(1)}, u32[]{:S(2)}, u32[]{:S(2)}) collective-permute-start(f32[72,128]{1,0:T(8,128)S(1)} %get-tuple-element.42.after_this), channel_id=1, source_target_pairs={{0,4},{4,0},{8,12},{12,8},{16,20},{20,16},{24,28},{28,24},{1,5},{5... | collective-permute-start | bytes 110600 | tf_op jit(solution)/shard_map/ppermute | solution.py:983
  20.8 7.8 %collective-permute-start.2 = (bf16[19,16,128]{2,1,0:T(8,128)(2,1)S(1)}, bf16[19,16,128]{2,1,0:T(8,128)(2,1)S(1)}, u32[]{:S(2)}, u32[]{:S(2)}) collective-permute-start(bf16[19,16,128]{2,1,0:T(8,128)(2,1)S(1)} %get-tuple-element.38), channel_id=1, source_target_pairs={{0,1},{1,0},{2,3},{3,2},{4,5},{5,4},{6,7},{7,6},{8,9},{9,8},{10,11... | collective-permute-start | bytes 233480 | tf_op jit(solution)/shard_map/ppermute | solution.py:50
  20.9 7.7 %collective-permute-start.3 = (bf16[19,16,128]{2,1,0:T(8,128)(2,1)S(1)}, bf16[19,16,128]{2,1,0:T(8,128)(2,1)S(1)}, u32[]{:S(2)}, u32[]{:S(2)}) collective-permute-start(bf16[19,16,128]{2,1,0:T(8,128)(2,1)S(1)} %get-tuple-element.39), channel_id=1, source_target_pairs={{0,3},{1,2},{2,1},{3,0},{4,7},{5,6},{6,5},{7,4},{8,11},{9,10},{10,... | collective-permute-start | bytes 233480 | tf_op jit(solution)/shard_map/ppermute | solution.py:50
  24.4 4.0 %collective-permute-start.7 = (f32[72,128]{1,0:T(8,128)S(1)}, f32[72,128]{1,0:T(8,128)S(1)}, u32[]{:S(2)}, u32[]{:S(2)}) collective-permute-start(f32[72,128]{1,0:T(8,128)S(1)} %add.9.after_this), channel_id=1, source_target_pairs={{0,8},{4,12},{8,0},{12,4},{16,24},{20,28},{24,16},{28,20},{1,9},{5... | collective-permute-start | bytes 110600 | tf_op jit(solution)/shard_map/ppermute | solution.py:983
  28.4 4.9 %collective-permute-start.8 = (f32[72,128]{1,0:T(8,128)S(1)}, f32[72,128]{1,0:T(8,128)S(1)}, u32[]{:S(2)}, u32[]{:S(2)}) collective-permute-start(f32[72,128]{1,0:T(8,128)S(1)} %add.10), channel_id=1, source_target_pairs={{0,16},{4,20},{8,24},{12,28},{16,0},{20,4},{24,8},{28,12},{1,17},{... | collective-permute-start | bytes 110600 | tf_op jit(solution)/shard_map/ppermute | solution.py:983
  40.4 13.4 %collective-permute-start.9 = (bf16[5,32,128]{2,1,0:T(8,128)(2,1)S(1)}, bf16[5,32,128]{2,1,0:T(8,128)(2,1)S(1)}, u32[]{:S(2)}, u32[]{:S(2)}) collective-permute-start(bf16[5,32,128]{2,1,0:T(8,128)(2,1)S(1)} %get-tuple-element.59), channel_id=1, source_target_pairs={{0,4},{4,0},{8,12},{12,8},{16,20},{20,16},{24,28},{28,24},{1,5},{5... | collective-permute-start | bytes 122888 | tf_op jit(solution)/shard_map/ppermute | solution.py:50
  40.6 13.2 %collective-permute-start.10 = (bf16[5,32,128]{2,1,0:T(8,128)(2,1)S(1)}, bf16[5,32,128]{2,1,0:T(8,128)(2,1)S(1)}, u32[]{:S(2)}, u32[]{:S(2)}) collective-permute-start(bf16[5,32,128]{2,1,0:T(8,128)(2,1)S(1)} %get-tuple-element.60), channel_id=1, source_target_pairs={{0,28},{4,8},{8,4},{12,16},{16,12},{20,24},{24,20},{28,0},{1,29},{... | collective-permute-start | bytes 122888 | tf_op jit(solution)/shard_map/ppermute | solution.py:50
